TPU v7x, 512 devices: a whole 4x8x8 slice. The times are simulated.
512 devices in a mesh: row: 16 (over z_lo, x, core), col: 32 (over z_hi, y).
Axes of the slice: x: 4, y: 8, z: 8 (z_hi: 4, z_lo: 2; z = z_hi * 2 + z_lo), core: 2. Of those that a mesh axis runs over, the one named last changes fastest.
Arguments:
- amplitudes: bfloat16 [8, 2048, 2048], P(None, 'col', 'row'), may hold values from -6 to 6
- factors: bfloat16 [8, 2048, 2048], P(None, 'col'), as said below
- amp_mask: int32 [16, 16], replicated, may hold values 0 or 1
- out_mask: int32 [16, 16], replicated, may hold values 0 or 1
- partner: int32 [8], replicated, may hold values from 0 to 7, as said below
Outputs:
- residual: float32 [8, 2048, 2048], P(None, ('col', 'row'))
Inputs may be any that keep to these rules, and one draw needn't show every extreme that they name: partner is an involution: partner[partner[p]] = p; exactly two pairs are their own partner. factors[q, x, y] = factors[q, y, x] for all q, x, y.
All inputs are finite; a program needn't handle non-finite values.
Results may differ from a plain program's by a relative error of at most 0.0029.
Values may be sent and summed in bfloat16 or wider, within the bound.
No kernel may reach another device: no remote copies, remote signals or barrier semaphores. Data moves between devices by JAX's collectives and lax.ppermute only.
A program may use at most 64 MiB of HBM per device.

v0:
```python
import jax
import jax.numpy as jnp
from jax import lax
from jax.sharding import PartitionSpec as P


def tile_lookup(occupancy, row_ids, col_ids, tile_width):
    tile_count = occupancy.shape[0]
    tile_slots = jnp.arange(tile_count, dtype=jnp.int32)
    row_hits = ((row_ids // tile_width)[:, None] == tile_slots[None, :]).astype(jnp.float32)
    col_hits = ((col_ids // tile_width)[:, None] == tile_slots[None, :]).astype(jnp.float32)
    picked = jnp.dot(row_hits, occupancy.astype(jnp.float32), precision=lax.Precision.HIGHEST)
    return jnp.dot(picked, col_hits.T, precision=lax.Precision.HIGHEST)


def on_device(amplitudes, factors, amp_mask, out_mask, partner):
    pair_count, amp_rows, amp_cols = amplitudes.shape
    batch_count, block_rows, full_width = factors.shape
    tile_width = full_width // amp_mask.shape[0]
    row_index = lax.axis_index("row")
    col_index = lax.axis_index("col")
    row_devices = lax.axis_size("row")
    col_devices = lax.axis_size("col")
    own_rows = block_rows // row_devices
    first_ids = col_index * amp_rows + jnp.arange(amp_rows, dtype=jnp.int32)
    second_ids = row_index * amp_cols + jnp.arange(amp_cols, dtype=jnp.int32)
    amp_weights = tile_lookup(amp_mask, first_ids, second_ids, tile_width)
    masked = amplitudes * amp_weights.astype(jnp.bfloat16)[None]
    whole_amps = lax.all_gather(masked, "col", axis=1, tiled=True)
    product = jnp.einsum("qac,pcd->pqad", factors, whole_amps, preferred_element_type=jnp.float32)
    inner = product.astype(jnp.bfloat16)
    factor_block = lax.dynamic_slice_in_dim(factors, row_index * amp_cols, amp_cols, 2)
    partial_sums = jnp.einsum(
        "pqad,qbd->pab",
        inner,
        lax.all_gather(factor_block, "col", axis=1, tiled=True),
        preferred_element_type=jnp.float32,
    )
    summed = lax.psum_scatter(partial_sums, "row", scatter_dimension=1, tiled=True)
    out_ids = col_index * block_rows + row_index * own_rows + jnp.arange(own_rows, dtype=jnp.int32)
    every_id = jnp.arange(full_width, dtype=jnp.int32)
    kept = summed * tile_lookup(out_mask, out_ids, every_id, tile_width)[None]
    regrouped = kept.reshape(pair_count, own_rows, col_devices, row_devices, own_rows)
    regrouped = jnp.transpose(regrouped, (0, 1, 3, 2, 4)).reshape(pair_count, own_rows, full_width)
    received = lax.all_to_all(
        lax.all_to_all(regrouped, "row", split_axis=2, concat_axis=1, tiled=True),
        "col",
        split_axis=2,
        concat_axis=1,
        tiled=True,
    )
    mirrored = jnp.swapaxes(received, 1, 2)
    pair_slots = jnp.arange(pair_count, dtype=jnp.int32)
    pair_hits = (partner[:, None] == pair_slots[None, :]).astype(jnp.float32)
    swapped = jnp.einsum("pq,qyx->pyx", pair_hits, mirrored, precision=lax.Precision.HIGHEST)
    return kept + swapped


def solution(mesh):
    return jax.shard_map(
        on_device,
        mesh=mesh,
        in_specs=(P(None, "col", "row"), P(None, "col", None), P(), P(), P()),
        out_specs=P(None, ("col", "row"), None),
        check_vma=False,
    )
```

profile of v0, /device:TPU:1, one launch (start us, length us, event | category | flops | bytes accessed | tf_op | source)
XLA Modules:
  0.0 374.6 jit_solution(18192545380769628654)
XLA Ops:
  6.5 0.0 copy-start
  6.5 0.0 all-gather.3.cloned.1.call-start
  6.6 1.0 fusion.23
  7.6 0.3 convolution_convert_fusion
  7.9 1.6 broadcast_multiply_fusion.1
  9.5 0.0 all-gather.3.cloned.1.call-update
  9.5 0.0 all-gather.5.cloned.1.call-start
  9.6 0.0 copy-done
  9.6 0.7 constant_dynamic-slice_fusion
  10.3 0.0 all-gather.5.cloned.1.call-update
  10.3 0.0 reduce-scatter.2.cloned.1.call-start
  10.3 107.7 %all-gather.3.cloned.1.call-done = bf16[8,2048,128]{2,1,0:T(8,128)(2,1)} async-done(((bf16[8,64,128]{2,1,0:T(8,128)(2,1)}), bf16[8,2048,128]{2,1,0:T(8,128)(2,1)}) %all-gather.3.cloned.1.call-update) | async-done | bytes 4194320 | tf_op jit(solution)/shard_map/all_gather | solution.py:29
  118.1 4.5 %fusion.13 = bf16[8,8,64,128]{3,2,1,0:T(8,128)(2,1)S(1)} fusion(bf16[8,64,2048]{2,1,0:T(8,128)(2,1)S(1)} %copy-done, bf16[8,2048,128]{2,1,0:T(8,128)(2,1)} %all-gather.3.cloned.1.call-done), kind=kOutput, calls=%fused_computation.8 | convolution fusion | flops 2148007936 | bytes 7340032 | tf_op jit(solution)/shard_map/qac,pcd->pqad/dot_general | solution.py:30
  122.6 97.1 %all-gather.5.cloned.1.call-done = bf16[8,2048,128]{2,1,0:T(8,128)(2,1)} async-done(((bf16[8,64,128]{2,1,0:T(8,128)(2,1)}), bf16[8,2048,128]{2,1,0:T(8,128)(2,1)}) %all-gather.5.cloned.1.call-update) | async-done | bytes 4194320 | tf_op jit(solution)/shard_map/all_gather | solution.py:36
  219.7 6.7 %fusion.4 = f32[8,64,2048]{2,0,1:T(8,128)} fusion(bf16[8,2048,128]{2,1,0:T(8,128)(2,1)} %all-gather.5.cloned.1.call-done, bf16[8,8,64,128]{3,2,1,0:T(8,128)(2,1)S(1)} %fusion.13), kind=kOutput, calls=%fused_computation.4 | convolution fusion | flops 2147483648 | bytes 9437184 | tf_op jit(solution)/shard_map/pqad,qbd->pab/dot_general | solution.py:33
  226.3 0.0 copy-start.2
  226.3 0.0 reduce-scatter.2.cloned.1.call-update
  226.4 0.6 copy-done.2
  227.0 0.2 fusion.27
  227.2 0.7 fusion.19
  227.9 64.3 %reduce-scatter.2.cloned.1.call-done = f32[8,4,2048]{2,0,1:T(8,128)} async-done(((f32[8,64,2048]{2,0,1:T(8,128)}), f32[8,4,2048]{2,0,1:T(8,128)}) %reduce-scatter.2.cloned.1.call-update) | async-done | bytes 262160 | tf_op jit(solution)/shard_map/reduce_scatter | solution.py:39
  292.2 1.0 broadcast_multiply_fusion
  293.2 2.8 copy.32
  296.0 3.3 copy.33
  299.3 10.0 %copy.49 = f32[8,4,2048]{0,1,2:T(4,128)} copy(f32[8,4,2048]{0,2,1:T(8,128)S(1)} %bitcast.55) | data formatting | bytes 524288 | tf_op jit(solution)/shard_map/reshape | solution.py:44
  309.3 6.5 %reshape.86 = f32[16,1,4096]{2,1,0:T(1,128)S(1)} reshape(f32[2048,4,8]{2,1,0:T(4,128)} %bitcast.56) | data formatting | bytes 524288
  315.8 13.2 %all_to_all.36 = f32[16,1,4096]{2,1,0:T(1,128)S(1)} all-to-all(f32[16,1,4096]{2,1,0:T(1,128)S(1)} %reshape.86), channel_id=1, replica_groups=mesh['row'=16,'col'=32] {'row'}, dimensions={0} | all-to-all | bytes 524288 | tf_op jit(solution)/shard_map/all_to_all | solution.py:46
  329.0 0.5 broadcast.150
  329.5 1.3 reduce
  330.8 6.3 %reshape.87 = f32[2048,4,8]{2,1,0:T(4,128)} reshape(f32[16,4096]{1,0:T(8,128)S(1)} %reduce) | data formatting | bytes 524288
  337.1 0.0 copy-start.1
  337.1 3.4 copy.45
  340.5 0.3 copy.37
  340.8 0.3 reshape.88
  341.2 23.7 %all_to_all.37 = f32[32,1,2048]{2,1,0:T(1,128)S(1)} all-to-all(f32[32,1,2048]{2,1,0:T(1,128)S(1)} %reshape.88), channel_id=1, replica_groups=mesh['row'=16,'col'=32] {'col'}, dimensions={0} | all-to-all | bytes 524288 | tf_op jit(solution)/shard_map/all_to_all | solution.py:45
  364.9 1.3 reduce.1
  366.1 0.2 reshape.89
  366.3 0.3 copy.38
  366.7 0.2 all_to_all.33
  366.8 0.0 copy-done.1
  366.8 0.3 convolution_add_fusion
  367.2 0.9 copy.39
  (4 shorter events, 0.0 us)
Async XLA Ops:
  6.5 3.0 copy-start
  6.5 111.5 %all-gather.3.cloned.1.call-start = ((), (), s32[]{:S(2)}) async-start(), calls=%async_computation.3 | async-start | bytes 4325376 | tf_op jit(solution)/shard_map/all_gather | solution.py:29
  9.5 210.2 %all-gather.5.cloned.1.call-start = ((), (), s32[]{:S(2)}) async-start(), calls=%async_computation.4 | async-start | bytes 4325376 | tf_op jit(solution)/shard_map/all_gather | solution.py:36
  10.3 281.9 %reduce-scatter.2.cloned.1.call-start = ((), (), s32[]{:S(2)}) async-start(), calls=%async_computation.5 | async-start | bytes 4456448 | tf_op jit(solution)/shard_map/reduce_scatter | solution.py:39
  226.3 0.7 copy-start.2
  337.1 29.7 %copy-start.1 = (s32[8]{0:T(128)S(1)}, s32[8]{0:T(128)}, u32[]{:S(2)}) copy-start(s32[8]{0:T(128)} %param.9) | copy-start | bytes 100
Sparse Core Ops, SparseCore 0:
  10.5 107.5 all-gather.2
  121.2 98.4 all-gather.4
  226.5 65.6 reduce-scatter.1
where the time goes:
time: 377 us; the launch traced here: 375 us
  waiting for transfers between devices  269 us (71%)
  blocking collectives  36.9 us (10%)
  local copies, waits for them, and re-layouts  36.4 us (10%)
  matrix products  13.7 us (4%)
  between operations  13.2 us (4%)
  other arithmetic  5.1 us (1%)
    all_gather x1, waiting for transfers between devices, on_device(): whole_amps = lax.all_gather(masked, 'col', axis=1, tiled=True)  108 us
    all_gather x1, waiting for transfers between devices, on_device(): lax.all_gather(factor_block, 'col', axis=1, tiled=True)  97.1 us
    reduce_scatter x1, waiting for transfers between devices, on_device(): lax.psum_scatter(partial_sums, 'row', scatter_dimension=1, tiled=True)  64.3 us
    all_to_all x1, blocking collectives, on_device(): lax.all_to_all(lax.all_to_all(regrouped, 'row', split_axis=2, concat_axis...  23.7 us
    unnamed x10, local copies, waits for them, and re-layouts  14 us
    all_to_all x1, blocking collectives, on_device(): lax.all_to_all(regrouped, 'row', split_axis=2, concat_axis=1, tiled=True)  13.2 us
    reshape x1, local copies, waits for them, and re-layouts, on_device(): jnp.transpose(regrouped, (0, 1, 3, 2, 4))  9.97 us
  transfers between devices with their start and end apart: 3, of which 3 were waited for; matrix products, arithmetic and copies ran while one was open for 2% of the time, Pallas kernels for 0%

commit v1 on v0

v1 whole, which is shorter than its diff:
```python
import jax
import jax.numpy as jnp
from jax import lax
from jax.experimental import pallas as pl
from jax.experimental.pallas import tpu as pltpu
from jax.sharding import Mesh, PartitionSpec as P

ROW = ("zl", "x", "core")
COL = ("zh", "y")
ALL = ROW + COL
VMEM_LIMIT = 48 * 1024 * 1024


def params():
    return pltpu.CompilerParams(vmem_limit_bytes=VMEM_LIMIT)


def inner_kernel(own_ref, amps_ref, out_ref):
    batch_count, block_rows, width = own_ref.shape
    own = own_ref[...].reshape(batch_count * block_rows, width)
    cols = amps_ref.shape[-1]
    lanes = [amps_ref[:, :, p].reshape(width, cols) for p in range(amps_ref.shape[2])]
    product = jnp.dot(own, jnp.concatenate(lanes, axis=1), preferred_element_type=jnp.float32).astype(jnp.bfloat16)
    for p in range(len(lanes)):
        for q in range(batch_count):
            out_ref[p, :, q * cols : (q + 1) * cols] = product[
                q * block_rows : (q + 1) * block_rows, p * cols : (p + 1) * cols
            ]


def inner_call(own, amps):
    batch_count, block_rows, width = own.shape
    y_count, z_count, pair_count, rows, cols = amps.shape
    step = 2
    return pl.pallas_call(
        inner_kernel,
        grid=(pair_count // step,),
        in_specs=[
            pl.BlockSpec((batch_count, block_rows, width), lambda i: (0, 0, 0)),
            pl.BlockSpec((y_count, z_count, step, rows, cols), lambda i: (0, 0, i, 0, 0)),
        ],
        out_specs=pl.BlockSpec((step, block_rows, batch_count * cols), lambda i: (i, 0, 0)),
        out_shape=jax.ShapeDtypeStruct((pair_count, block_rows, batch_count * cols), jnp.bfloat16),
        compiler_params=params(),
    )(own, amps)


def ladder_kernel(place_ref, inner_ref, near_ref, back_ref, far_ref, ahead_ref, out_ref):
    pair_count, block_rows, depth = inner_ref.shape
    inner = inner_ref[...].reshape(pair_count * block_rows, depth)

    def emit(ref):
        blocks, batch_count, rows, cols = ref.shape
        lanes = [ref[:, q].reshape(blocks * rows, cols) for q in range(batch_count)]
        factor = jnp.concatenate(lanes, axis=1)
        product = lax.dot_general(inner, factor, (((1,), (1,)), ((), ())), preferred_element_type=jnp.float32)
        product = product.astype(jnp.bfloat16)
        for k in range(out_ref.shape[0]):
            out_ref[k] = product[:, k * 128 : (k + 1) * 128].reshape(pair_count, block_rows, 128)

    step = pl.program_id(0)
    for k, ref in enumerate((near_ref, back_ref, far_ref, ahead_ref)):
        pl.when(step // 2 == k)(lambda ref=ref: emit(ref))


def ladder_call(place, inner, parts):
    pair_count, block_rows, depth = inner.shape
    y_count, batch_count, rows, cols = parts[0].shape
    half = y_count // 2
    moves = (0, 3, 2, 1)

    def out_index(i, place):
        shift = jnp.where(i // 2 == 0, 0, 4 - i // 2)
        return (lax.rem(place[0] + shift, 4) * 2 + lax.rem(i, 2), 0, 0, 0)

    def part_spec(k):
        return pl.BlockSpec((half, batch_count, rows, cols), lambda i, place: (jnp.clip(i - 2 * k, 0, 1), 0, 0, 0))

    return pl.pallas_call(
        ladder_kernel,
        grid_spec=pltpu.PrefetchScalarGridSpec(
            num_scalar_prefetch=1,
            grid=(8,),
            in_specs=[pl.BlockSpec((pair_count, block_rows, depth), lambda i, place: (0, 0, 0))]
            + [part_spec(k) for k in range(4)],
            out_specs=pl.BlockSpec((half // 2, pair_count, block_rows, 2 * rows), out_index),
        ),
        out_shape=jax.ShapeDtypeStruct((16, pair_count, block_rows, 2 * rows), jnp.bfloat16),
        compiler_params=params(),
    )(place, inner, *parts)


def reduce_kernel(info_ref, part_ref, kept_ref, same_ref, other_ref):
    weight = info_ref[0].astype(jnp.float32)
    side = info_ref[1]
    halves = []
    for p in range(2):
        total = part_ref[0, p].astype(jnp.float32)
        for k in range(1, part_ref.shape[0]):
            total = total + part_ref[k, p].astype(jnp.float32)
        total = total * weight
        kept_ref[p] = total
        halves.append(total.T)
    turned = jnp.concatenate(halves, axis=1).astype(jnp.bfloat16)
    low, high = turned[:64], turned[64:]
    same_ref[0] = jnp.where(side == 0, low, high)
    other_ref[0] = jnp.where(side == 0, high, low)


def reduce_call(info, pieces):
    sources, pair_count, rows, cols = pieces.shape
    return pl.pallas_call(
        reduce_kernel,
        grid_spec=pltpu.PrefetchScalarGridSpec(
            num_scalar_prefetch=1,
            grid=(pair_count // 2,),
            in_specs=[pl.BlockSpec((sources, 2, rows, cols), lambda i, info: (0, i, 0, 0))],
            out_specs=[
                pl.BlockSpec((2, rows, cols), lambda i, info: (i, 0, 0)),
                pl.BlockSpec((1, rows, cols), lambda i, info: (i, 0, 0)),
                pl.BlockSpec((1, rows, cols), lambda i, info: (i, 0, 0)),
            ],
        ),
        out_shape=[
            jax.ShapeDtypeStruct((pair_count, rows, cols), jnp.float32),
            jax.ShapeDtypeStruct((pair_count // 2, rows, cols), jnp.bfloat16),
            jax.ShapeDtypeStruct((pair_count // 2, rows, cols), jnp.bfloat16),
        ],
        compiler_params=params(),
    )(info, pieces)


def combine_kernel(info_ref, partner_ref, kept_ref, same_ref, other_ref, out_ref):
    side = info_ref[1]
    pair_count, rows, cols = kept_ref.shape
    half = cols // 2
    for p in range(pair_count):
        mate = partner_ref[p]
        odd = lax.rem(mate, 2) == 1
        same = same_ref[mate // 2].astype(jnp.float32)
        other = other_ref[mate // 2].astype(jnp.float32)
        same = jnp.where(odd, same[:, half:], same[:, :half])
        other = jnp.where(odd, other[:, half:], other[:, :half])
        first = jnp.where(side == 0, same, other)
        second = jnp.where(side == 0, other, same)
        total = kept_ref[p] + jnp.concatenate([first, second], axis=1)
        for k in range(16):
            out_ref[k, p * 4 : (p + 1) * 4, :] = total[k * 4 : (k + 1) * 4]


def combine_call(info, partner, kept, same, other):
    pair_count, rows, cols = kept.shape
    smem = pl.BlockSpec(memory_space=pltpu.SMEM)
    vmem = pl.BlockSpec(memory_space=pltpu.VMEM)
    return pl.pallas_call(
        combine_kernel,
        in_specs=[smem, smem, vmem, vmem, vmem],
        out_specs=vmem,
        out_shape=jax.ShapeDtypeStruct((16, pair_count * rows // 16, cols), jnp.float32),
        compiler_params=params(),
    )(info, partner, kept, same, other)


def turn(count, step):
    return [(i, (i + step) % count) for i in range(count)]


def mirror_pairs(other):
    pairs = []
    for r in range(16):
        for c in range(32):
            side = 1 - c % 2 if other else c % 2
            pairs.append((r * 32 + c, (c // 2) * 32 + 2 * r + side))
    return pairs


def on_device(amplitudes, factors, amp_mask, out_mask, partner):
    pair_count, amp_rows, amp_cols = amplitudes.shape
    batch_count, block_rows, full_width = factors.shape
    r = lax.axis_index(ROW)
    c = lax.axis_index(COL)
    zh = lax.axis_index("zh")
    masked = amplitudes * amp_mask[c // 2, r].astype(jnp.bfloat16)

    block = lax.dynamic_slice_in_dim(factors, r * amp_cols, amp_cols, 2)
    near = lax.all_gather(block, "y", axis=0)
    amps = lax.all_gather(lax.all_gather(masked, "zh", axis=0), "y", axis=0)

    back = lax.ppermute(near, "zh", turn(4, 1))
    ahead = lax.ppermute(near, "zh", turn(4, -1))
    far = jnp.concatenate(
        [lax.ppermute(back[:4], "zh", turn(4, 1)), lax.ppermute(ahead[4:], "zh", turn(4, -1))], axis=0
    )
    own = factors.reshape(batch_count, block_rows, 4, 8, 64).transpose(0, 1, 3, 2, 4)
    own = own.reshape(batch_count, block_rows, full_width)

    inner = inner_call(own, amps)
    partial = ladder_call(zh.reshape(1), inner, (near, back, far, ahead))
    pieces = lax.all_to_all(partial, ROW, split_axis=0, concat_axis=0)
    info = jnp.stack([out_mask[c // 2, r], c % 2])
    kept, same, other = reduce_call(info, pieces)
    same = lax.ppermute(same, ALL, mirror_pairs(False))
    other = lax.ppermute(other, ALL, mirror_pairs(True))
    rows = lax.all_to_all(combine_call(info, partner, kept, same, other), ROW, split_axis=0, concat_axis=0)
    rows = rows.reshape(16, pair_count, 4, 128).transpose(1, 2, 0, 3)
    return rows.reshape(pair_count, 4, full_width)


def solution(mesh):
    fine = Mesh(mesh.devices.reshape(2, 4, 2, 4, 8), ALL)
    return jax.shard_map(
        on_device,
        mesh=fine,
        in_specs=(P(None, COL, ROW), P(None, COL, None), P(), P(), P()),
        out_specs=P(None, COL + ROW, None),
        check_vma=False,
    )
```

time: 377 us -> 236 us (0.63)
  waiting for transfers between devices: 269 us -> 92.4 us
  starting transfers between devices: 0.09 us -> 41.8 us
  matrix products: 13.7 us -> 0 us
  Pallas kernels: 0 us -> 13 us
  local copies, waits for them, and re-layouts: 36.4 us -> 25.5 us
  blocking collectives: 36.9 us -> 45.9 us
    all_gather x2, waiting for transfers between devices: 205 us -> 19.6 us  [the longest x1 19.6 us: on_device(): near = lax.all_gather(block, 'y', axis=0)]
    reduce_scatter x1 -> x0, waiting for transfers between devices: 64.3 us -> none  [on_device(): lax.psum_scatter(partial_sums, 'row', scatter_dimension=1, tiled=True)]
    ppermute x0 -> x6, waiting for transfers between devices: none -> 46.8 us  [the longest x1 41.8 us: on_device(): ahead = lax.ppermute(near, 'zh', turn(4, -1))]
    all_to_all x0 -> x1, waiting for transfers between devices: none -> 25.9 us  [on_device(): pieces = lax.all_to_all(partial, ROW, split_axis=0, concat_axis=0)]
    ppermute x0 -> x6, starting transfers between devices: none -> 22.8 us  [the longest x1 5.9 us: on_device(): ahead = lax.ppermute(near, 'zh', turn(4, -1))]
    all_gather x0 -> x1, blocking collectives: none -> 21 us  [on_device(): amps = lax.all_gather(lax.all_gather(masked, 'zh', axis=0), 'y', axis=0)]
    all_to_all x0 -> x1, starting transfers between devices: none -> 19 us  [on_device(): pieces = lax.all_to_all(partial, ROW, split_axis=0, concat_axis=0)]
    dot_general x7 -> x0, matrix products: 13.7 us -> none  [the longest x1 6.65 us: on_device(): jnp.einsum('pqad,qbd->pab', inner, lax.all_gather(factor_block, 'col', ax...]
  transfers between devices with their start and end apart: 3 -> 9, of which waited for: 3 -> 4; matrix products, arithmetic and copies ran while one was open for 2% -> 10% of each run, Pallas kernels for 0% -> 0%
where the time goes in v1:
time: 236 us
  waiting for transfers between devices  92.4 us (39%)
  blocking collectives  45.9 us (19%)
  starting transfers between devices  41.8 us (18%)
  local copies, waits for them, and re-layouts  25.5 us (11%)
  between operations  14.2 us (6%)
  Pallas kernels  13 us (6%)
  other arithmetic  2.9 us (1%)
    ppermute x1, waiting for transfers between devices, on_device(): ahead = lax.ppermute(near, 'zh', turn(4, -1))  41.8 us
    all_to_all x1, waiting for transfers between devices, on_device(): pieces = lax.all_to_all(partial, ROW, split_axis=0, concat_axis=0)  25.9 us
    all_to_all x1, blocking collectives, on_device(): lax.all_to_all(combine_call(info, partner, kept, same, other), ROW, split...  24.9 us
    all_gather x1, blocking collectives, on_device(): amps = lax.all_gather(lax.all_gather(masked, 'zh', axis=0), 'y', axis=0)  21 us
    all_gather x1, waiting for transfers between devices, on_device(): near = lax.all_gather(block, 'y', axis=0)  19.6 us
    all_to_all x1, starting transfers between devices, on_device(): pieces = lax.all_to_all(partial, ROW, split_axis=0, concat_axis=0)  19 us
    reshape x2, local copies, waits for them, and re-layouts, on_device(): factors.reshape(batch_count, block_rows, 4, 8, 64).transpose(0, 1, 3, 2, 4)  11.7 us
    reshape x1, local copies, waits for them, and re-layouts, on_device(): own = own.reshape(batch_count, block_rows, full_width)  6.69 us
  transfers between devices with their start and end apart: 9, of which 4 were waited for; matrix products, arithmetic and copies ran while one was open for 10% of the time, Pallas kernels for 0%

profile of v1, /device:TPU:1, one launch (start us, length us, event | category | flops | bytes accessed | tf_op | source)
XLA Modules:
  0.0 235.8 jit_solution(9485188863017588840)
XLA Ops:
  6.5 0.0 all-gather.8.cloned.1.call-start
  6.5 1.7 constant_dynamic-slice_fusion
  8.3 0.0 all-gather.8.cloned.1.call-update
  8.3 0.0 all-gather.6.cloned.1.call-start
  8.4 1.2 dynamic_slice.10
  10.2 0.9 broadcast_multiply_fusion
  11.1 21.0 %all-gather = bf16[32,64,128]{2,1,0:T(8,128)(2,1)} all-gather(bf16[8,64,128]{2,1,0:T(8,128)(2,1)S(1)} %broadcast_multiply_fusion), channel_id=2, replica_groups=mesh['zl'=2,'x'=4,'core'=2,'zh'=4,'y'=8] {'zh'}, dimensions={0}, use_global_device_ids=true | all-gather | bytes 655360 | tf_op jit(solution)/shard_map/all_gather | solution.py:187
  32.1 0.0 all-gather.6.cloned.1.call-update
  32.1 19.6 %all-gather.8.cloned.1.call-done = bf16[64,64,128]{2,1,0:T(8,128)(2,1)} async-done(((bf16[8,64,128]{2,1,0:T(8,128)(2,1)}), bf16[64,64,128]{2,1,0:T(8,128)(2,1)}) %all-gather.8.cloned.1.call-update) | async-done | bytes 1048592 | tf_op jit(solution)/shard_map/all_gather | solution.py:186
  51.7 5.9 %collective-permute-start.2 = (bf16[8,8,64,128]{3,2,1,0:T(8,128)(2,1)}, bf16[8,8,64,128]{3,2,1,0:T(8,128)(2,1)S(1)}, u32[]{:S(2)}, u32[]{:S(2)}) collective-permute-start(bf16[8,8,64,128]{3,2,1,0:T(8,128)(2,1)} %bitcast.17), channel_id=1, source_target_pairs={{0,24},{8,0},{16,8},{24,16},{1,25},{9,1},{17,9},{25,17},{2,26},{10... | collective-permute-start | bytes 3145736 | tf_op jit(solution)/shard_map/ppermute | solution.py:190
  57.7 1.9 collective-permute-start
  59.6 41.8 %collective-permute-done.2.ahead_ref = bf16[8,8,64,128]{3,2,1,0:T(8,128)(2,1)S(1)} collective-permute-done((bf16[8,8,64,128]{3,2,1,0:T(8,128)(2,1)}, bf16[8,8,64,128]{3,2,1,0:T(8,128)(2,1)S(1)}, u32[]{:S(2)}, u32[]{:S(2)}) %collective-permute-start.2) | collective-permute-done | bytes 1048608 | tf_op jit(solution)/shard_map/ppermute | solution.py:190
  101.4 0.0 copy-start
  101.4 1.0 copy-done
  102.4 5.5 %collective-permute-start.3 = (bf16[4,8,64,128]{3,2,1,0:T(8,128)(2,1)S(1)}, bf16[4,8,64,128]{3,2,1,0:T(8,128)(2,1)}, u32[]{:S(2)}, u32[]{:S(2)}) collective-permute-start(bf16[4,8,64,128]{3,2,1,0:T(8,128)(2,1)S(1)} %slice.9), channel_id=1, source_target_pairs={{0,24},{8,0},{16,8},{24,16},{1,25},{9,1},{17,9},{25,17},{2,26},{10... | collective-permute-start | bytes 1572872 | tf_op jit(solution)/shard_map/ppermute | solution.py:192
  107.9 0.0 collective-permute-done.back_ref
  108.0 0.0 copy-start.2
  108.0 1.0 copy-done.2
  109.0 1.9 collective-permute-start.1
  110.9 0.0 copy-done.6
  110.9 5.4 %reshape.17 = bf16[8,64,4,8,64]{4,3,2,1,0:T(8,128)(2,1)} reshape(bf16[8,64,2048]{2,1,0:T(8,128)(2,1)S(1)} %copy-done.6) | data formatting | bytes 4194304 | tf_op jit(solution)/shard_map/reshape | solution.py:194
  116.3 6.3 %copy.13 = bf16[8,64,4,8,64]{4,2,3,1,0:T(4,128)(2,1)} copy(bf16[8,64,4,8,64]{4,3,2,1,0:T(8,128)(2,1)} %reshape.17) | data formatting | bytes 4194304 | tf_op jit(solution)/shard_map/reshape | solution.py:194
  122.6 6.7 %reshape.18.own_ref = bf16[8,64,2048]{2,1,0:T(8,128)(2,1)S(1)} reshape(bf16[8,64,8,4,64]{4,3,2,1,0:T(4,128)(2,1)} %bitcast.20) | data formatting | bytes 4194304 | tf_op jit(solution)/shard_map/reshape | solution.py:195
  129.3 0.0 collective-permute-done.3
  129.3 0.0 collective-permute-done.1
  129.3 1.3 pad_maximum_fusion.far_ref
  130.6 0.0 all-gather.6.cloned.1.call-done
  130.7 0.0 copy-start.1
  130.7 0.0 copy-start.3
  130.7 0.0 copy-start.4
  130.7 4.9 %shard_map.55.inner_ref = bf16[8,64,1024]{2,1,0:T(8,128)(2,1)S(1)} custom-call(bf16[8,64,2048]{2,1,0:T(8,128)(2,1)S(1)} %reshape.18.own_ref, bf16[8,4,8,64,128]{4,3,2,1,0:T(8,128)(2,1)} %bitcast.21), custom_call_target="tpu_custom_call" | custom-call | tf_op jit(solution)/shard_map/pallas_call | solution.py:35
  135.6 0.0 copy-done.1
  135.6 0.0 copy-done.3
  135.6 0.0 copy-done.4
  135.6 5.6 %shard_map.56 = bf16[16,8,64,128]{3,2,1,0:T(8,128)(2,1)} custom-call(s32[1]{0:T(128)} %bitcast.2.place_ref, bf16[8,64,1024]{2,1,0:T(8,128)(2,1)S(1)} %shard_map.55.inner_ref, bf16[8,8,64,128]{3,2,1,0:T(8,128)(2,1)S(1)} %bitcast.19, bf16[8,8,64,128]{3,2,1,0:T(8,128)(2,1)S(1)} %copy-done.3, bf16[8,8,64,128]{3,2,1,0:T(8,128)(2,1)S(1)} %pad_maximum_fusion.far_ref, ...), custom_call_target="tpu_custom_call" | custom-call | tf_op jit(solution)/shard_map/pallas_call | solution.py:79
  141.2 19.0 %all-to-all-start = ((bf16[16,8,64,128]{3,2,1,0:T(8,128)(2,1)}), bf16[16,8,64,128]{3,2,1,0:T(8,128)(2,1)S(1)}, u32[]{:S(2)}, u32[]{:S(2)}) async-start(bf16[16,8,64,128]{3,2,1,0:T(8,128)(2,1)} %shard_map.56), calls=%async_computation | async-start | bytes 4194304 | tf_op jit(solution)/shard_map/all_to_all | solution.py:199
  160.3 1.3 dynamic_slice.9
  161.6 0.7 pad_add_fusion.info_ref
  162.3 25.9 %all-to-all-done.part_ref = bf16[16,8,64,128]{3,2,1,0:T(8,128)(2,1)S(1)} async-done(((bf16[16,8,64,128]{3,2,1,0:T(8,128)(2,1)}), bf16[16,8,64,128]{3,2,1,0:T(8,128)(2,1)S(1)}, u32[]{:S(2)}, u32[]{:S(2)}) %all-to-all-start) | async-done | bytes 2097184 | tf_op jit(solution)/shard_map/all_to_all | solution.py:199
  188.3 1.7 shard_map.57
  190.0 4.8 %collective-permute-start.4 = (bf16[4,64,128]{2,1,0:T(8,128)(2,1)S(1)}, bf16[4,64,128]{2,1,0:T(8,128)(2,1)S(1)}, u32[]{:S(2)}, u32[]{:S(2)}) collective-permute-start(bf16[4,64,128]{2,1,0:T(8,128)(2,1)S(1)} %get-tuple-element.9), channel_id=1, source_target_pairs={{0,0},{1,1},{2,32},{3,33},{4,64},{5,65},{6,96},{7,97},{8,128},{9,1... | collective-permute-start | bytes 196616 | tf_op jit(solution)/shard_map/ppermute | solution.py:202
  194.7 2.7 %collective-permute-start.5 = (bf16[4,64,128]{2,1,0:T(8,128)(2,1)S(1)}, bf16[4,64,128]{2,1,0:T(8,128)(2,1)S(1)}, u32[]{:S(2)}, u32[]{:S(2)}) collective-permute-start(bf16[4,64,128]{2,1,0:T(8,128)(2,1)S(1)} %get-tuple-element.10), channel_id=1, source_target_pairs={{0,1},{1,0},{2,33},{3,32},{4,65},{5,64},{6,97},{7,96},{8,129},{9,1... | collective-permute-start | bytes 196616 | tf_op jit(solution)/shard_map/ppermute | solution.py:203
  197.5 0.0 collective-permute-done.4.same_ref
  197.5 5.0 %collective-permute-done.5.other_ref = bf16[4,64,128]{2,1,0:T(8,128)(2,1)S(1)} collective-permute-done((bf16[4,64,128]{2,1,0:T(8,128)(2,1)S(1)}, bf16[4,64,128]{2,1,0:T(8,128)(2,1)S(1)}, u32[]{:S(2)}, u32[]{:S(2)}) %collective-permute-start.5) | collective-permute-done | bytes 65568 | tf_op jit(solution)/shard_map/ppermute | solution.py:203
  202.5 0.0 copy-done.5
  202.5 0.8 shard_map.58
  203.3 24.9 %all_to_all.10 = f32[16,32,128]{2,1,0:T(8,128)S(1)} all-to-all(f32[16,32,128]{2,1,0:T(8,128)S(1)} %shard_map.58), channel_id=1, replica_groups=mesh['zl'=2,'x'=4,'core'=2,'zh'=4,'y'=8] {'zl','x','core'}, dimensions={0} | all-to-all | bytes 524288 | tf_op jit(solution)/shard_map/all_to_all | solution.py:204
  228.2 0.8 copy.14
  (4 shorter events, 0.1 us)
Async XLA Ops:
  6.5 104.4 %copy-start.6 = (bf16[8,64,2048]{2,1,0:T(8,128)(2,1)S(1)}, bf16[8,64,2048]{2,1,0:T(8,128)(2,1)}, u32[]{:S(2)}) copy-start(bf16[8,64,2048]{2,1,0:T(8,128)(2,1)} %param.6) | copy-start | bytes 6291460
  6.5 45.2 %all-gather.8.cloned.1.call-start = ((), (), s32[]{:S(2)}) async-start(), calls=%async_computation.3 | async-start | bytes 1179648 | tf_op jit(solution)/shard_map/all_gather | solution.py:186
  8.3 122.4 %all-gather.6.cloned.1.call-start = ((), (), s32[]{:S(2)}) async-start(), calls=%async_computation.2 | async-start | bytes 4718592 | tf_op jit(solution)/shard_map/all_gather | solution.py:187
  51.7 49.6 %collective-permute-start.2 = (bf16[8,8,64,128]{3,2,1,0:T(8,128)(2,1)}, bf16[8,8,64,128]{3,2,1,0:T(8,128)(2,1)S(1)}, u32[]{:S(2)}, u32[]{:S(2)}) collective-permute-start(bf16[8,8,64,128]{3,2,1,0:T(8,128)(2,1)} %bitcast.17), channel_id=1, source_target_pairs={{0,24},{8,0},{16,8},{24,16},{1,25},{9,1},{17,9},{25,17},{2,26},{10... | collective-permute-start | bytes 3145736 | tf_op jit(solution)/shard_map/ppermute | solution.py:190
  57.7 50.3 %collective-permute-start = (bf16[8,8,64,128]{3,2,1,0:T(8,128)(2,1)}, bf16[8,8,64,128]{3,2,1,0:T(8,128)(2,1)S(1)}, u32[]{:S(2)}, u32[]{:S(2)}) collective-permute-start(bf16[8,8,64,128]{3,2,1,0:T(8,128)(2,1)} %bitcast.18), channel_id=1, source_target_pairs={{0,8},{8,16},{16,24},{24,0},{1,9},{9,17},{17,25},{25,1},{2,10},{10... | collective-permute-start | bytes 3145736 | tf_op jit(solution)/shard_map/ppermute | solution.py:189
  101.4 1.0 copy-start
  102.4 26.9 %collective-permute-start.3 = (bf16[4,8,64,128]{3,2,1,0:T(8,128)(2,1)S(1)}, bf16[4,8,64,128]{3,2,1,0:T(8,128)(2,1)}, u32[]{:S(2)}, u32[]{:S(2)}) collective-permute-start(bf16[4,8,64,128]{3,2,1,0:T(8,128)(2,1)S(1)} %slice.9), channel_id=1, source_target_pairs={{0,24},{8,0},{16,8},{24,16},{1,25},{9,1},{17,9},{25,17},{2,26},{10... | collective-permute-start | bytes 1572872 | tf_op jit(solution)/shard_map/ppermute | solution.py:192
  108.0 1.0 copy-start.2
  109.0 20.4 %collective-permute-start.1 = (bf16[4,8,64,128]{3,2,1,0:T(8,128)(2,1)S(1)}, bf16[4,8,64,128]{3,2,1,0:T(8,128)(2,1)}, u32[]{:S(2)}, u32[]{:S(2)}) collective-permute-start(bf16[4,8,64,128]{3,2,1,0:T(8,128)(2,1)S(1)} %slice.8), channel_id=1, source_target_pairs={{0,8},{8,16},{16,24},{24,0},{1,9},{9,17},{17,25},{25,1},{2,10},{10... | collective-permute-start | bytes 1572872 | tf_op jit(solution)/shard_map/ppermute | solution.py:192
  130.7 4.9 %copy-start.1 = (bf16[8,8,64,128]{3,2,1,0:T(8,128)(2,1)S(1)}, bf16[8,8,64,128]{3,2,1,0:T(8,128)(2,1)}, u32[]{:S(2)}) copy-start(bf16[8,8,64,128]{3,2,1,0:T(8,128)(2,1)} %copy-done) | copy-start | bytes 3145732
  130.7 4.9 %copy-start.3 = (bf16[8,8,64,128]{3,2,1,0:T(8,128)(2,1)S(1)}, bf16[8,8,64,128]{3,2,1,0:T(8,128)(2,1)}, u32[]{:S(2)}) copy-start(bf16[8,8,64,128]{3,2,1,0:T(8,128)(2,1)} %copy-done.2) | copy-start | bytes 3145732
  130.7 4.9 %copy-start.4 = (bf16[64,64,128]{2,1,0:T(8,128)(2,1)S(1)}, bf16[64,64,128]{2,1,0:T(8,128)(2,1)}, u32[]{:S(2)}) copy-start(bf16[64,64,128]{2,1,0:T(8,128)(2,1)} %all-gather.8.cloned.1.call-done) | copy-start | bytes 3145732
  141.2 47.0 %all-to-all-start = ((bf16[16,8,64,128]{3,2,1,0:T(8,128)(2,1)}), bf16[16,8,64,128]{3,2,1,0:T(8,128)(2,1)S(1)}, u32[]{:S(2)}, u32[]{:S(2)}) async-start(bf16[16,8,64,128]{3,2,1,0:T(8,128)(2,1)} %shard_map.56), calls=%async_computation | async-start | bytes 4194304 | tf_op jit(solution)/shard_map/all_to_all | solution.py:199
  160.3 42.2 %copy-start.5 = (s32[8]{0:T(128)S(1)}, s32[8]{0:T(128)}, u32[]{:S(2)}) copy-start(s32[8]{0:T(128)} %partner_ref.1) | copy-start | bytes 100
  190.0 7.5 %collective-permute-start.4 = (bf16[4,64,128]{2,1,0:T(8,128)(2,1)S(1)}, bf16[4,64,128]{2,1,0:T(8,128)(2,1)S(1)}, u32[]{:S(2)}, u32[]{:S(2)}) collective-permute-start(bf16[4,64,128]{2,1,0:T(8,128)(2,1)S(1)} %get-tuple-element.9), channel_id=1, source_target_pairs={{0,0},{1,1},{2,32},{3,33},{4,64},{5,65},{6,96},{7,97},{8,128},{9,1... | collective-permute-start | bytes 196616 | tf_op jit(solution)/shard_map/ppermute | solution.py:202
  194.7 7.8 %collective-permute-start.5 = (bf16[4,64,128]{2,1,0:T(8,128)(2,1)S(1)}, bf16[4,64,128]{2,1,0:T(8,128)(2,1)S(1)}, u32[]{:S(2)}, u32[]{:S(2)}) collective-permute-start(bf16[4,64,128]{2,1,0:T(8,128)(2,1)S(1)} %get-tuple-element.10), channel_id=1, source_target_pairs={{0,1},{1,0},{2,33},{3,32},{4,65},{5,64},{6,97},{7,96},{8,129},{9,1... | collective-permute-start | bytes 196616 | tf_op jit(solution)/shard_map/ppermute | solution.py:203
Sparse Core Ops, SparseCore 0:
  9.4 42.2 all-gather.7
  53.8 60.3 all-gather.5

commit v2 on v1

--- a/solution.py
+++ b/solution.py
@@ -15,79 +15,157 @@
     return pltpu.CompilerParams(vmem_limit_bytes=VMEM_LIMIT)
 
 
-def inner_kernel(own_ref, amps_ref, out_ref):
-    batch_count, block_rows, width = own_ref.shape
-    own = own_ref[...].reshape(batch_count * block_rows, width)
-    cols = amps_ref.shape[-1]
-    lanes = [amps_ref[:, :, p].reshape(width, cols) for p in range(amps_ref.shape[2])]
-    product = jnp.dot(own, jnp.concatenate(lanes, axis=1), preferred_element_type=jnp.float32).astype(jnp.bfloat16)
-    for p in range(len(lanes)):
+def prepare_kernel(info_ref, amps_ref, factor_ref, first_ref, second_ref):
+    weight = info_ref[0].astype(jnp.bfloat16)
+    batch_count = factor_ref.shape[0]
+    ring = second_ref.shape[1]
+    first_ref[:batch_count] = factor_ref[...]
+    first_ref[batch_count:] = amps_ref[ring:] * weight
+    masked = amps_ref[:ring] * weight
+    for k in range(second_ref.shape[0]):
+        second_ref[k] = masked
+
+
+def prepare_call(info, amplitudes, factors, ring, copies):
+    pair_count, rows, cols = amplitudes.shape
+    batch_count = factors.shape[0]
+    flat = batch_count + pair_count - ring
+    return pl.pallas_call(
+        prepare_kernel,
+        grid_spec=pltpu.PrefetchScalarGridSpec(
+            num_scalar_prefetch=1,
+            grid=(1,),
+            in_specs=[
+                pl.BlockSpec((pair_count, rows, cols), lambda i, info: (0, 0, 0)),
+                pl.BlockSpec((batch_count, rows, cols), lambda i, info: (0, 0, info[1])),
+            ],
+            out_specs=[
+                pl.BlockSpec((flat, rows, cols), lambda i, info: (0, 0, 0)),
+                pl.BlockSpec((copies, ring, rows, cols), lambda i, info: (0, 0, 0, 0)),
+            ],
+        ),
+        out_shape=[
+            jax.ShapeDtypeStruct((flat, rows, cols), jnp.bfloat16),
+            jax.ShapeDtypeStruct((copies, ring, rows, cols), jnp.bfloat16),
+        ],
+        compiler_params=params(),
+    )(info, amplitudes, factors)
+
+
+def spread_product(product, out_ref, batch_count, block_rows, cols):
+    product = product.astype(jnp.bfloat16)
+    for p in range(out_ref.shape[0]):
         for q in range(batch_count):
             out_ref[p, :, q * cols : (q + 1) * cols] = product[
                 q * block_rows : (q + 1) * block_rows, p * cols : (p + 1) * cols
             ]
 
 
-def inner_call(own, amps):
+def ring_kernel(place_ref, own_ref, near_ref, back_ref, ahead_ref, left_ref, right_ref, out_ref):
+    batch_count, block_rows, width = own_ref.shape
+    cols = near_ref.shape[-1]
+    group = width // 4
+
+    def term(blocks, move):
+        at = pl.multiple_of(lax.rem(place_ref[0] + move, 4) * group, group)
+        own = own_ref[:, :, pl.ds(at, group)].reshape(batch_count * block_rows, group)
+        lanes = [jnp.concatenate([ref[k, p] for ref in blocks for k in range(ref.shape[0])], axis=0) for p in range(2)]
+        return jnp.dot(own, jnp.concatenate(lanes, axis=1), preferred_element_type=jnp.float32)
+
+    product = term([near_ref], 0)
+    product = product + term([back_ref], 3)
+    product = product + term([ahead_ref], 1)
+    product = product + term([left_ref, right_ref], 2)
+    spread_product(product, out_ref, batch_count, block_rows, cols)
+
+
+def ring_call(place, own, parts):
     batch_count, block_rows, width = own.shape
-    y_count, z_count, pair_count, rows, cols = amps.shape
-    step = 2
-    return pl.pallas_call(
-        inner_kernel,
-        grid=(pair_count // step,),
+    pair_count, rows, cols = parts[0].shape[1:]
+    return pl.pallas_call(
+        ring_kernel,
+        grid_spec=pltpu.PrefetchScalarGridSpec(
+            num_scalar_prefetch=1,
+            grid=(pair_count // 2,),
+            in_specs=[pl.BlockSpec((batch_count, block_rows, width), lambda i, place: (0, 0, 0))]
+            + [pl.BlockSpec((part.shape[0], 2, rows, cols), lambda i, place: (0, i, 0, 0)) for part in parts],
+            out_specs=pl.BlockSpec((2, block_rows, batch_count * cols), lambda i, place: (i, 0, 0)),
+        ),
+        out_shape=jax.ShapeDtypeStruct((pair_count, block_rows, batch_count * cols), jnp.bfloat16),
+        compiler_params=params(),
+    )(place, own, *parts)
+
+
+def flat_kernel(own_ref, amps_ref, out_ref):
+    batch_count, block_rows, width = own_ref.shape
+    y_count, z_count, pairs, rows, cols = amps_ref.shape
+    own = own_ref[...].reshape(batch_count * block_rows, width)
+    lanes = [
+        jnp.concatenate([amps_ref[y, z, p] for z in range(z_count) for y in range(y_count)], axis=0)
+        for p in range(pairs)
+    ]
+    product = jnp.dot(own, jnp.concatenate(lanes, axis=1), preferred_element_type=jnp.float32)
+    spread_product(product, out_ref, batch_count, block_rows, cols)
+
+
+def flat_call(own, units):
+    batch_count, block_rows, width = own.shape
+    y_count, z_count, unit_count, rows, cols = units.shape
+    return pl.pallas_call(
+        flat_kernel,
+        grid=(1,),
         in_specs=[
             pl.BlockSpec((batch_count, block_rows, width), lambda i: (0, 0, 0)),
-            pl.BlockSpec((y_count, z_count, step, rows, cols), lambda i: (0, 0, i, 0, 0)),
-        ],
-        out_specs=pl.BlockSpec((step, block_rows, batch_count * cols), lambda i: (i, 0, 0)),
-        out_shape=jax.ShapeDtypeStruct((pair_count, block_rows, batch_count * cols), jnp.bfloat16),
-        compiler_params=params(),
-    )(own, amps)
-
-
-def ladder_kernel(place_ref, inner_ref, near_ref, back_ref, far_ref, ahead_ref, out_ref):
-    pair_count, block_rows, depth = inner_ref.shape
-    inner = inner_ref[...].reshape(pair_count * block_rows, depth)
-
-    def emit(ref):
-        blocks, batch_count, rows, cols = ref.shape
-        lanes = [ref[:, q].reshape(blocks * rows, cols) for q in range(batch_count)]
-        factor = jnp.concatenate(lanes, axis=1)
-        product = lax.dot_general(inner, factor, (((1,), (1,)), ((), ())), preferred_element_type=jnp.float32)
-        product = product.astype(jnp.bfloat16)
-        for k in range(out_ref.shape[0]):
-            out_ref[k] = product[:, k * 128 : (k + 1) * 128].reshape(pair_count, block_rows, 128)
-
-    step = pl.program_id(0)
-    for k, ref in enumerate((near_ref, back_ref, far_ref, ahead_ref)):
-        pl.when(step // 2 == k)(lambda ref=ref: emit(ref))
-
-
-def ladder_call(place, inner, parts):
-    pair_count, block_rows, depth = inner.shape
-    y_count, batch_count, rows, cols = parts[0].shape
+            pl.BlockSpec((y_count, z_count, 2, rows, cols), lambda i: (0, 0, batch_count // 2, 0, 0)),
+        ],
+        out_specs=pl.BlockSpec((2, block_rows, batch_count * cols), lambda i: (0, 0, 0)),
+        out_shape=jax.ShapeDtypeStruct((2, block_rows, batch_count * cols), jnp.bfloat16),
+        compiler_params=params(),
+    )(own, units)
+
+
+def ladder_kernel(core_ref, ring_ref, flat_ref, units_ref, keep_ref, send_ref):
+    y_count, z_count, batch_count, rows, cols = units_ref.shape
+    pair_count, block_rows = keep_ref.shape[1:3]
+    depth = ring_ref.shape[2]
+    inner = jnp.concatenate([ring_ref[...].reshape(-1, depth), flat_ref[...].reshape(-1, depth)], axis=0)
+    lanes = [jnp.concatenate([units_ref[y, 0, q] for y in range(y_count)], axis=0) for q in range(batch_count)]
+    factor = jnp.concatenate(lanes, axis=1)
+    product = lax.dot_general(inner, factor, (((1,), (1,)), ((), ())), preferred_element_type=jnp.float32)
+    half = product.shape[1] // 2
+    first = product[:, :half].reshape(pair_count, block_rows, half)
+    second = product[:, half:].reshape(pair_count, block_rows, half)
+    own_first = core_ref[0] == 0
+    keep_ref[0] = jnp.where(own_first, first, second)
+    send_ref[0] = jnp.where(own_first, second, first).astype(jnp.bfloat16)
+
+
+def ladder_call(core, ring, flat, units):
+    depth = ring.shape[2]
+    block_rows = ring.shape[1]
+    pair_count = ring.shape[0] + flat.shape[0]
+    y_count, z_count, unit_count, rows, cols = units.shape
+    batch_count = depth // cols
     half = y_count // 2
-    moves = (0, 3, 2, 1)
-
-    def out_index(i, place):
-        shift = jnp.where(i // 2 == 0, 0, 4 - i // 2)
-        return (lax.rem(place[0] + shift, 4) * 2 + lax.rem(i, 2), 0, 0, 0)
-
-    def part_spec(k):
-        return pl.BlockSpec((half, batch_count, rows, cols), lambda i, place: (jnp.clip(i - 2 * k, 0, 1), 0, 0, 0))
-
+    out_spec = pl.BlockSpec((1, pair_count, block_rows, 2 * rows), lambda i, core: (i, 0, 0, 0))
     return pl.pallas_call(
         ladder_kernel,
         grid_spec=pltpu.PrefetchScalarGridSpec(
             num_scalar_prefetch=1,
             grid=(8,),
-            in_specs=[pl.BlockSpec((pair_count, block_rows, depth), lambda i, place: (0, 0, 0))]
-            + [part_spec(k) for k in range(4)],
-            out_specs=pl.BlockSpec((half // 2, pair_count, block_rows, 2 * rows), out_index),
-        ),
-        out_shape=jax.ShapeDtypeStruct((16, pair_count, block_rows, 2 * rows), jnp.bfloat16),
-        compiler_params=params(),
-    )(place, inner, *parts)
+            in_specs=[
+                pl.BlockSpec(ring.shape, lambda i, core: (0, 0, 0)),
+                pl.BlockSpec(flat.shape, lambda i, core: (0, 0, 0)),
+                pl.BlockSpec((half, 1, batch_count, rows, cols), lambda i, core: (i % 2, i // 2, 0, 0, 0)),
+            ],
+            out_specs=[out_spec, out_spec],
+        ),
+        out_shape=[
+            jax.ShapeDtypeStruct((8, pair_count, block_rows, 2 * rows), jnp.float32),
+            jax.ShapeDtypeStruct((8, pair_count, block_rows, 2 * rows), jnp.bfloat16),
+        ],
+        compiler_params=params(),
+    )(core, ring, flat, units)
 
 
 def reduce_kernel(info_ref, part_ref, kept_ref, same_ref, other_ref):
@@ -180,23 +258,23 @@
     r = lax.axis_index(ROW)
     c = lax.axis_index(COL)
     zh = lax.axis_index("zh")
-    masked = amplitudes * amp_mask[c // 2, r].astype(jnp.bfloat16)
-
-    block = lax.dynamic_slice_in_dim(factors, r * amp_cols, amp_cols, 2)
-    near = lax.all_gather(block, "y", axis=0)
-    amps = lax.all_gather(lax.all_gather(masked, "zh", axis=0), "y", axis=0)
+    core = lax.axis_index("core")
+    ring = 6
+    first, second = prepare_call(jnp.stack([amp_mask[c // 2, r], r]), amplitudes, factors, ring, 8)
+    near = lax.all_to_all(second, "y", split_axis=0, concat_axis=0)
+    units = lax.all_gather(lax.all_gather(first, "zh", axis=0), "y", axis=0)
 
     back = lax.ppermute(near, "zh", turn(4, 1))
     ahead = lax.ppermute(near, "zh", turn(4, -1))
-    far = jnp.concatenate(
-        [lax.ppermute(back[:4], "zh", turn(4, 1)), lax.ppermute(ahead[4:], "zh", turn(4, -1))], axis=0
-    )
-    own = factors.reshape(batch_count, block_rows, 4, 8, 64).transpose(0, 1, 3, 2, 4)
-    own = own.reshape(batch_count, block_rows, full_width)
-
-    inner = inner_call(own, amps)
-    partial = ladder_call(zh.reshape(1), inner, (near, back, far, ahead))
-    pieces = lax.all_to_all(partial, ROW, split_axis=0, concat_axis=0)
+    left = lax.ppermute(back[:4], "zh", turn(4, 1))
+    right = lax.ppermute(ahead[4:], "zh", turn(4, -1))
+
+    ring_inner = ring_call(zh.reshape(1), factors, (near, back, ahead, left, right))
+    flat_inner = flat_call(factors, units)
+    keep, send = ladder_call(core.reshape(1), ring_inner, flat_inner, units)
+    swapped = lax.ppermute(send, "core", turn(2, 1))
+    partial = (keep + swapped.astype(jnp.float32)).astype(jnp.bfloat16)
+    pieces = lax.all_to_all(partial, ("zl", "x"), split_axis=0, concat_axis=0)
     info = jnp.stack([out_mask[c // 2, r], c % 2])
     kept, same, other = reduce_call(info, pieces)
     same = lax.ppermute(same, ALL, mirror_pairs(False))

time: 236 us -> 209 us (0.89)
  waiting for transfers between devices: 92.4 us -> 50.5 us
  blocking collectives: 45.9 us -> 76.3 us
  local copies, waits for them, and re-layouts: 25.5 us -> 5.93 us
  starting transfers between devices: 41.8 us -> 44.6 us
    ppermute x1, waiting for transfers between devices: 41.8 us -> 0.01 us  [on_device(): ahead = lax.ppermute(near, 'zh', turn(4, -1))]
    all_to_all x0 -> x1, blocking collectives: none -> 28.9 us  [on_device(): near = lax.all_to_all(second, 'y', split_axis=0, concat_axis=0)]
    ppermute x2 -> x3, waiting for transfers between devices: 0.01 us -> 25.3 us  [the longest x1 22.6 us: on_device(): left = lax.ppermute(back[:4], 'zh', turn(4, 1))]
    all_gather x2 -> x1, waiting for transfers between devices: 19.6 us -> 0.02 us  [on_device(): units = lax.all_gather(lax.all_gather(first, 'zh', axis=0), 'y', axis=0)]
    reshape x3 -> x0, local copies, waits for them, and re-layouts: 18.4 us -> none  [the longest x2 11.7 us: on_device(): factors.reshape(batch_count, block_rows, 4, 8, 64).transpose(0, 1, 3, 2, 4)]
    all_to_all x1, waiting for transfers between devices: 25.9 us -> 13 us  [on_device(): pieces = lax.all_to_all(partial, ('zl', 'x'), split_axis=0, concat_axis=0)]
    ppermute x1, waiting for transfers between devices: 0.01 us -> 9.12 us  [on_device(): back = lax.ppermute(near, 'zh', turn(4, 1))]
    ppermute x2 -> x3, starting transfers between devices: 7.44 us -> 14.8 us  [the longest x1 7.42 us: on_device(): swapped = lax.ppermute(send, 'core', turn(2, 1))]
  transfers between devices with their start and end apart: 9 -> 9, of which waited for: 4 -> 6; matrix products, arithmetic and copies ran while one was open for 10% -> 1% of each run, Pallas kernels for 0% -> 1%
where the time goes in v2:
time: 209 us; the launch traced here: 208 us
  blocking collectives  76.3 us (37%)
  waiting for transfers between devices  50.5 us (24%)
  starting transfers between devices  44.6 us (21%)
  Pallas kernels  14.2 us (7%)
  between operations  13.5 us (6%)
  local copies, waits for them, and re-layouts  5.93 us (3%)
  other arithmetic  2.76 us (1%)
    all_to_all x1, blocking collectives, on_device(): near = lax.all_to_all(second, 'y', split_axis=0, concat_axis=0)  28.9 us
    all_to_all x1, blocking collectives, on_device(): lax.all_to_all(combine_call(info, partner, kept, same, other), ROW, split...  24.3 us
    all_gather x1, blocking collectives, on_device(): units = lax.all_gather(lax.all_gather(first, 'zh', axis=0), 'y', axis=0)  23.1 us
    ppermute x1, waiting for transfers between devices, on_device(): left = lax.ppermute(back[:4], 'zh', turn(4, 1))  22.6 us
    all_to_all x1, starting transfers between devices, on_device(): pieces = lax.all_to_all(partial, ('zl', 'x'), split_axis=0, concat_axis=0)  14.1 us
    all_to_all x1, waiting for transfers between devices, on_device(): pieces = lax.all_to_all(partial, ('zl', 'x'), split_axis=0, concat_axis=0)  13 us
    ppermute x1, waiting for transfers between devices, on_device(): back = lax.ppermute(near, 'zh', turn(4, 1))  9.12 us
    ppermute x1, starting transfers between devices, on_device(): swapped = lax.ppermute(send, 'core', turn(2, 1))  7.42 us
  transfers between devices with their start and end apart: 9, of which 6 were waited for; matrix products, arithmetic and copies ran while one was open for 1% of the time, Pallas kernels for 1%

profile of v2, /device:TPU:1, one launch (start us, length us, event | category | flops | bytes accessed | tf_op | source)
XLA Modules:
  0.0 207.8 jit_solution(964558017448845459)
XLA Ops:
  6.5 0.0 all-gather.4.cloned.1.call-start
  6.5 1.3 dynamic_slice.7
  7.9 0.8 pad_add_fusion.1.info_ref
  8.6 0.0 copy-start
  8.6 1.6 copy-done
  10.2 0.0 copy-start.2
  10.2 0.9 copy-done.2
  11.1 0.7 shard_map.55
  11.8 23.1 %all-gather = bf16[40,64,128]{2,1,0:T(8,128)(2,1)} all-gather(bf16[10,64,128]{2,1,0:T(8,128)(2,1)S(1)} %get-tuple-element.13), channel_id=2, replica_groups=mesh['zl'=2,'x'=4,'core'=2,'zh'=4,'y'=8] {'zh'}, dimensions={0}, use_global_device_ids=true | all-gather | bytes 819200 | tf_op jit(solution)/shard_map/all_gather | solution.py:265
  34.9 0.0 copy-start.1
  34.9 0.0 all-gather.4.cloned.1.call-update
  35.0 28.9 %all_to_all.15.near_ref = bf16[8,6,64,128]{3,2,1,0:T(8,128)(2,1)S(1)} all-to-all(bf16[8,6,64,128]{3,2,1,0:T(8,128)(2,1)S(1)} %get-tuple-element.12), channel_id=1, replica_groups=mesh['zl'=2,'x'=4,'core'=2,'zh'=4,'y'=8] {'y'}, dimensions={0} | all-to-all | bytes 1572864 | tf_op jit(solution)/shard_map/all_to_all | solution.py:264
  63.8 1.9 collective-permute-start
  65.8 5.5 %collective-permute-start.1 = (bf16[8,6,64,128]{3,2,1,0:T(8,128)(2,1)S(1)}, bf16[8,6,64,128]{3,2,1,0:T(8,128)(2,1)S(1)}, u32[]{:S(2)}, u32[]{:S(2)}) collective-permute-start(bf16[8,6,64,128]{3,2,1,0:T(8,128)(2,1)S(1)} %all_to_all.15.near_ref), channel_id=1, source_target_pairs={{0,24},{8,0},{16,8},{24,16},{1,25},{9,1},{17,9},{25,17},{2,26},{10... | collective-permute-start | bytes 2359304 | tf_op jit(solution)/shard_map/ppermute | solution.py:268
  71.2 9.1 %collective-permute-done.back_ref = bf16[8,6,64,128]{3,2,1,0:T(8,128)(2,1)S(1)} collective-permute-done((bf16[8,6,64,128]{3,2,1,0:T(8,128)(2,1)S(1)}, bf16[8,6,64,128]{3,2,1,0:T(8,128)(2,1)S(1)}, u32[]{:S(2)}, u32[]{:S(2)}) %collective-permute-start) | collective-permute-done | bytes 786464 | tf_op jit(solution)/shard_map/ppermute | solution.py:267
  80.4 1.9 collective-permute-start.2
  82.3 0.0 collective-permute-done.1.ahead_ref
  82.4 5.5 %collective-permute-start.3 = (bf16[4,6,64,128]{3,2,1,0:T(8,128)(2,1)S(1)}, bf16[4,6,64,128]{3,2,1,0:T(8,128)(2,1)S(1)}, u32[]{:S(2)}, u32[]{:S(2)}) collective-permute-start(bf16[4,6,64,128]{3,2,1,0:T(8,128)(2,1)S(1)} %slice.9), channel_id=1, source_target_pairs={{0,24},{8,0},{16,8},{24,16},{1,25},{9,1},{17,9},{25,17},{2,26},{10... | collective-permute-start | bytes 1179656 | tf_op jit(solution)/shard_map/ppermute | solution.py:270
  87.8 22.6 %collective-permute-done.2.left_ref = bf16[4,6,64,128]{3,2,1,0:T(8,128)(2,1)S(1)} collective-permute-done((bf16[4,6,64,128]{3,2,1,0:T(8,128)(2,1)S(1)}, bf16[4,6,64,128]{3,2,1,0:T(8,128)(2,1)S(1)}, u32[]{:S(2)}, u32[]{:S(2)}) %collective-permute-start.2) | collective-permute-done | bytes 393248 | tf_op jit(solution)/shard_map/ppermute | solution.py:269
  110.5 0.4 collective-permute-done.3.right_ref
  110.9 0.0 copy-done.1
  110.9 2.5 %shard_map.56.ring_ref = bf16[6,64,1024]{2,1,0:T(8,128)(2,1)S(1)} custom-call(s32[1]{0:T(128)} %bitcast.3.place_ref, bf16[8,64,2048]{2,1,0:T(8,128)(2,1)S(1)} %copy-done.1, bf16[8,6,64,128]{3,2,1,0:T(8,128)(2,1)S(1)} %all_to_all.15.near_ref, bf16[8,6,64,128]{3,2,1,0:T(8,128)(2,1)S(1)} %collective-permute-done.back_ref, ...), custom_call_target="tpu_custom_call" | custom-call | tf_op jit(solution)/shard_map/pallas_call | solution.py:85
  113.4 0.0 all-gather.4.cloned.1.call-done
  113.4 1.9 shard_map.57.flat_ref
  115.4 6.8 %shard_map.58 = (f32[8,8,64,128]{3,2,1,0:T(8,128)S(1)}, bf16[8,8,64,128]{3,2,1,0:T(8,128)(2,1)S(1)}) custom-call(s32[1]{0:T(128)} %bitcast.2.core_ref, bf16[6,64,1024]{2,1,0:T(8,128)(2,1)S(1)} %shard_map.56.ring_ref, bf16[2,64,1024]{2,1,0:T(8,128)(2,1)S(1)} %shard_map.57.flat_ref, bf16[8,4,10,64,128]{4,3,2,1,0:T(8,128)(2,1)} %bitcast.16), custom_call_target="tpu_custom_call" | custom-call | tf_op jit(solution)/shard_map/pallas_call | solution.py:151
  122.2 7.4 %collective-permute-start.4 = (bf16[8,8,64,128]{3,2,1,0:T(8,128)(2,1)S(1)}, bf16[8,8,64,128]{3,2,1,0:T(8,128)(2,1)S(1)}, u32[]{:S(2)}, u32[]{:S(2)}) collective-permute-start(bf16[8,8,64,128]{3,2,1,0:T(8,128)(2,1)S(1)} %get-tuple-element.15), channel_id=1, source_target_pairs={{0,32},{32,0},{1,33},{33,1},{2,34},{34,2},{3,35},{35,3},{4,36},{36... | collective-permute-start | bytes 3145736 | tf_op jit(solution)/shard_map/ppermute | solution.py:275
  129.6 2.3 %collective-permute-done.4 = bf16[8,8,64,128]{3,2,1,0:T(8,128)(2,1)S(1)} collective-permute-done((bf16[8,8,64,128]{3,2,1,0:T(8,128)(2,1)S(1)}, bf16[8,8,64,128]{3,2,1,0:T(8,128)(2,1)S(1)}, u32[]{:S(2)}, u32[]{:S(2)}) %collective-permute-start.4) | collective-permute-done | bytes 1048608 | tf_op jit(solution)/shard_map/ppermute | solution.py:275
  131.9 1.4 add_convert_fusion
  133.2 0.0 copy-start.3
  133.2 14.1 %all-to-all-start.1 = ((bf16[8,8,64,128]{3,2,1,0:T(8,128)(2,1)}), bf16[8,8,64,128]{3,2,1,0:T(8,128)(2,1)S(1)}, u32[]{:S(2)}, u32[]{:S(2)}) async-start(bf16[8,8,64,128]{3,2,1,0:T(8,128)(2,1)} %add_convert_fusion), calls=%async_computation.1 | async-start | bytes 2097152 | tf_op jit(solution)/shard_map/all_to_all | solution.py:277
  147.4 1.3 dynamic_slice.6
  148.6 0.6 pad_add_fusion.info_ref
  149.3 13.0 %all-to-all-done.1.part_ref = bf16[8,8,64,128]{3,2,1,0:T(8,128)(2,1)S(1)} async-done(((bf16[8,8,64,128]{3,2,1,0:T(8,128)(2,1)}), bf16[8,8,64,128]{3,2,1,0:T(8,128)(2,1)S(1)}, u32[]{:S(2)}, u32[]{:S(2)}) %all-to-all-start.1) | async-done | bytes 1048608 | tf_op jit(solution)/shard_map/all_to_all | solution.py:277
  162.3 1.5 shard_map.59
  163.8 3.9 %collective-permute-start.5 = (bf16[4,64,128]{2,1,0:T(8,128)(2,1)S(1)}, bf16[4,64,128]{2,1,0:T(8,128)(2,1)S(1)}, u32[]{:S(2)}, u32[]{:S(2)}) collective-permute-start(bf16[4,64,128]{2,1,0:T(8,128)(2,1)S(1)} %get-tuple-element.17), channel_id=1, source_target_pairs={{0,0},{1,1},{2,32},{3,33},{4,64},{5,65},{6,96},{7,97},{8,128},{9,1... | collective-permute-start | bytes 196616 | tf_op jit(solution)/shard_map/ppermute | solution.py:280
  167.7 4.3 %collective-permute-start.6 = (bf16[4,64,128]{2,1,0:T(8,128)(2,1)S(1)}, bf16[4,64,128]{2,1,0:T(8,128)(2,1)S(1)}, u32[]{:S(2)}, u32[]{:S(2)}) collective-permute-start(bf16[4,64,128]{2,1,0:T(8,128)(2,1)S(1)} %get-tuple-element.18), channel_id=1, source_target_pairs={{0,1},{1,0},{2,33},{3,32},{4,65},{5,64},{6,97},{7,96},{8,129},{9,1... | collective-permute-start | bytes 196616 | tf_op jit(solution)/shard_map/ppermute | solution.py:281
  172.0 0.0 collective-permute-done.5.same_ref
  172.0 3.0 %collective-permute-done.6.other_ref = bf16[4,64,128]{2,1,0:T(8,128)(2,1)S(1)} collective-permute-done((bf16[4,64,128]{2,1,0:T(8,128)(2,1)S(1)}, bf16[4,64,128]{2,1,0:T(8,128)(2,1)S(1)}, u32[]{:S(2)}, u32[]{:S(2)}) %collective-permute-start.6) | collective-permute-done | bytes 65568 | tf_op jit(solution)/shard_map/ppermute | solution.py:281
  175.1 0.0 copy-done.3
  175.1 0.8 shard_map.60
  175.9 24.3 %all_to_all.16 = f32[16,32,128]{2,1,0:T(8,128)S(1)} all-to-all(f32[16,32,128]{2,1,0:T(8,128)S(1)} %shard_map.60), channel_id=1, replica_groups=mesh['zl'=2,'x'=4,'core'=2,'zh'=4,'y'=8] {'zl','x','core'}, dimensions={0} | all-to-all | bytes 524288 | tf_op jit(solution)/shard_map/all_to_all | solution.py:282
  200.2 0.8 copy.10
  (2 shorter events, 0.1 us)
Async XLA Ops:
  6.5 106.9 %all-gather.4.cloned.1.call-start = ((), (), s32[]{:S(2)}) async-start(), calls=%async_computation.3 | async-start | bytes 5898240 | tf_op jit(solution)/shard_map/all_gather | solution.py:265
  8.6 1.6 copy-start
  10.2 0.9 copy-start.2
  34.9 76.0 %copy-start.1 = (bf16[8,64,2048]{2,1,0:T(8,128)(2,1)S(1)}, bf16[8,64,2048]{2,1,0:T(8,128)(2,1)}, u32[]{:S(2)}) copy-start(bf16[8,64,2048]{2,1,0:T(8,128)(2,1)} %own_ref.3) | copy-start | bytes 6291460
  63.8 16.5 %collective-permute-start = (bf16[8,6,64,128]{3,2,1,0:T(8,128)(2,1)S(1)}, bf16[8,6,64,128]{3,2,1,0:T(8,128)(2,1)S(1)}, u32[]{:S(2)}, u32[]{:S(2)}) collective-permute-start(bf16[8,6,64,128]{3,2,1,0:T(8,128)(2,1)S(1)} %all_to_all.15.near_ref), channel_id=1, source_target_pairs={{0,8},{8,16},{16,24},{24,0},{1,9},{9,17},{17,25},{25,1},{2,10},{10... | collective-permute-start | bytes 2359304 | tf_op jit(solution)/shard_map/ppermute | solution.py:267
  65.8 16.6 %collective-permute-start.1 = (bf16[8,6,64,128]{3,2,1,0:T(8,128)(2,1)S(1)}, bf16[8,6,64,128]{3,2,1,0:T(8,128)(2,1)S(1)}, u32[]{:S(2)}, u32[]{:S(2)}) collective-permute-start(bf16[8,6,64,128]{3,2,1,0:T(8,128)(2,1)S(1)} %all_to_all.15.near_ref), channel_id=1, source_target_pairs={{0,24},{8,0},{16,8},{24,16},{1,25},{9,1},{17,9},{25,17},{2,26},{10... | collective-permute-start | bytes 2359304 | tf_op jit(solution)/shard_map/ppermute | solution.py:268
  80.4 30.1 %collective-permute-start.2 = (bf16[4,6,64,128]{3,2,1,0:T(8,128)(2,1)S(1)}, bf16[4,6,64,128]{3,2,1,0:T(8,128)(2,1)S(1)}, u32[]{:S(2)}, u32[]{:S(2)}) collective-permute-start(bf16[4,6,64,128]{3,2,1,0:T(8,128)(2,1)S(1)} %slice.8), channel_id=1, source_target_pairs={{0,8},{8,16},{16,24},{24,0},{1,9},{9,17},{17,25},{25,1},{2,10},{10... | collective-permute-start | bytes 1179656 | tf_op jit(solution)/shard_map/ppermute | solution.py:269
  82.4 28.5 %collective-permute-start.3 = (bf16[4,6,64,128]{3,2,1,0:T(8,128)(2,1)S(1)}, bf16[4,6,64,128]{3,2,1,0:T(8,128)(2,1)S(1)}, u32[]{:S(2)}, u32[]{:S(2)}) collective-permute-start(bf16[4,6,64,128]{3,2,1,0:T(8,128)(2,1)S(1)} %slice.9), channel_id=1, source_target_pairs={{0,24},{8,0},{16,8},{24,16},{1,25},{9,1},{17,9},{25,17},{2,26},{10... | collective-permute-start | bytes 1179656 | tf_op jit(solution)/shard_map/ppermute | solution.py:270
  122.2 9.7 %collective-permute-start.4 = (bf16[8,8,64,128]{3,2,1,0:T(8,128)(2,1)S(1)}, bf16[8,8,64,128]{3,2,1,0:T(8,128)(2,1)S(1)}, u32[]{:S(2)}, u32[]{:S(2)}) collective-permute-start(bf16[8,8,64,128]{3,2,1,0:T(8,128)(2,1)S(1)} %get-tuple-element.15), channel_id=1, source_target_pairs={{0,32},{32,0},{1,33},{33,1},{2,34},{34,2},{3,35},{35,3},{4,36},{36... | collective-permute-start | bytes 3145736 | tf_op jit(solution)/shard_map/ppermute | solution.py:275
  133.2 41.9 %copy-start.3 = (s32[8]{0:T(128)S(1)}, s32[8]{0:T(128)}, u32[]{:S(2)}) copy-start(s32[8]{0:T(128)} %partner_ref.1) | copy-start | bytes 100
  133.2 29.1 %all-to-all-start.1 = ((bf16[8,8,64,128]{3,2,1,0:T(8,128)(2,1)}), bf16[8,8,64,128]{3,2,1,0:T(8,128)(2,1)S(1)}, u32[]{:S(2)}, u32[]{:S(2)}) async-start(bf16[8,8,64,128]{3,2,1,0:T(8,128)(2,1)} %add_convert_fusion), calls=%async_computation.1 | async-start | bytes 2097152 | tf_op jit(solution)/shard_map/all_to_all | solution.py:277
  163.8 8.2 %collective-permute-start.5 = (bf16[4,64,128]{2,1,0:T(8,128)(2,1)S(1)}, bf16[4,64,128]{2,1,0:T(8,128)(2,1)S(1)}, u32[]{:S(2)}, u32[]{:S(2)}) collective-permute-start(bf16[4,64,128]{2,1,0:T(8,128)(2,1)S(1)} %get-tuple-element.17), channel_id=1, source_target_pairs={{0,0},{1,1},{2,32},{3,33},{4,64},{5,65},{6,96},{7,97},{8,128},{9,1... | collective-permute-start | bytes 196616 | tf_op jit(solution)/shard_map/ppermute | solution.py:280
  167.7 7.4 %collective-permute-start.6 = (bf16[4,64,128]{2,1,0:T(8,128)(2,1)S(1)}, bf16[4,64,128]{2,1,0:T(8,128)(2,1)S(1)}, u32[]{:S(2)}, u32[]{:S(2)}) collective-permute-start(bf16[4,64,128]{2,1,0:T(8,128)(2,1)S(1)} %get-tuple-element.18), channel_id=1, source_target_pairs={{0,1},{1,0},{2,33},{3,32},{4,65},{5,64},{6,97},{7,96},{8,129},{9,1... | collective-permute-start | bytes 196616 | tf_op jit(solution)/shard_map/ppermute | solution.py:281
Sparse Core Ops, SparseCore 0:
  35.1 77.2 all-gather.3

commit v3 on v1

v3 whole, which is shorter than its diff:
```python
import jax
import jax.numpy as jnp
from jax import lax
from jax.experimental import pallas as pl
from jax.experimental.pallas import tpu as pltpu
from jax.sharding import Mesh, PartitionSpec as P

ROW = ("zl", "x", "core")
COL = ("zh", "y")
ALL = ROW + COL
MIB = 1024 * 1024


def params(mib=16):
    return pltpu.CompilerParams(vmem_limit_bytes=mib * MIB)


def place(names):
    at = lax.axis_index(names[0])
    for name in names[1:]:
        at = at * lax.axis_size(name) + lax.axis_index(name)
    return at


def prepare_kernel(mask_ref, amps_ref, factor_ref, first_ref, second_ref, copy_sem):
    batch_count, ring = factor_ref.shape[0], second_ref.shape[1]
    r = place(ROW)
    cols = amps_ref.shape[2]
    block = factor_ref.at[:, :, pl.ds(pl.multiple_of(r * cols, cols), cols)]
    copy = pltpu.make_async_copy(block, first_ref.at[:batch_count], copy_sem)
    copy.start()
    weight = mask_ref[place(COL) // 2, r].astype(jnp.float32).astype(jnp.bfloat16)
    masked = amps_ref[:ring] * weight
    for k in range(second_ref.shape[0]):
        second_ref[k] = masked
    first_ref[batch_count:] = amps_ref[ring:] * weight
    copy.wait()


def prepare_call(mask, amplitudes, factors, ring, copies):
    pair_count, rows, cols = amplitudes.shape
    flat = factors.shape[0] + pair_count - ring
    vmem = pl.BlockSpec(memory_space=pltpu.VMEM)
    return pl.pallas_call(
        prepare_kernel,
        in_specs=[pl.BlockSpec(memory_space=pltpu.SMEM), vmem, pl.BlockSpec(memory_space=pltpu.HBM)],
        out_specs=[vmem, vmem],
        out_shape=[
            jax.ShapeDtypeStruct((flat, rows, cols), jnp.bfloat16),
            jax.ShapeDtypeStruct((copies, ring, rows, cols), jnp.bfloat16),
        ],
        scratch_shapes=[pltpu.SemaphoreType.DMA],
        compiler_params=params(60),
    )(mask, amplitudes, factors)


def gate_kernel(held_ref, other_ref, out_ref):
    pass


def gate_call(held, other):
    anywhere = pl.BlockSpec(memory_space=pl.ANY)
    return pl.pallas_call(
        gate_kernel,
        in_specs=[anywhere, anywhere],
        out_specs=anywhere,
        out_shape=jax.ShapeDtypeStruct(held.shape, held.dtype),
        input_output_aliases={0: 0},
        compiler_params=params(),
    )(held, other)


def spread_product(product, out_ref, first, batch_count, block_rows):
    product = product.astype(jnp.bfloat16)
    cols = out_ref.shape[2] // batch_count
    for p in range(product.shape[1] // cols):
        for q in range(batch_count):
            out_ref[first + p, :, q * cols : (q + 1) * cols] = product[
                q * block_rows : (q + 1) * block_rows, p * cols : (p + 1) * cols
            ]


def ring_term(own_ref, blocks, move):
    batch_count, block_rows, width = own_ref.shape
    group = width // 4
    at = pl.multiple_of(lax.rem(lax.axis_index("zh") + move, 4) * group, group)
    own = own_ref[:, :, pl.ds(at, group)].reshape(batch_count * block_rows, group)
    lanes = [
        jnp.concatenate([ref[k, p] for ref in blocks for k in range(ref.shape[0])], axis=0)
        for p in range(blocks[0].shape[1])
    ]
    return jnp.dot(own, jnp.concatenate(lanes, axis=1), preferred_element_type=jnp.float32)


def early_kernel(own_ref, near_ref, back_ref, ahead_ref, out_ref):
    product = ring_term(own_ref, [near_ref], 0)
    product = product + ring_term(own_ref, [back_ref], 3)
    out_ref[...] = product + ring_term(own_ref, [ahead_ref], 1)


def early_call(own, parts):
    batch_count, block_rows, width = own.shape
    pair_count, rows, cols = parts[0].shape[1:]
    return pl.pallas_call(
        early_kernel,
        grid=(pair_count // 2,),
        in_specs=[pl.BlockSpec(memory_space=pltpu.VMEM)]
        + [pl.BlockSpec((part.shape[0], 2, rows, cols), lambda i: (0, i, 0, 0)) for part in parts],
        out_specs=pl.BlockSpec((batch_count * block_rows, 2 * cols), lambda i: (0, i)),
        out_shape=jax.ShapeDtypeStruct((batch_count * block_rows, pair_count * cols), jnp.float32),
        compiler_params=params(),
    )(own, *parts)


def late_kernel(own_ref, left_ref, right_ref, early_ref, out_ref):
    batch_count, block_rows, width = own_ref.shape
    product = early_ref[...] + ring_term(own_ref, [left_ref, right_ref], 2)
    spread_product(product, out_ref, 0, batch_count, block_rows)


def late_call(own, parts, early):
    batch_count, block_rows, width = own.shape
    pair_count, rows, cols = parts[0].shape[1:]
    vmem = pl.BlockSpec(memory_space=pltpu.VMEM)
    return pl.pallas_call(
        late_kernel,
        in_specs=[vmem] * 4,
        out_specs=vmem,
        out_shape=jax.ShapeDtypeStruct((pair_count, block_rows, batch_count * cols), jnp.bfloat16),
        compiler_params=params(),
    )(own, *parts, early)


def ladder_term(inner_ref, low_ref, high_ref, out_ref):
    y_count, z_count, batch_count, rows, cols = low_ref.shape
    pair_count, block_rows, depth = inner_ref.shape
    inner = inner_ref[...].reshape(pair_count * block_rows, depth)
    lanes = [
        jnp.concatenate([ref[y, 0, q] for ref in (low_ref, high_ref) for y in range(y_count)], axis=0)
        for q in range(batch_count)
    ]
    factor = jnp.concatenate(lanes, axis=1)
    product = lax.dot_general(inner, factor, (((1,), (1,)), ((), ())), preferred_element_type=jnp.float32)
    half = product.shape[1] // 2
    for k in range(2):
        out_ref[k] = product[:, k * half : (k + 1) * half].reshape(pair_count, block_rows, half).astype(out_ref.dtype)


def send_kernel(side_ref, own_ref, ring_ref, *refs):
    amps_refs, (low_ref, high_ref, out_ref, inner_ref) = refs[:-4], refs[-4:]
    batch_count, block_rows, width = own_ref.shape
    ring = ring_ref.shape[0]

    @pl.when(pl.program_id(0) == 0)
    def _():
        inner_ref[:ring] = ring_ref[...]
        own = own_ref[...].reshape(batch_count * block_rows, width)
        lanes = [
            jnp.concatenate([ref[y, z, 0] for z in range(ref.shape[1]) for y in range(ref.shape[0])], axis=0)
            for ref in amps_refs
        ]
        product = jnp.dot(own, jnp.concatenate(lanes, axis=1), preferred_element_type=jnp.float32)
        spread_product(product, inner_ref, ring, batch_count, block_rows)

    pl.when(pl.program_id(0) > 0)(lambda: ladder_term(inner_ref, low_ref, high_ref, out_ref))


def send_call(side, own, ring_inner, units):
    ring, block_rows, depth = ring_inner.shape
    y_count, z_count, unit_count, rows, cols = units.shape
    batch_count = depth // cols
    flat = unit_count - batch_count
    pair_count = ring + flat
    quarter = (y_count // 4, 1, batch_count, rows, cols)

    def amps_spec(k):
        return pl.BlockSpec((y_count, z_count, 1, rows, cols), lambda i, side: (0, 0, batch_count + k, 0, 0))

    return pl.pallas_call(
        send_kernel,
        grid_spec=pltpu.PrefetchScalarGridSpec(
            num_scalar_prefetch=1,
            grid=(z_count + 1,),
            in_specs=[
                pl.BlockSpec(memory_space=pltpu.VMEM),
                pl.BlockSpec(memory_space=pltpu.VMEM),
            ]
            + [amps_spec(k) for k in range(flat)]
            + [
                pl.BlockSpec(quarter, lambda i, side: (side[0], jnp.maximum(i - 1, 0), 0, 0, 0)),
                pl.BlockSpec(quarter, lambda i, side: (side[0] + 2, jnp.maximum(i - 1, 0), 0, 0, 0)),
            ],
            out_specs=[
                pl.BlockSpec((2, pair_count, block_rows, 2 * rows), lambda i, side: (jnp.maximum(i - 1, 0), 0, 0, 0)),
                pl.BlockSpec((pair_count, block_rows, depth), lambda i, side: (0, 0, 0)),
            ],
        ),
        out_shape=[
            jax.ShapeDtypeStruct((8, pair_count, block_rows, 2 * rows), jnp.bfloat16),
            jax.ShapeDtypeStruct((pair_count, block_rows, depth), jnp.bfloat16),
        ],
        compiler_params=params(48),
    )(side, own, ring_inner, *[units] * (flat + 2))


def keep_kernel(side_ref, inner_ref, low_ref, high_ref, out_ref):
    ladder_term(inner_ref, low_ref, high_ref, out_ref)


def keep_call(side, inner, units):
    pair_count, block_rows, depth = inner.shape
    y_count, z_count, unit_count, rows, cols = units.shape
    quarter = (y_count // 4, 1, depth // cols, rows, cols)
    return pl.pallas_call(
        keep_kernel,
        grid_spec=pltpu.PrefetchScalarGridSpec(
            num_scalar_prefetch=1,
            grid=(z_count,),
            in_specs=[
                pl.BlockSpec(memory_space=pltpu.VMEM),
                pl.BlockSpec(quarter, lambda i, side: (side[0], i, 0, 0, 0)),
                pl.BlockSpec(quarter, lambda i, side: (side[0] + 2, i, 0, 0, 0)),
            ],
            out_specs=pl.BlockSpec((2, pair_count, block_rows, 2 * rows), lambda i, side: (i, 0, 0, 0)),
        ),
        out_shape=jax.ShapeDtypeStruct((8, pair_count, block_rows, 2 * rows), jnp.float32),
        compiler_params=params(48),
    )(side, inner, units, units)


def reduce_kernel(mask_ref, part_ref, kept_ref, same_ref, other_ref):
    c = place(COL)
    weight = mask_ref[c // 2, place(ROW)].astype(jnp.float32)
    side = lax.rem(c, 2)
    halves = []
    for p in range(2):
        total = part_ref[0, p].astype(jnp.float32)
        for k in range(1, part_ref.shape[0]):
            total = total + part_ref[k, p].astype(jnp.float32)
        total = total * weight
        kept_ref[p] = total
        halves.append(total.T)
    turned = jnp.concatenate(halves, axis=1).astype(jnp.bfloat16)
    low, high = turned[:64], turned[64:]
    same_ref[0] = jnp.where(side == 0, low, high)
    other_ref[0] = jnp.where(side == 0, high, low)


def reduce_call(mask, pieces):
    sources, pair_count, rows, cols = pieces.shape
    half_spec = pl.BlockSpec((1, rows, cols), lambda i: (i, 0, 0))
    return pl.pallas_call(
        reduce_kernel,
        grid=(pair_count // 2,),
        in_specs=[
            pl.BlockSpec(memory_space=pltpu.SMEM),
            pl.BlockSpec((sources, 2, rows, cols), lambda i: (0, i, 0, 0)),
        ],
        out_specs=[pl.BlockSpec((2, rows, cols), lambda i: (i, 0, 0)), half_spec, half_spec],
        out_shape=[
            jax.ShapeDtypeStruct((pair_count, rows, cols), jnp.float32),
            jax.ShapeDtypeStruct((pair_count // 2, rows, cols), jnp.bfloat16),
            jax.ShapeDtypeStruct((pair_count // 2, rows, cols), jnp.bfloat16),
        ],
        compiler_params=params(),
    )(mask, pieces)


def combine_kernel(partner_ref, kept_ref, same_ref, other_ref, out_ref):
    side = lax.rem(place(COL), 2)
    pair_count, rows, cols = kept_ref.shape
    half = cols // 2
    for p in range(pair_count):
        mate = partner_ref[p]
        odd = lax.rem(mate, 2) == 1
        same = same_ref[mate // 2].astype(jnp.float32)
        other = other_ref[mate // 2].astype(jnp.float32)
        same = jnp.where(odd, same[:, half:], same[:, :half])
        other = jnp.where(odd, other[:, half:], other[:, :half])
        first = jnp.where(side == 0, same, other)
        second = jnp.where(side == 0, other, same)
        total = kept_ref[p] + jnp.concatenate([first, second], axis=1)
        for k in range(16):
            out_ref[k, p * 4 : (p + 1) * 4, :] = total[k * 4 : (k + 1) * 4]


def combine_call(partner, kept, same, other):
    pair_count, rows, cols = kept.shape
    smem = pl.BlockSpec(memory_space=pltpu.SMEM)
    vmem = pl.BlockSpec(memory_space=pltpu.VMEM)
    return pl.pallas_call(
        combine_kernel,
        in_specs=[smem, vmem, vmem, vmem],
        out_specs=vmem,
        out_shape=jax.ShapeDtypeStruct((16, pair_count * rows // 16, cols), jnp.float32),
        compiler_params=params(),
    )(partner, kept, same, other)


def turn(count, step):
    return [(i, (i + step) % count) for i in range(count)]


def mirror_pairs(other):
    pairs = []
    for r in range(16):
        for c in range(32):
            side = 1 - c % 2 if other else c % 2
            pairs.append((r * 32 + c, (c // 2) * 32 + 2 * r + side))
    return pairs


def on_device(amplitudes, factors, amp_mask, out_mask, partner):
    pair_count, amp_rows, amp_cols = amplitudes.shape
    batch_count, block_rows, full_width = factors.shape
    ring = 6
    first, second = prepare_call(amp_mask, amplitudes, factors, ring, 8)
    near = lax.all_to_all(second, "y", split_axis=0, concat_axis=0)
    units = lax.all_gather(gate_call(lax.all_gather(first, "zh", axis=0), near), "y", axis=0)

    back = lax.ppermute(near, "zh", turn(4, 1))
    ahead = lax.ppermute(near, "zh", turn(4, -1))
    left = lax.ppermute(back[:4], "zh", turn(4, 1))
    right = lax.ppermute(ahead[4:], "zh", turn(4, -1))

    early = early_call(factors, (near, back, ahead))
    late = late_call(factors, (left, right), early)
    core = lax.axis_index("core").reshape(1)
    send, inner = send_call(1 - core, factors, late, units)
    swapped = lax.ppermute(send, "core", turn(2, 1))
    keep = keep_call(core, inner, units)
    partial = (keep + swapped.astype(jnp.float32)).astype(jnp.bfloat16)
    pieces = lax.all_to_all(partial, ("zl", "x"), split_axis=0, concat_axis=0)
    kept, same, other = reduce_call(out_mask, pieces)
    same = lax.ppermute(same, ALL, mirror_pairs(False))
    other = lax.ppermute(other, ALL, mirror_pairs(True))
    rows = lax.all_to_all(combine_call(partner, kept, same, other), ROW, split_axis=0, concat_axis=0)
    rows = rows.reshape(16, pair_count, 4, 128).transpose(1, 2, 0, 3)
    return rows.reshape(pair_count, 4, full_width)


def solution(mesh):
    fine = Mesh(mesh.devices.reshape(2, 4, 2, 4, 8), ALL)
    return jax.shard_map(
        on_device,
        mesh=fine,
        in_specs=(P(None, COL, ROW), P(None, COL, None), P(), P(), P()),
        out_specs=P(None, COL + ROW, None),
        check_vma=False,
    )
```

time: 236 us -> 189 us (0.80)
  waiting for transfers between devices: 92.4 us -> 31.7 us
  blocking collectives: 45.9 us -> 67.9 us
  local copies, waits for them, and re-layouts: 25.5 us -> 4.91 us
  starting transfers between devices: 41.8 us -> 52.4 us
  Pallas kernels: 13 us -> 17.8 us
  other arithmetic: 2.9 us -> 0.33 us
    ppermute x1, waiting for transfers between devices: 41.8 us -> 0.01 us  [on_device(): ahead = lax.ppermute(near, 'zh', turn(4, -1))]
    all_to_all x1, waiting for transfers between devices: 25.9 us -> 0.01 us  [on_device(): near = lax.all_to_all(second, 'y', split_axis=0, concat_axis=0)]
    ppermute x2 -> x3, starting transfers between devices: 7.44 us -> 27.6 us  [the longest x1 17.7 us: on_device(): left = lax.ppermute(back[:4], 'zh', turn(4, 1))]
    all_to_all x1 -> x2, blocking collectives: 24.9 us -> 44.9 us  [the longest x1 23.7 us: on_device(): lax.all_to_all(combine_call(partner, kept, same, other), ROW, split_axis=...]
    all_gather x2 -> x1, waiting for transfers between devices: 19.6 us -> 0.02 us  [on_device(): lax.all_gather(gate_call(lax.all_gather(first, 'zh', axis=0), near), 'y',...]
    reshape x3 -> x0, local copies, waits for them, and re-layouts: 18.4 us -> none  [the longest x2 11.7 us: on_device(): factors.reshape(batch_count, block_rows, 4, 8, 64).transpose(0, 1, 3, 2, 4)]
    ppermute x1, waiting for transfers between devices: 0.01 us -> 15.7 us  [on_device(): back = lax.ppermute(near, 'zh', turn(4, 1))]
    all_to_all x1, starting transfers between devices: 19 us -> 7.66 us  [on_device(): near = lax.all_to_all(second, 'y', split_axis=0, concat_axis=0)]
  transfers between devices with their start and end apart: 9 -> 9, of which waited for: 4 -> 5; matrix products, arithmetic and copies ran while one was open for 10% -> 1% of each run, Pallas kernels for 0% -> 4%
where the time goes in v3:
time: 189 us
  blocking collectives  67.9 us (36%)
  starting transfers between devices  52.4 us (28%)
  waiting for transfers between devices  31.7 us (17%)
  Pallas kernels  17.8 us (9%)
  between operations  13.6 us (7%)
  local copies, waits for them, and re-layouts  4.91 us (3%)
    all_to_all x1, blocking collectives, on_device(): lax.all_to_all(combine_call(partner, kept, same, other), ROW, split_axis=...  23.7 us
    all_gather x1, blocking collectives, on_device(): lax.all_gather(first, 'zh', axis=0)  23 us
    all_to_all x1, blocking collectives, on_device(): pieces = lax.all_to_all(partial, ('zl', 'x'), split_axis=0, concat_axis=0)  21.2 us
    ppermute x1, starting transfers between devices, on_device(): left = lax.ppermute(back[:4], 'zh', turn(4, 1))  17.7 us
    ppermute x1, waiting for transfers between devices, on_device(): back = lax.ppermute(near, 'zh', turn(4, 1))  15.7 us
    all_to_all x1, starting transfers between devices, on_device(): near = lax.all_to_all(second, 'y', split_axis=0, concat_axis=0)  7.66 us
    ppermute x1, starting transfers between devices, on_device(): ahead = lax.ppermute(near, 'zh', turn(4, -1))  6.77 us
    ppermute x1, starting transfers between devices, on_device(): back = lax.ppermute(near, 'zh', turn(4, 1))  6.48 us
  transfers between devices with their start and end apart: 9, of which 5 were waited for; matrix products, arithmetic and copies ran while one was open for 1% of the time, Pallas kernels for 4%

profile of v3, /device:TPU:1, one launch (start us, length us, event | category | flops | bytes accessed | tf_op | source)
XLA Modules:
  0.0 188.6 jit_solution(12337541029693243426)
XLA Ops:
  6.5 2.8 %shard_map.55 = (bf16[10,64,128]{2,1,0:T(8,128)(2,1)}, bf16[8,6,64,128]{3,2,1,0:T(8,128)(2,1)}) custom-call(s32[16,16]{1,0:T(8,128)} %mask_ref.2, bf16[8,64,128]{2,1,0:T(8,128)(2,1)} %amps_ref.1, bf16[8,64,2048]{2,1,0:T(8,128)(2,1)} %own_ref.5), custom_call_target="tpu_custom_call" | custom-call | tf_op jit(solution)/shard_map/pallas_call | solution.py:44
  9.3 7.7 %all-to-all-start = ((bf16[8,6,64,128]{3,2,1,0:T(8,128)(2,1)}), bf16[8,6,64,128]{3,2,1,0:T(8,128)(2,1)S(1)}, u32[]{:S(2)}, u32[]{:S(2)}) async-start(bf16[8,6,64,128]{3,2,1,0:T(8,128)(2,1)} %get-tuple-element.12), calls=%async_computation | async-start | bytes 1572864 | tf_op jit(solution)/shard_map/all_to_all | solution.py:318
  17.0 0.0 all-gather.4.cloned.1.call-start
  17.0 23.0 %all-gather = bf16[40,64,128]{2,1,0:T(8,128)(2,1)} all-gather(bf16[10,64,128]{2,1,0:T(8,128)(2,1)} %get-tuple-element.13), channel_id=2, replica_groups=mesh['zl'=2,'x'=4,'core'=2,'zh'=4,'y'=8] {'zh'}, dimensions={0}, use_global_device_ids=true | all-gather | bytes 819200 | tf_op jit(solution)/shard_map/all_gather | solution.py:319
  40.0 0.0 all-to-all-done.near_ref.other_ref
  40.0 0.0 copy-start
  40.0 0.0 all-gather.4.cloned.1.call-update
  40.0 6.5 %collective-permute-start = (bf16[8,6,64,128]{3,2,1,0:T(8,128)(2,1)S(1)}, bf16[8,6,64,128]{3,2,1,0:T(8,128)(2,1)S(1)}, u32[]{:S(2)}, u32[]{:S(2)}) collective-permute-start(bf16[8,6,64,128]{3,2,1,0:T(8,128)(2,1)S(1)} %all-to-all-done.near_ref.other_ref), channel_id=1, source_target_pairs={{0,8},{8,16},{16,24},{24,0},{1,9},{9,17},{17,25},{25,1},{2,10},{10... | collective-permute-start | bytes 2359304 | tf_op jit(solution)/shard_map/ppermute | solution.py:321
  46.5 6.8 %collective-permute-start.2 = (bf16[8,6,64,128]{3,2,1,0:T(8,128)(2,1)S(1)}, bf16[8,6,64,128]{3,2,1,0:T(8,128)(2,1)S(1)}, u32[]{:S(2)}, u32[]{:S(2)}) collective-permute-start(bf16[8,6,64,128]{3,2,1,0:T(8,128)(2,1)S(1)} %all-to-all-done.near_ref.other_ref), channel_id=1, source_target_pairs={{0,24},{8,0},{16,8},{24,16},{1,25},{9,1},{17,9},{25,17},{2,26},{10... | collective-permute-start | bytes 2359304 | tf_op jit(solution)/shard_map/ppermute | solution.py:322
  53.3 15.7 %collective-permute-done.back_ref = bf16[8,6,64,128]{3,2,1,0:T(8,128)(2,1)S(1)} collective-permute-done((bf16[8,6,64,128]{3,2,1,0:T(8,128)(2,1)S(1)}, bf16[8,6,64,128]{3,2,1,0:T(8,128)(2,1)S(1)}, u32[]{:S(2)}, u32[]{:S(2)}) %collective-permute-start) | collective-permute-done | bytes 786464 | tf_op jit(solution)/shard_map/ppermute | solution.py:321
  69.0 0.0 copy-start.1
  69.0 0.8 slice.8
  69.9 17.7 %collective-permute-start.1 = (bf16[4,6,64,128]{3,2,1,0:T(8,128)(2,1)}, bf16[4,6,64,128]{3,2,1,0:T(8,128)(2,1)S(1)}, u32[]{:S(2)}, u32[]{:S(2)}) collective-permute-start(bf16[4,6,64,128]{3,2,1,0:T(8,128)(2,1)} %slice.8), channel_id=1, source_target_pairs={{0,8},{8,16},{16,24},{24,0},{1,9},{9,17},{17,25},{25,1},{2,10},{10... | collective-permute-start | bytes 1179656 | tf_op jit(solution)/shard_map/ppermute | solution.py:323
  87.6 0.0 collective-permute-done.2.ahead_ref
  87.6 0.0 copy-done.1
  87.6 0.0 copy-start.3
  87.6 0.9 slice.9
  88.5 0.2 copy-done.3
  88.6 4.9 %collective-permute-start.3 = (bf16[4,6,64,128]{3,2,1,0:T(8,128)(2,1)}, bf16[4,6,64,128]{3,2,1,0:T(8,128)(2,1)}, u32[]{:S(2)}, u32[]{:S(2)}) collective-permute-start(bf16[4,6,64,128]{3,2,1,0:T(8,128)(2,1)} %slice.9), channel_id=1, source_target_pairs={{0,24},{8,0},{16,8},{24,16},{1,25},{9,1},{17,9},{25,17},{2,26},{10... | collective-permute-start | bytes 1179656 | tf_op jit(solution)/shard_map/ppermute | solution.py:324
  93.5 0.0 copy-done
  93.5 0.0 copy-start.2
  93.6 1.1 copy-done.2
  94.7 0.0 copy-start.4
  94.7 1.1 copy-done.4
  95.8 2.0 %shard_map.56.early_ref = f32[512,768]{1,0:T(8,128)S(1)} custom-call(bf16[8,64,2048]{2,1,0:T(8,128)(2,1)S(1)} %copy-done, bf16[8,6,64,128]{3,2,1,0:T(8,128)(2,1)S(1)} %all-to-all-done.near_ref.other_ref, bf16[8,6,64,128]{3,2,1,0:T(8,128)(2,1)S(1)} %copy-done.2, bf16[8,6,64,128]{3,2,1,0:T(8,128)(2,1)S(1)} %copy-done.4), custom_call_target="tpu_custom_call" | custom-call | tf_op jit(solution)/shard_map/pallas_call | solution.py:104
  97.9 6.5 %collective-permute-done.1.left_ref = bf16[4,6,64,128]{3,2,1,0:T(8,128)(2,1)S(1)} collective-permute-done((bf16[4,6,64,128]{3,2,1,0:T(8,128)(2,1)}, bf16[4,6,64,128]{3,2,1,0:T(8,128)(2,1)S(1)}, u32[]{:S(2)}, u32[]{:S(2)}) %collective-permute-start.1) | collective-permute-done | bytes 393248 | tf_op jit(solution)/shard_map/ppermute | solution.py:323
  104.4 3.9 %collective-permute-done.3.right_ref = bf16[4,6,64,128]{3,2,1,0:T(8,128)(2,1)} collective-permute-done((bf16[4,6,64,128]{3,2,1,0:T(8,128)(2,1)}, bf16[4,6,64,128]{3,2,1,0:T(8,128)(2,1)}, u32[]{:S(2)}, u32[]{:S(2)}) %collective-permute-start.3) | collective-permute-done | bytes 393248 | tf_op jit(solution)/shard_map/ppermute | solution.py:324
  108.2 1.6 shard_map.57.ring_ref
  109.8 0.0 all-gather.4.cloned.1.call-done
  109.8 5.3 %shard_map.59 = (bf16[8,8,64,128]{3,2,1,0:T(8,128)(2,1)S(1)}, bf16[8,64,1024]{2,1,0:T(8,128)(2,1)S(1)}) custom-call(s32[1]{0:T(128)S(6)} %sub.3.side_ref, bf16[8,64,2048]{2,1,0:T(8,128)(2,1)S(1)} %copy-done, bf16[6,64,1024]{2,1,0:T(8,128)(2,1)S(1)} %shard_map.57.ring_ref, bf16[8,4,10,64,128]{4,3,2,1,0:T(8,128)(2,1)} %bitcast.10, ...), custom_call_target="tpu_custom_call" | custom-call | tf_op jit(solution)/shard_map/pallas_call | solution.py:179
  115.2 5.0 %collective-permute-start.4 = (bf16[8,8,64,128]{3,2,1,0:T(8,128)(2,1)S(1)}, bf16[8,8,64,128]{3,2,1,0:T(8,128)(2,1)S(1)}, u32[]{:S(2)}, u32[]{:S(2)}) collective-permute-start(bf16[8,8,64,128]{3,2,1,0:T(8,128)(2,1)S(1)} %get-tuple-element.15), channel_id=1, source_target_pairs={{0,32},{32,0},{1,33},{33,1},{2,34},{34,2},{3,35},{35,3},{4,36},{36... | collective-permute-start | bytes 3145736 | tf_op jit(solution)/shard_map/ppermute | solution.py:330
  120.1 3.6 %shard_map.60 = f32[8,8,64,128]{3,2,1,0:T(8,128)S(1)} custom-call(s32[1]{0:T(128)} %bitcast.side_ref, bf16[8,64,1024]{2,1,0:T(8,128)(2,1)S(1)} %get-tuple-element.14.inner_ref, bf16[8,4,10,64,128]{4,3,2,1,0:T(8,128)(2,1)} %bitcast.14, bf16[8,4,10,64,128]{4,3,2,1,0:T(8,128)(2,1)} %bitcast.15), custom_call_target="tpu_custom_call" | custom-call | tf_op jit(solution)/shard_map/pallas_call | solution.py:214
  123.8 0.0 collective-permute-done.4
  123.8 0.3 add_convert_fusion
  124.1 0.0 copy-start.5
  124.1 0.0 copy-start.6
  124.1 21.2 %all_to_all.15.part_ref = bf16[8,8,64,128]{3,2,1,0:T(8,128)(2,1)S(1)} all-to-all(bf16[8,8,64,128]{3,2,1,0:T(8,128)(2,1)S(1)} %add_convert_fusion), channel_id=1, replica_groups=mesh['zl'=2,'x'=4,'core'=2,'zh'=4,'y'=8] {'zl','x'}, dimensions={0} | all-to-all | bytes 2097152 | tf_op jit(solution)/shard_map/all_to_all | solution.py:333
  145.3 0.0 copy-done.5
  145.3 1.6 shard_map.61
  147.0 1.9 %collective-permute-start.5 = (bf16[4,64,128]{2,1,0:T(8,128)(2,1)S(1)}, bf16[4,64,128]{2,1,0:T(8,128)(2,1)S(1)}, u32[]{:S(2)}, u32[]{:S(2)}) collective-permute-start(bf16[4,64,128]{2,1,0:T(8,128)(2,1)S(1)} %get-tuple-element.17), channel_id=1, source_target_pairs={{0,0},{1,1},{2,32},{3,33},{4,64},{5,65},{6,96},{7,97},{8,128},{9,1... | collective-permute-start | bytes 196616 | tf_op jit(solution)/shard_map/ppermute | solution.py:335
  148.9 1.9 %collective-permute-start.6 = (bf16[4,64,128]{2,1,0:T(8,128)(2,1)S(1)}, bf16[4,64,128]{2,1,0:T(8,128)(2,1)S(1)}, u32[]{:S(2)}, u32[]{:S(2)}) collective-permute-start(bf16[4,64,128]{2,1,0:T(8,128)(2,1)S(1)} %get-tuple-element.18), channel_id=1, source_target_pairs={{0,1},{1,0},{2,33},{3,32},{4,65},{5,64},{6,97},{7,96},{8,129},{9,1... | collective-permute-start | bytes 196616 | tf_op jit(solution)/shard_map/ppermute | solution.py:336
  150.8 2.6 %collective-permute-done.5.same_ref = bf16[4,64,128]{2,1,0:T(8,128)(2,1)S(1)} collective-permute-done((bf16[4,64,128]{2,1,0:T(8,128)(2,1)S(1)}, bf16[4,64,128]{2,1,0:T(8,128)(2,1)S(1)}, u32[]{:S(2)}, u32[]{:S(2)}) %collective-permute-start.5) | collective-permute-done | bytes 65568 | tf_op jit(solution)/shard_map/ppermute | solution.py:335
  153.5 3.0 %collective-permute-done.6.other_ref = bf16[4,64,128]{2,1,0:T(8,128)(2,1)S(1)} collective-permute-done((bf16[4,64,128]{2,1,0:T(8,128)(2,1)S(1)}, bf16[4,64,128]{2,1,0:T(8,128)(2,1)S(1)}, u32[]{:S(2)}, u32[]{:S(2)}) %collective-permute-start.6) | collective-permute-done | bytes 65568 | tf_op jit(solution)/shard_map/ppermute | solution.py:336
  156.5 0.0 copy-done.6
  156.5 0.8 shard_map.62
  157.3 23.7 %all_to_all.16 = f32[16,32,128]{2,1,0:T(8,128)S(1)} all-to-all(f32[16,32,128]{2,1,0:T(8,128)S(1)} %shard_map.62), channel_id=1, replica_groups=mesh['zl'=2,'x'=4,'core'=2,'zh'=4,'y'=8] {'zl','x','core'}, dimensions={0} | all-to-all | bytes 524288 | tf_op jit(solution)/shard_map/all_to_all | solution.py:337
  181.0 0.8 copy.11
  (1 shorter events, 0.0 us)
Async XLA Ops:
  9.3 30.7 %all-to-all-start = ((bf16[8,6,64,128]{3,2,1,0:T(8,128)(2,1)}), bf16[8,6,64,128]{3,2,1,0:T(8,128)(2,1)S(1)}, u32[]{:S(2)}, u32[]{:S(2)}) async-start(bf16[8,6,64,128]{3,2,1,0:T(8,128)(2,1)} %get-tuple-element.12), calls=%async_computation | async-start | bytes 1572864 | tf_op jit(solution)/shard_map/all_to_all | solution.py:318
  17.0 92.9 %all-gather.4.cloned.1.call-start = ((), (), s32[]{:S(2)}) async-start(), calls=%async_computation.3 | async-start | bytes 5898240 | tf_op jit(solution)/shard_map/all_gather | solution.py:319
  40.0 53.5 %copy-start = (bf16[8,64,2048]{2,1,0:T(8,128)(2,1)S(1)}, bf16[8,64,2048]{2,1,0:T(8,128)(2,1)}, u32[]{:S(2)}) copy-start(bf16[8,64,2048]{2,1,0:T(8,128)(2,1)} %own_ref.5) | copy-start | bytes 6291460
  40.0 29.0 %collective-permute-start = (bf16[8,6,64,128]{3,2,1,0:T(8,128)(2,1)S(1)}, bf16[8,6,64,128]{3,2,1,0:T(8,128)(2,1)S(1)}, u32[]{:S(2)}, u32[]{:S(2)}) collective-permute-start(bf16[8,6,64,128]{3,2,1,0:T(8,128)(2,1)S(1)} %all-to-all-done.near_ref.other_ref), channel_id=1, source_target_pairs={{0,8},{8,16},{16,24},{24,0},{1,9},{9,17},{17,25},{25,1},{2,10},{10... | collective-permute-start | bytes 2359304 | tf_op jit(solution)/shard_map/ppermute | solution.py:321
  46.5 41.0 %collective-permute-start.2 = (bf16[8,6,64,128]{3,2,1,0:T(8,128)(2,1)S(1)}, bf16[8,6,64,128]{3,2,1,0:T(8,128)(2,1)S(1)}, u32[]{:S(2)}, u32[]{:S(2)}) collective-permute-start(bf16[8,6,64,128]{3,2,1,0:T(8,128)(2,1)S(1)} %all-to-all-done.near_ref.other_ref), channel_id=1, source_target_pairs={{0,24},{8,0},{16,8},{24,16},{1,25},{9,1},{17,9},{25,17},{2,26},{10... | collective-permute-start | bytes 2359304 | tf_op jit(solution)/shard_map/ppermute | solution.py:322
  69.0 18.5 %copy-start.1 = (bf16[8,6,64,128]{3,2,1,0:T(8,128)(2,1)}, bf16[8,6,64,128]{3,2,1,0:T(8,128)(2,1)S(1)}, u32[]{:S(2)}) copy-start(bf16[8,6,64,128]{3,2,1,0:T(8,128)(2,1)S(1)} %collective-permute-done.back_ref) | copy-start | bytes 2359300
  69.9 34.5 %collective-permute-start.1 = (bf16[4,6,64,128]{3,2,1,0:T(8,128)(2,1)}, bf16[4,6,64,128]{3,2,1,0:T(8,128)(2,1)S(1)}, u32[]{:S(2)}, u32[]{:S(2)}) collective-permute-start(bf16[4,6,64,128]{3,2,1,0:T(8,128)(2,1)} %slice.8), channel_id=1, source_target_pairs={{0,8},{8,16},{16,24},{24,0},{1,9},{9,17},{17,25},{25,1},{2,10},{10... | collective-permute-start | bytes 1179656 | tf_op jit(solution)/shard_map/ppermute | solution.py:323
  87.6 1.0 copy-start.3
  88.6 19.6 %collective-permute-start.3 = (bf16[4,6,64,128]{3,2,1,0:T(8,128)(2,1)}, bf16[4,6,64,128]{3,2,1,0:T(8,128)(2,1)}, u32[]{:S(2)}, u32[]{:S(2)}) collective-permute-start(bf16[4,6,64,128]{3,2,1,0:T(8,128)(2,1)} %slice.9), channel_id=1, source_target_pairs={{0,24},{8,0},{16,8},{24,16},{1,25},{9,1},{17,9},{25,17},{2,26},{10... | collective-permute-start | bytes 1179656 | tf_op jit(solution)/shard_map/ppermute | solution.py:324
  93.5 1.1 copy-start.2
  94.7 1.1 copy-start.4
  115.2 8.6 %collective-permute-start.4 = (bf16[8,8,64,128]{3,2,1,0:T(8,128)(2,1)S(1)}, bf16[8,8,64,128]{3,2,1,0:T(8,128)(2,1)S(1)}, u32[]{:S(2)}, u32[]{:S(2)}) collective-permute-start(bf16[8,8,64,128]{3,2,1,0:T(8,128)(2,1)S(1)} %get-tuple-element.15), channel_id=1, source_target_pairs={{0,32},{32,0},{1,33},{33,1},{2,34},{34,2},{3,35},{35,3},{4,36},{36... | collective-permute-start | bytes 3145736 | tf_op jit(solution)/shard_map/ppermute | solution.py:330
  124.1 21.2 %copy-start.5 = (s32[16,16]{1,0:T(8,128)S(1)}, s32[16,16]{1,0:T(8,128)}, u32[]{:S(2)}) copy-start(s32[16,16]{1,0:T(8,128)} %mask_ref.3) | copy-start | bytes 3076
  124.1 32.3 %copy-start.6 = (s32[8]{0:T(128)S(1)}, s32[8]{0:T(128)}, u32[]{:S(2)}) copy-start(s32[8]{0:T(128)} %partner_ref.1) | copy-start | bytes 100
  147.0 6.5 %collective-permute-start.5 = (bf16[4,64,128]{2,1,0:T(8,128)(2,1)S(1)}, bf16[4,64,128]{2,1,0:T(8,128)(2,1)S(1)}, u32[]{:S(2)}, u32[]{:S(2)}) collective-permute-start(bf16[4,64,128]{2,1,0:T(8,128)(2,1)S(1)} %get-tuple-element.17), channel_id=1, source_target_pairs={{0,0},{1,1},{2,32},{3,33},{4,64},{5,65},{6,96},{7,97},{8,128},{9,1... | collective-permute-start | bytes 196616 | tf_op jit(solution)/shard_map/ppermute | solution.py:335
  148.9 7.6 %collective-permute-start.6 = (bf16[4,64,128]{2,1,0:T(8,128)(2,1)S(1)}, bf16[4,64,128]{2,1,0:T(8,128)(2,1)S(1)}, u32[]{:S(2)}, u32[]{:S(2)}) collective-permute-start(bf16[4,64,128]{2,1,0:T(8,128)(2,1)S(1)} %get-tuple-element.18), channel_id=1, source_target_pairs={{0,1},{1,0},{2,33},{3,32},{4,65},{5,64},{6,97},{7,96},{8,129},{9,1... | collective-permute-start | bytes 196616 | tf_op jit(solution)/shard_map/ppermute | solution.py:336
Sparse Core Ops, SparseCore 0:
  40.2 68.6 all-gather.3

commit v4 on v3

--- a/solution.py
+++ b/solution.py
@@ -71,13 +71,13 @@
 
 
 def spread_product(product, out_ref, first, batch_count, block_rows):
-    product = product.astype(jnp.bfloat16)
-    cols = out_ref.shape[2] // batch_count
-    for p in range(product.shape[1] // cols):
+    cols = out_ref.shape[0] // batch_count
+    for pair in range(product.shape[1] // cols // 2):
         for q in range(batch_count):
-            out_ref[first + p, :, q * cols : (q + 1) * cols] = product[
-                q * block_rows : (q + 1) * block_rows, p * cols : (p + 1) * cols
-            ]
+            rows = product[q * block_rows : (q + 1) * block_rows, 2 * pair * cols : 2 * (pair + 1) * cols]
+            block = jnp.concatenate([rows[:, :cols], rows[:, cols:]], axis=0)
+            at = first + 2 * pair * block_rows
+            out_ref[q * cols : (q + 1) * cols, at : at + 2 * block_rows] = block.T.astype(jnp.bfloat16)
 
 
 def ring_term(own_ref, blocks, move):
@@ -126,34 +126,33 @@
         late_kernel,
         in_specs=[vmem] * 4,
         out_specs=vmem,
-        out_shape=jax.ShapeDtypeStruct((pair_count, block_rows, batch_count * cols), jnp.bfloat16),
+        out_shape=jax.ShapeDtypeStruct((batch_count * cols, pair_count * block_rows), jnp.bfloat16),
         compiler_params=params(),
     )(own, *parts, early)
 
 
 def ladder_term(inner_ref, low_ref, high_ref, out_ref):
     y_count, z_count, batch_count, rows, cols = low_ref.shape
-    pair_count, block_rows, depth = inner_ref.shape
-    inner = inner_ref[...].reshape(pair_count * block_rows, depth)
+    blocks = [(ref, z) for z in range(z_count) for ref in (low_ref, high_ref)]
     lanes = [
-        jnp.concatenate([ref[y, 0, q] for ref in (low_ref, high_ref) for y in range(y_count)], axis=0)
+        jnp.concatenate([ref[y, z, q] for ref, z in blocks for y in range(y_count)], axis=0)
         for q in range(batch_count)
     ]
     factor = jnp.concatenate(lanes, axis=1)
-    product = lax.dot_general(inner, factor, (((1,), (1,)), ((), ())), preferred_element_type=jnp.float32)
-    half = product.shape[1] // 2
-    for k in range(2):
-        out_ref[k] = product[:, k * half : (k + 1) * half].reshape(pair_count, block_rows, half).astype(out_ref.dtype)
+    product = jnp.dot(factor, inner_ref[...], preferred_element_type=jnp.float32).astype(out_ref.dtype)
+    height = y_count * rows
+    for k in range(len(blocks)):
+        out_ref[k] = product[k * height : (k + 1) * height]
 
 
 def send_kernel(side_ref, own_ref, ring_ref, *refs):
     amps_refs, (low_ref, high_ref, out_ref, inner_ref) = refs[:-4], refs[-4:]
     batch_count, block_rows, width = own_ref.shape
-    ring = ring_ref.shape[0]
+    ring = ring_ref.shape[1]
 
     @pl.when(pl.program_id(0) == 0)
     def _():
-        inner_ref[:ring] = ring_ref[...]
+        inner_ref[:, :ring] = ring_ref[...]
         own = own_ref[...].reshape(batch_count * block_rows, width)
         lanes = [
             jnp.concatenate([ref[y, z, 0] for z in range(ref.shape[1]) for y in range(ref.shape[0])], axis=0)
@@ -165,13 +164,17 @@
     pl.when(pl.program_id(0) > 0)(lambda: ladder_term(inner_ref, low_ref, high_ref, out_ref))
 
 
+ZSTEP = 2
+
+
 def send_call(side, own, ring_inner, units):
-    ring, block_rows, depth = ring_inner.shape
+    depth, ring_width = ring_inner.shape
+    batch_count, block_rows, width = own.shape
     y_count, z_count, unit_count, rows, cols = units.shape
-    batch_count = depth // cols
     flat = unit_count - batch_count
-    pair_count = ring + flat
-    quarter = (y_count // 4, 1, batch_count, rows, cols)
+    inner_width = ring_width + flat * block_rows
+    quarter = (y_count // 4, ZSTEP, batch_count, rows, cols)
+    blocks = 2 * ZSTEP
 
     def amps_spec(k):
         return pl.BlockSpec((y_count, z_count, 1, rows, cols), lambda i, side: (0, 0, batch_count + k, 0, 0))
@@ -180,24 +183,21 @@
         send_kernel,
         grid_spec=pltpu.PrefetchScalarGridSpec(
             num_scalar_prefetch=1,
-            grid=(z_count + 1,),
-            in_specs=[
-                pl.BlockSpec(memory_space=pltpu.VMEM),
-                pl.BlockSpec(memory_space=pltpu.VMEM),
-            ]
+            grid=(z_count // ZSTEP + 1,),
+            in_specs=[pl.BlockSpec(memory_space=pltpu.VMEM)] * 2
             + [amps_spec(k) for k in range(flat)]
             + [
                 pl.BlockSpec(quarter, lambda i, side: (side[0], jnp.maximum(i - 1, 0), 0, 0, 0)),
                 pl.BlockSpec(quarter, lambda i, side: (side[0] + 2, jnp.maximum(i - 1, 0), 0, 0, 0)),
             ],
             out_specs=[
-                pl.BlockSpec((2, pair_count, block_rows, 2 * rows), lambda i, side: (jnp.maximum(i - 1, 0), 0, 0, 0)),
-                pl.BlockSpec((pair_count, block_rows, depth), lambda i, side: (0, 0, 0)),
+                pl.BlockSpec((blocks, 2 * rows, inner_width), lambda i, side: (jnp.maximum(i - 1, 0), 0, 0)),
+                pl.BlockSpec((depth, inner_width), lambda i, side: (0, 0)),
             ],
         ),
         out_shape=[
-            jax.ShapeDtypeStruct((8, pair_count, block_rows, 2 * rows), jnp.bfloat16),
-            jax.ShapeDtypeStruct((pair_count, block_rows, depth), jnp.bfloat16),
+            jax.ShapeDtypeStruct((8, 2 * rows, inner_width), jnp.bfloat16),
+            jax.ShapeDtypeStruct((depth, inner_width), jnp.bfloat16),
         ],
         compiler_params=params(48),
     )(side, own, ring_inner, *[units] * (flat + 2))
@@ -208,22 +208,22 @@
 
 
 def keep_call(side, inner, units):
-    pair_count, block_rows, depth = inner.shape
+    depth, inner_width = inner.shape
     y_count, z_count, unit_count, rows, cols = units.shape
-    quarter = (y_count // 4, 1, depth // cols, rows, cols)
+    quarter = (y_count // 4, ZSTEP, depth // cols, rows, cols)
     return pl.pallas_call(
         keep_kernel,
         grid_spec=pltpu.PrefetchScalarGridSpec(
             num_scalar_prefetch=1,
-            grid=(z_count,),
+            grid=(z_count // ZSTEP,),
             in_specs=[
                 pl.BlockSpec(memory_space=pltpu.VMEM),
                 pl.BlockSpec(quarter, lambda i, side: (side[0], i, 0, 0, 0)),
                 pl.BlockSpec(quarter, lambda i, side: (side[0] + 2, i, 0, 0, 0)),
             ],
-            out_specs=pl.BlockSpec((2, pair_count, block_rows, 2 * rows), lambda i, side: (i, 0, 0, 0)),
+            out_specs=pl.BlockSpec((2 * ZSTEP, 2 * rows, inner_width), lambda i, side: (i, 0, 0)),
         ),
-        out_shape=jax.ShapeDtypeStruct((8, pair_count, block_rows, 2 * rows), jnp.float32),
+        out_shape=jax.ShapeDtypeStruct((8, 2 * rows, inner_width), jnp.float32),
         compiler_params=params(48),
     )(side, inner, units, units)
 
@@ -232,29 +232,29 @@
     c = place(COL)
     weight = mask_ref[c // 2, place(ROW)].astype(jnp.float32)
     side = lax.rem(c, 2)
-    halves = []
-    for p in range(2):
-        total = part_ref[0, p].astype(jnp.float32)
-        for k in range(1, part_ref.shape[0]):
-            total = total + part_ref[k, p].astype(jnp.float32)
-        total = total * weight
-        kept_ref[p] = total
-        halves.append(total.T)
-    turned = jnp.concatenate(halves, axis=1).astype(jnp.bfloat16)
-    low, high = turned[:64], turned[64:]
+    half = kept_ref.shape[1]
+    total = part_ref[0].astype(jnp.float32)
+    for k in range(1, part_ref.shape[0]):
+        total = total + part_ref[k].astype(jnp.float32)
+    total = total * weight
+    straight = total.T
+    kept_ref[0], kept_ref[1] = straight[:half], straight[half:]
+    turned = total.astype(jnp.bfloat16)
+    low, high = turned[:half], turned[half:]
     same_ref[0] = jnp.where(side == 0, low, high)
     other_ref[0] = jnp.where(side == 0, high, low)
 
 
-def reduce_call(mask, pieces):
-    sources, pair_count, rows, cols = pieces.shape
+def reduce_call(mask, pieces, rows):
+    sources, cols, inner_width = pieces.shape
+    pair_count = inner_width // rows
     half_spec = pl.BlockSpec((1, rows, cols), lambda i: (i, 0, 0))
     return pl.pallas_call(
         reduce_kernel,
         grid=(pair_count // 2,),
         in_specs=[
             pl.BlockSpec(memory_space=pltpu.SMEM),
-            pl.BlockSpec((sources, 2, rows, cols), lambda i: (0, i, 0, 0)),
+            pl.BlockSpec((sources, cols, 2 * rows), lambda i: (0, 0, i)),
         ],
         out_specs=[pl.BlockSpec((2, rows, cols), lambda i: (i, 0, 0)), half_spec, half_spec],
         out_shape=[
@@ -331,7 +331,7 @@
     keep = keep_call(core, inner, units)
     partial = (keep + swapped.astype(jnp.float32)).astype(jnp.bfloat16)
     pieces = lax.all_to_all(partial, ("zl", "x"), split_axis=0, concat_axis=0)
-    kept, same, other = reduce_call(out_mask, pieces)
+    kept, same, other = reduce_call(out_mask, pieces, block_rows)
     same = lax.ppermute(same, ALL, mirror_pairs(False))
     other = lax.ppermute(other, ALL, mirror_pairs(True))
     rows = lax.all_to_all(combine_call(partner, kept, same, other), ROW, split_axis=0, concat_axis=0)

time: 189 us -> 187 us (0.989)
  Pallas kernels: 17.8 us -> 15.8 us
  transfers between devices with their start and end apart: 9 -> 9, of which waited for: 5 -> 5; matrix products, arithmetic and copies ran while one was open for 1% -> 1% of each run, Pallas kernels for 4% -> 3%
where the time goes in v4:
time: 187 us
  blocking collectives  68 us (36%)
  starting transfers between devices  52.4 us (28%)
  waiting for transfers between devices  31.6 us (17%)
  Pallas kernels  15.8 us (8%)
  between operations  13.6 us (7%)
  local copies, waits for them, and re-layouts  4.91 us (3%)
    all_to_all x1, blocking collectives, on_device(): lax.all_to_all(combine_call(partner, kept, same, other), ROW, split_axis=...  23.8 us
    all_gather x1, blocking collectives, on_device(): lax.all_gather(first, 'zh', axis=0)  23 us
    all_to_all x1, blocking collectives, on_device(): pieces = lax.all_to_all(partial, ('zl', 'x'), split_axis=0, concat_axis=0)  21.2 us
    ppermute x1, starting transfers between devices, on_device(): left = lax.ppermute(back[:4], 'zh', turn(4, 1))  17.7 us
    ppermute x1, waiting for transfers between devices, on_device(): back = lax.ppermute(near, 'zh', turn(4, 1))  15.7 us
    all_to_all x1, starting transfers between devices, on_device(): near = lax.all_to_all(second, 'y', split_axis=0, concat_axis=0)  7.66 us
    ppermute x1, starting transfers between devices, on_device(): ahead = lax.ppermute(near, 'zh', turn(4, -1))  6.77 us
    ppermute x1, starting transfers between devices, on_device(): back = lax.ppermute(near, 'zh', turn(4, 1))  6.48 us
  transfers between devices with their start and end apart: 9, of which 5 were waited for; matrix products, arithmetic and copies ran while one was open for 1% of the time, Pallas kernels for 3%

profile of v4, /device:TPU:1, one launch (start us, length us, event | category | flops | bytes accessed | tf_op | source)
XLA Modules:
  0.0 186.6 jit_solution(1999625359071793795)
XLA Ops:
  6.5 2.8 %shard_map.55 = (bf16[10,64,128]{2,1,0:T(8,128)(2,1)}, bf16[8,6,64,128]{3,2,1,0:T(8,128)(2,1)}) custom-call(s32[16,16]{1,0:T(8,128)} %mask_ref.2, bf16[8,64,128]{2,1,0:T(8,128)(2,1)} %amps_ref.1, bf16[8,64,2048]{2,1,0:T(8,128)(2,1)} %own_ref.5), custom_call_target="tpu_custom_call" | custom-call | tf_op jit(solution)/shard_map/pallas_call | solution.py:44
  9.3 7.7 %all-to-all-start = ((bf16[8,6,64,128]{3,2,1,0:T(8,128)(2,1)}), bf16[8,6,64,128]{3,2,1,0:T(8,128)(2,1)S(1)}, u32[]{:S(2)}, u32[]{:S(2)}) async-start(bf16[8,6,64,128]{3,2,1,0:T(8,128)(2,1)} %get-tuple-element.12), calls=%async_computation | async-start | bytes 1572864 | tf_op jit(solution)/shard_map/all_to_all | solution.py:318
  17.0 0.0 all-gather.4.cloned.1.call-start
  17.0 23.0 %all-gather = bf16[40,64,128]{2,1,0:T(8,128)(2,1)} all-gather(bf16[10,64,128]{2,1,0:T(8,128)(2,1)} %get-tuple-element.13), channel_id=2, replica_groups=mesh['zl'=2,'x'=4,'core'=2,'zh'=4,'y'=8] {'zh'}, dimensions={0}, use_global_device_ids=true | all-gather | bytes 819200 | tf_op jit(solution)/shard_map/all_gather | solution.py:319
  40.0 0.0 all-to-all-done.near_ref.other_ref
  40.0 0.0 copy-start
  40.0 0.0 all-gather.4.cloned.1.call-update
  40.0 6.5 %collective-permute-start = (bf16[8,6,64,128]{3,2,1,0:T(8,128)(2,1)S(1)}, bf16[8,6,64,128]{3,2,1,0:T(8,128)(2,1)S(1)}, u32[]{:S(2)}, u32[]{:S(2)}) collective-permute-start(bf16[8,6,64,128]{3,2,1,0:T(8,128)(2,1)S(1)} %all-to-all-done.near_ref.other_ref), channel_id=1, source_target_pairs={{0,8},{8,16},{16,24},{24,0},{1,9},{9,17},{17,25},{25,1},{2,10},{10... | collective-permute-start | bytes 2359304 | tf_op jit(solution)/shard_map/ppermute | solution.py:321
  46.5 6.8 %collective-permute-start.2 = (bf16[8,6,64,128]{3,2,1,0:T(8,128)(2,1)S(1)}, bf16[8,6,64,128]{3,2,1,0:T(8,128)(2,1)S(1)}, u32[]{:S(2)}, u32[]{:S(2)}) collective-permute-start(bf16[8,6,64,128]{3,2,1,0:T(8,128)(2,1)S(1)} %all-to-all-done.near_ref.other_ref), channel_id=1, source_target_pairs={{0,24},{8,0},{16,8},{24,16},{1,25},{9,1},{17,9},{25,17},{2,26},{10... | collective-permute-start | bytes 2359304 | tf_op jit(solution)/shard_map/ppermute | solution.py:322
  53.3 15.7 %collective-permute-done.back_ref = bf16[8,6,64,128]{3,2,1,0:T(8,128)(2,1)S(1)} collective-permute-done((bf16[8,6,64,128]{3,2,1,0:T(8,128)(2,1)S(1)}, bf16[8,6,64,128]{3,2,1,0:T(8,128)(2,1)S(1)}, u32[]{:S(2)}, u32[]{:S(2)}) %collective-permute-start) | collective-permute-done | bytes 786464 | tf_op jit(solution)/shard_map/ppermute | solution.py:321
  69.0 0.0 copy-start.1
  69.0 0.8 slice.8
  69.9 17.7 %collective-permute-start.1 = (bf16[4,6,64,128]{3,2,1,0:T(8,128)(2,1)}, bf16[4,6,64,128]{3,2,1,0:T(8,128)(2,1)S(1)}, u32[]{:S(2)}, u32[]{:S(2)}) collective-permute-start(bf16[4,6,64,128]{3,2,1,0:T(8,128)(2,1)} %slice.8), channel_id=1, source_target_pairs={{0,8},{8,16},{16,24},{24,0},{1,9},{9,17},{17,25},{25,1},{2,10},{10... | collective-permute-start | bytes 1179656 | tf_op jit(solution)/shard_map/ppermute | solution.py:323
  87.6 0.0 collective-permute-done.2.ahead_ref
  87.6 0.0 copy-done.1
  87.6 0.0 copy-start.3
  87.6 0.9 slice.9
  88.5 0.2 copy-done.3
  88.6 4.9 %collective-permute-start.3 = (bf16[4,6,64,128]{3,2,1,0:T(8,128)(2,1)}, bf16[4,6,64,128]{3,2,1,0:T(8,128)(2,1)}, u32[]{:S(2)}, u32[]{:S(2)}) collective-permute-start(bf16[4,6,64,128]{3,2,1,0:T(8,128)(2,1)} %slice.9), channel_id=1, source_target_pairs={{0,24},{8,0},{16,8},{24,16},{1,25},{9,1},{17,9},{25,17},{2,26},{10... | collective-permute-start | bytes 1179656 | tf_op jit(solution)/shard_map/ppermute | solution.py:324
  93.5 0.0 copy-done
  93.5 0.0 copy-start.2
  93.6 1.1 copy-done.2
  94.7 0.0 copy-start.4
  94.7 1.1 copy-done.4
  95.8 2.0 %shard_map.56.early_ref = f32[512,768]{1,0:T(8,128)S(1)} custom-call(bf16[8,64,2048]{2,1,0:T(8,128)(2,1)S(1)} %copy-done, bf16[8,6,64,128]{3,2,1,0:T(8,128)(2,1)S(1)} %all-to-all-done.near_ref.other_ref, bf16[8,6,64,128]{3,2,1,0:T(8,128)(2,1)S(1)} %copy-done.2, bf16[8,6,64,128]{3,2,1,0:T(8,128)(2,1)S(1)} %copy-done.4), custom_call_target="tpu_custom_call" | custom-call | tf_op jit(solution)/shard_map/pallas_call | solution.py:104
  97.9 6.5 %collective-permute-done.1.left_ref = bf16[4,6,64,128]{3,2,1,0:T(8,128)(2,1)S(1)} collective-permute-done((bf16[4,6,64,128]{3,2,1,0:T(8,128)(2,1)}, bf16[4,6,64,128]{3,2,1,0:T(8,128)(2,1)S(1)}, u32[]{:S(2)}, u32[]{:S(2)}) %collective-permute-start.1) | collective-permute-done | bytes 393248 | tf_op jit(solution)/shard_map/ppermute | solution.py:323
  104.4 3.9 %collective-permute-done.3.right_ref = bf16[4,6,64,128]{3,2,1,0:T(8,128)(2,1)} collective-permute-done((bf16[4,6,64,128]{3,2,1,0:T(8,128)(2,1)}, bf16[4,6,64,128]{3,2,1,0:T(8,128)(2,1)}, u32[]{:S(2)}, u32[]{:S(2)}) %collective-permute-start.3) | collective-permute-done | bytes 393248 | tf_op jit(solution)/shard_map/ppermute | solution.py:324
  108.2 1.7 shard_map.57.ring_ref
  109.9 0.0 all-gather.4.cloned.1.call-done
  109.9 4.4 %shard_map.59 = (bf16[8,128,512]{2,1,0:T(8,128)(2,1)S(1)}, bf16[1024,512]{1,0:T(8,128)(2,1)S(1)}) custom-call(s32[1]{0:T(128)S(6)} %sub.3.side_ref, bf16[8,64,2048]{2,1,0:T(8,128)(2,1)S(1)} %copy-done, bf16[1024,384]{1,0:T(8,128)(2,1)S(1)} %shard_map.57.ring_ref, bf16[8,4,10,64,128]{4,3,2,1,0:T(8,128)(2,1)} %bitcast.10, ...), custom_call_target="tpu_custom_call" | custom-call | tf_op jit(solution)/shard_map/pallas_call | solution.py:182
  114.4 5.0 %collective-permute-start.4 = (bf16[8,128,512]{2,1,0:T(8,128)(2,1)S(1)}, bf16[8,128,512]{2,1,0:T(8,128)(2,1)S(1)}, u32[]{:S(2)}, u32[]{:S(2)}) collective-permute-start(bf16[8,128,512]{2,1,0:T(8,128)(2,1)S(1)} %get-tuple-element.15), channel_id=1, source_target_pairs={{0,32},{32,0},{1,33},{33,1},{2,34},{34,2},{3,35},{35,3},{4,36},{36... | collective-permute-start | bytes 3145736 | tf_op jit(solution)/shard_map/ppermute | solution.py:330
  119.3 2.7 %shard_map.60 = f32[8,128,512]{2,1,0:T(8,128)S(1)} custom-call(s32[1]{0:T(128)} %bitcast.side_ref, bf16[1024,512]{1,0:T(8,128)(2,1)S(1)} %get-tuple-element.14.inner_ref, bf16[8,4,10,64,128]{4,3,2,1,0:T(8,128)(2,1)} %bitcast.14, bf16[8,4,10,64,128]{4,3,2,1,0:T(8,128)(2,1)} %bitcast.15), custom_call_target="tpu_custom_call" | custom-call | tf_op jit(solution)/shard_map/pallas_call | solution.py:214
  122.0 0.0 collective-permute-done.4
  122.0 0.3 add_convert_fusion
  122.4 0.0 copy-start.5
  122.4 0.0 copy-start.6
  122.4 21.2 %all_to_all.15.part_ref = bf16[8,128,512]{2,1,0:T(8,128)(2,1)S(1)} all-to-all(bf16[8,128,512]{2,1,0:T(8,128)(2,1)S(1)} %add_convert_fusion), channel_id=1, replica_groups=mesh['zl'=2,'x'=4,'core'=2,'zh'=4,'y'=8] {'zl','x'}, dimensions={0} | all-to-all | bytes 2097152 | tf_op jit(solution)/shard_map/all_to_all | solution.py:333
  143.6 0.0 copy-done.5
  143.6 1.4 shard_map.61
  145.0 1.9 %collective-permute-start.5 = (bf16[4,64,128]{2,1,0:T(8,128)(2,1)S(1)}, bf16[4,64,128]{2,1,0:T(8,128)(2,1)S(1)}, u32[]{:S(2)}, u32[]{:S(2)}) collective-permute-start(bf16[4,64,128]{2,1,0:T(8,128)(2,1)S(1)} %get-tuple-element.17), channel_id=1, source_target_pairs={{0,0},{1,1},{2,32},{3,33},{4,64},{5,65},{6,96},{7,97},{8,128},{9,1... | collective-permute-start | bytes 196616 | tf_op jit(solution)/shard_map/ppermute | solution.py:335
  146.9 1.9 %collective-permute-start.6 = (bf16[4,64,128]{2,1,0:T(8,128)(2,1)S(1)}, bf16[4,64,128]{2,1,0:T(8,128)(2,1)S(1)}, u32[]{:S(2)}, u32[]{:S(2)}) collective-permute-start(bf16[4,64,128]{2,1,0:T(8,128)(2,1)S(1)} %get-tuple-element.18), channel_id=1, source_target_pairs={{0,1},{1,0},{2,33},{3,32},{4,65},{5,64},{6,97},{7,96},{8,129},{9,1... | collective-permute-start | bytes 196616 | tf_op jit(solution)/shard_map/ppermute | solution.py:336
  148.9 2.6 %collective-permute-done.5.same_ref = bf16[4,64,128]{2,1,0:T(8,128)(2,1)S(1)} collective-permute-done((bf16[4,64,128]{2,1,0:T(8,128)(2,1)S(1)}, bf16[4,64,128]{2,1,0:T(8,128)(2,1)S(1)}, u32[]{:S(2)}, u32[]{:S(2)}) %collective-permute-start.5) | collective-permute-done | bytes 65568 | tf_op jit(solution)/shard_map/ppermute | solution.py:335
  151.5 2.9 %collective-permute-done.6.other_ref = bf16[4,64,128]{2,1,0:T(8,128)(2,1)S(1)} collective-permute-done((bf16[4,64,128]{2,1,0:T(8,128)(2,1)S(1)}, bf16[4,64,128]{2,1,0:T(8,128)(2,1)S(1)}, u32[]{:S(2)}, u32[]{:S(2)}) %collective-permute-start.6) | collective-permute-done | bytes 65568 | tf_op jit(solution)/shard_map/ppermute | solution.py:336
  154.4 0.0 copy-done.6
  154.4 0.8 shard_map.62
  155.2 23.8 %all_to_all.16 = f32[16,32,128]{2,1,0:T(8,128)S(1)} all-to-all(f32[16,32,128]{2,1,0:T(8,128)S(1)} %shard_map.62), channel_id=1, replica_groups=mesh['zl'=2,'x'=4,'core'=2,'zh'=4,'y'=8] {'zl','x','core'}, dimensions={0} | all-to-all | bytes 524288 | tf_op jit(solution)/shard_map/all_to_all | solution.py:337
  179.0 0.8 copy.11
  (1 shorter events, 0.0 us)
Async XLA Ops:
  9.3 30.7 %all-to-all-start = ((bf16[8,6,64,128]{3,2,1,0:T(8,128)(2,1)}), bf16[8,6,64,128]{3,2,1,0:T(8,128)(2,1)S(1)}, u32[]{:S(2)}, u32[]{:S(2)}) async-start(bf16[8,6,64,128]{3,2,1,0:T(8,128)(2,1)} %get-tuple-element.12), calls=%async_computation | async-start | bytes 1572864 | tf_op jit(solution)/shard_map/all_to_all | solution.py:318
  17.0 92.9 %all-gather.4.cloned.1.call-start = ((), (), s32[]{:S(2)}) async-start(), calls=%async_computation.3 | async-start | bytes 5898240 | tf_op jit(solution)/shard_map/all_gather | solution.py:319
  40.0 53.5 %copy-start = (bf16[8,64,2048]{2,1,0:T(8,128)(2,1)S(1)}, bf16[8,64,2048]{2,1,0:T(8,128)(2,1)}, u32[]{:S(2)}) copy-start(bf16[8,64,2048]{2,1,0:T(8,128)(2,1)} %own_ref.5) | copy-start | bytes 6291460
  40.0 29.0 %collective-permute-start = (bf16[8,6,64,128]{3,2,1,0:T(8,128)(2,1)S(1)}, bf16[8,6,64,128]{3,2,1,0:T(8,128)(2,1)S(1)}, u32[]{:S(2)}, u32[]{:S(2)}) collective-permute-start(bf16[8,6,64,128]{3,2,1,0:T(8,128)(2,1)S(1)} %all-to-all-done.near_ref.other_ref), channel_id=1, source_target_pairs={{0,8},{8,16},{16,24},{24,0},{1,9},{9,17},{17,25},{25,1},{2,10},{10... | collective-permute-start | bytes 2359304 | tf_op jit(solution)/shard_map/ppermute | solution.py:321
  46.5 41.0 %collective-permute-start.2 = (bf16[8,6,64,128]{3,2,1,0:T(8,128)(2,1)S(1)}, bf16[8,6,64,128]{3,2,1,0:T(8,128)(2,1)S(1)}, u32[]{:S(2)}, u32[]{:S(2)}) collective-permute-start(bf16[8,6,64,128]{3,2,1,0:T(8,128)(2,1)S(1)} %all-to-all-done.near_ref.other_ref), channel_id=1, source_target_pairs={{0,24},{8,0},{16,8},{24,16},{1,25},{9,1},{17,9},{25,17},{2,26},{10... | collective-permute-start | bytes 2359304 | tf_op jit(solution)/shard_map/ppermute | solution.py:322
  69.0 18.5 %copy-start.1 = (bf16[8,6,64,128]{3,2,1,0:T(8,128)(2,1)}, bf16[8,6,64,128]{3,2,1,0:T(8,128)(2,1)S(1)}, u32[]{:S(2)}) copy-start(bf16[8,6,64,128]{3,2,1,0:T(8,128)(2,1)S(1)} %collective-permute-done.back_ref) | copy-start | bytes 2359300
  69.9 34.5 %collective-permute-start.1 = (bf16[4,6,64,128]{3,2,1,0:T(8,128)(2,1)}, bf16[4,6,64,128]{3,2,1,0:T(8,128)(2,1)S(1)}, u32[]{:S(2)}, u32[]{:S(2)}) collective-permute-start(bf16[4,6,64,128]{3,2,1,0:T(8,128)(2,1)} %slice.8), channel_id=1, source_target_pairs={{0,8},{8,16},{16,24},{24,0},{1,9},{9,17},{17,25},{25,1},{2,10},{10... | collective-permute-start | bytes 1179656 | tf_op jit(solution)/shard_map/ppermute | solution.py:323
  87.6 1.0 copy-start.3
  88.6 19.6 %collective-permute-start.3 = (bf16[4,6,64,128]{3,2,1,0:T(8,128)(2,1)}, bf16[4,6,64,128]{3,2,1,0:T(8,128)(2,1)}, u32[]{:S(2)}, u32[]{:S(2)}) collective-permute-start(bf16[4,6,64,128]{3,2,1,0:T(8,128)(2,1)} %slice.9), channel_id=1, source_target_pairs={{0,24},{8,0},{16,8},{24,16},{1,25},{9,1},{17,9},{25,17},{2,26},{10... | collective-permute-start | bytes 1179656 | tf_op jit(solution)/shard_map/ppermute | solution.py:324
  93.5 1.1 copy-start.2
  94.7 1.1 copy-start.4
  114.4 7.7 %collective-permute-start.4 = (bf16[8,128,512]{2,1,0:T(8,128)(2,1)S(1)}, bf16[8,128,512]{2,1,0:T(8,128)(2,1)S(1)}, u32[]{:S(2)}, u32[]{:S(2)}) collective-permute-start(bf16[8,128,512]{2,1,0:T(8,128)(2,1)S(1)} %get-tuple-element.15), channel_id=1, source_target_pairs={{0,32},{32,0},{1,33},{33,1},{2,34},{34,2},{3,35},{35,3},{4,36},{36... | collective-permute-start | bytes 3145736 | tf_op jit(solution)/shard_map/ppermute | solution.py:330
  122.4 21.2 %copy-start.5 = (s32[16,16]{1,0:T(8,128)S(1)}, s32[16,16]{1,0:T(8,128)}, u32[]{:S(2)}) copy-start(s32[16,16]{1,0:T(8,128)} %mask_ref.3) | copy-start | bytes 3076
  122.4 32.0 %copy-start.6 = (s32[8]{0:T(128)S(1)}, s32[8]{0:T(128)}, u32[]{:S(2)}) copy-start(s32[8]{0:T(128)} %partner_ref.1) | copy-start | bytes 100
  145.0 6.5 %collective-permute-start.5 = (bf16[4,64,128]{2,1,0:T(8,128)(2,1)S(1)}, bf16[4,64,128]{2,1,0:T(8,128)(2,1)S(1)}, u32[]{:S(2)}, u32[]{:S(2)}) collective-permute-start(bf16[4,64,128]{2,1,0:T(8,128)(2,1)S(1)} %get-tuple-element.17), channel_id=1, source_target_pairs={{0,0},{1,1},{2,32},{3,33},{4,64},{5,65},{6,96},{7,97},{8,128},{9,1... | collective-permute-start | bytes 196616 | tf_op jit(solution)/shard_map/ppermute | solution.py:335
  146.9 7.5 %collective-permute-start.6 = (bf16[4,64,128]{2,1,0:T(8,128)(2,1)S(1)}, bf16[4,64,128]{2,1,0:T(8,128)(2,1)S(1)}, u32[]{:S(2)}, u32[]{:S(2)}) collective-permute-start(bf16[4,64,128]{2,1,0:T(8,128)(2,1)S(1)} %get-tuple-element.18), channel_id=1, source_target_pairs={{0,1},{1,0},{2,33},{3,32},{4,65},{5,64},{6,97},{7,96},{8,129},{9,1... | collective-permute-start | bytes 196616 | tf_op jit(solution)/shard_map/ppermute | solution.py:336
Sparse Core Ops, SparseCore 0:
  40.2 68.6 all-gather.3

commit v5 on v4

--- a/solution.py
+++ b/solution.py
@@ -1,3 +1,5 @@
+import functools
+
 import jax
 import jax.numpy as jnp
 from jax import lax
@@ -22,34 +24,47 @@
     return at
 
 
-def prepare_kernel(mask_ref, amps_ref, factor_ref, first_ref, second_ref, copy_sem):
-    batch_count, ring = factor_ref.shape[0], second_ref.shape[1]
+def prepare_kernel(mask_ref, amps_ref, factor_ref, first_ref, second_ref, masked_ref, slice_ref, sems):
+    batch_count, (copies, ring) = factor_ref.shape[0], second_ref.shape[:2]
     r = place(ROW)
     cols = amps_ref.shape[2]
+    load = pltpu.make_async_copy(amps_ref, masked_ref, sems.at[0])
+    load.start()
     block = factor_ref.at[:, :, pl.ds(pl.multiple_of(r * cols, cols), cols)]
-    copy = pltpu.make_async_copy(block, first_ref.at[:batch_count], copy_sem)
-    copy.start()
+    fetch = pltpu.make_async_copy(block, slice_ref, sems.at[1])
+    fetch.start()
     weight = mask_ref[place(COL) // 2, r].astype(jnp.float32).astype(jnp.bfloat16)
-    masked = amps_ref[:ring] * weight
-    for k in range(second_ref.shape[0]):
-        second_ref[k] = masked
-    first_ref[batch_count:] = amps_ref[ring:] * weight
-    copy.wait()
+    load.wait()
+    masked_ref[...] = masked_ref[...] * weight
+    stores = [pltpu.make_async_copy(masked_ref.at[ring:], first_ref.at[batch_count:], sems.at[2])]
+    for k in range(copies):
+        stores.append(pltpu.make_async_copy(masked_ref.at[:ring], second_ref.at[k], sems.at[4 + k]))
+    for store in stores:
+        store.start()
+    fetch.wait()
+    stores.append(pltpu.make_async_copy(slice_ref, first_ref.at[:batch_count], sems.at[3]))
+    stores[-1].start()
+    for store in stores:
+        store.wait()
 
 
 def prepare_call(mask, amplitudes, factors, ring, copies):
     pair_count, rows, cols = amplitudes.shape
     flat = factors.shape[0] + pair_count - ring
-    vmem = pl.BlockSpec(memory_space=pltpu.VMEM)
+    hbm = pl.BlockSpec(memory_space=pltpu.HBM)
     return pl.pallas_call(
         prepare_kernel,
-        in_specs=[pl.BlockSpec(memory_space=pltpu.SMEM), vmem, pl.BlockSpec(memory_space=pltpu.HBM)],
-        out_specs=[vmem, vmem],
+        in_specs=[pl.BlockSpec(memory_space=pltpu.SMEM), hbm, hbm],
+        out_specs=[hbm, hbm],
         out_shape=[
             jax.ShapeDtypeStruct((flat, rows, cols), jnp.bfloat16),
             jax.ShapeDtypeStruct((copies, ring, rows, cols), jnp.bfloat16),
         ],
-        scratch_shapes=[pltpu.SemaphoreType.DMA],
+        scratch_shapes=[
+            pltpu.VMEM(amplitudes.shape, jnp.bfloat16),
+            pltpu.VMEM((factors.shape[0], rows, cols), jnp.bfloat16),
+            pltpu.SemaphoreType.DMA((4 + copies,)),
+        ],
         compiler_params=params(60),
     )(mask, amplitudes, factors)
 
@@ -131,101 +146,81 @@
     )(own, *parts, early)
 
 
-def ladder_term(inner_ref, low_ref, high_ref, out_ref):
-    y_count, z_count, batch_count, rows, cols = low_ref.shape
-    blocks = [(ref, z) for z in range(z_count) for ref in (low_ref, high_ref)]
-    lanes = [
-        jnp.concatenate([ref[y, z, q] for ref, z in blocks for y in range(y_count)], axis=0)
-        for q in range(batch_count)
-    ]
-    factor = jnp.concatenate(lanes, axis=1)
-    product = jnp.dot(factor, inner_ref[...], preferred_element_type=jnp.float32).astype(out_ref.dtype)
-    height = y_count * rows
-    for k in range(len(blocks)):
-        out_ref[k] = product[k * height : (k + 1) * height]
-
-
-def send_kernel(side_ref, own_ref, ring_ref, *refs):
-    amps_refs, (low_ref, high_ref, out_ref, inner_ref) = refs[:-4], refs[-4:]
+def flat_kernel(own_ref, units_ref, out_ref, amps_ref, sems):
     batch_count, block_rows, width = own_ref.shape
-    ring = ring_ref.shape[1]
-
-    @pl.when(pl.program_id(0) == 0)
-    def _():
-        inner_ref[:, :ring] = ring_ref[...]
-        own = own_ref[...].reshape(batch_count * block_rows, width)
-        lanes = [
-            jnp.concatenate([ref[y, z, 0] for z in range(ref.shape[1]) for y in range(ref.shape[0])], axis=0)
-            for ref in amps_refs
-        ]
-        product = jnp.dot(own, jnp.concatenate(lanes, axis=1), preferred_element_type=jnp.float32)
-        spread_product(product, inner_ref, ring, batch_count, block_rows)
-
-    pl.when(pl.program_id(0) > 0)(lambda: ladder_term(inner_ref, low_ref, high_ref, out_ref))
-
-
-ZSTEP = 2
-
-
-def send_call(side, own, ring_inner, units):
-    depth, ring_width = ring_inner.shape
+    y_count, z_count, pairs, rows, cols = amps_ref.shape
+    loads = []
+    for p in range(pairs):
+        block = units_ref.at[:, :, batch_count + p]
+        loads.append(pltpu.make_async_copy(block, amps_ref.at[:, :, p], sems.at[p]))
+        loads[p].start()
+    lanes = []
+    for p in range(pairs):
+        loads[p].wait()
+        lanes.append(jnp.concatenate([amps_ref[y, z, p] for z in range(z_count) for y in range(y_count)], axis=0))
+    own = own_ref[...].reshape(batch_count * block_rows, width)
+    product = jnp.dot(own, jnp.concatenate(lanes, axis=1), preferred_element_type=jnp.float32)
+    spread_product(product, out_ref, 0, batch_count, block_rows)
+
+
+def flat_call(own, units):
     batch_count, block_rows, width = own.shape
     y_count, z_count, unit_count, rows, cols = units.shape
-    flat = unit_count - batch_count
-    inner_width = ring_width + flat * block_rows
-    quarter = (y_count // 4, ZSTEP, batch_count, rows, cols)
-    blocks = 2 * ZSTEP
-
-    def amps_spec(k):
-        return pl.BlockSpec((y_count, z_count, 1, rows, cols), lambda i, side: (0, 0, batch_count + k, 0, 0))
-
-    return pl.pallas_call(
-        send_kernel,
-        grid_spec=pltpu.PrefetchScalarGridSpec(
-            num_scalar_prefetch=1,
-            grid=(z_count // ZSTEP + 1,),
-            in_specs=[pl.BlockSpec(memory_space=pltpu.VMEM)] * 2
-            + [amps_spec(k) for k in range(flat)]
-            + [
-                pl.BlockSpec(quarter, lambda i, side: (side[0], jnp.maximum(i - 1, 0), 0, 0, 0)),
-                pl.BlockSpec(quarter, lambda i, side: (side[0] + 2, jnp.maximum(i - 1, 0), 0, 0, 0)),
-            ],
-            out_specs=[
-                pl.BlockSpec((blocks, 2 * rows, inner_width), lambda i, side: (jnp.maximum(i - 1, 0), 0, 0)),
-                pl.BlockSpec((depth, inner_width), lambda i, side: (0, 0)),
-            ],
-        ),
-        out_shape=[
-            jax.ShapeDtypeStruct((8, 2 * rows, inner_width), jnp.bfloat16),
-            jax.ShapeDtypeStruct((depth, inner_width), jnp.bfloat16),
+    pairs = unit_count - batch_count
+    vmem = pl.BlockSpec(memory_space=pltpu.VMEM)
+    return pl.pallas_call(
+        flat_kernel,
+        in_specs=[vmem, pl.BlockSpec(memory_space=pltpu.HBM)],
+        out_specs=vmem,
+        out_shape=jax.ShapeDtypeStruct((batch_count * cols, pairs * block_rows), jnp.bfloat16),
+        scratch_shapes=[
+            pltpu.VMEM((y_count, z_count, pairs, rows, cols), jnp.bfloat16),
+            pltpu.SemaphoreType.DMA((pairs,)),
         ],
         compiler_params=params(48),
-    )(side, own, ring_inner, *[units] * (flat + 2))
-
-
-def keep_kernel(side_ref, inner_ref, low_ref, high_ref, out_ref):
-    ladder_term(inner_ref, low_ref, high_ref, out_ref)
-
-
-def keep_call(side, inner, units):
-    depth, inner_width = inner.shape
+    )(own, units)
+
+
+def ladder_kernel(flip, ring_ref, flat_ref, units_ref, out_ref, block_ref, sems):
+    y_count, z_count, batch_count, rows, cols = block_ref.shape
+    side = lax.rem(lax.axis_index("core") + flip, 2)
+    pair, step = y_count // 2, z_count // 2
+    loads = []
+    for k in range(2):
+        for half in range(2):
+            source = units_ref.at[pl.ds((side + 2 * half) * pair, pair), pl.ds(k * step, step), pl.ds(0, batch_count)]
+            target = block_ref.at[pl.ds(half * pair, pair), pl.ds(k * step, step)]
+            loads.append(pltpu.make_async_copy(source, target, sems.at[2 * k + half]))
+            loads[-1].start()
+    inner = jnp.concatenate([ring_ref[...], flat_ref[...]], axis=1)
+    height = pair * rows
+    for k in range(2):
+        loads[2 * k].wait()
+        loads[2 * k + 1].wait()
+        places = [(z, y) for z in range(k * step, (k + 1) * step) for y in range(y_count)]
+        lanes = [jnp.concatenate([block_ref[y, z, q] for z, y in places], axis=0) for q in range(batch_count)]
+        factor = jnp.concatenate(lanes, axis=1)
+        product = jnp.dot(factor, inner, preferred_element_type=jnp.float32).astype(out_ref.dtype)
+        for m in range(2 * step):
+            out_ref[2 * step * k + m] = product[m * height : (m + 1) * height]
+
+
+def ladder_call(flip, ring, flat, units, kind):
+    depth, width = ring.shape[0], ring.shape[1] + flat.shape[1]
     y_count, z_count, unit_count, rows, cols = units.shape
-    quarter = (y_count // 4, ZSTEP, depth // cols, rows, cols)
-    return pl.pallas_call(
-        keep_kernel,
-        grid_spec=pltpu.PrefetchScalarGridSpec(
-            num_scalar_prefetch=1,
-            grid=(z_count // ZSTEP,),
-            in_specs=[
-                pl.BlockSpec(memory_space=pltpu.VMEM),
-                pl.BlockSpec(quarter, lambda i, side: (side[0], i, 0, 0, 0)),
-                pl.BlockSpec(quarter, lambda i, side: (side[0] + 2, i, 0, 0, 0)),
-            ],
-            out_specs=pl.BlockSpec((2 * ZSTEP, 2 * rows, inner_width), lambda i, side: (i, 0, 0)),
-        ),
-        out_shape=jax.ShapeDtypeStruct((8, 2 * rows, inner_width), jnp.float32),
+    batch_count = depth // cols
+    vmem = pl.BlockSpec(memory_space=pltpu.VMEM)
+    return pl.pallas_call(
+        functools.partial(ladder_kernel, flip),
+        in_specs=[vmem, vmem, pl.BlockSpec(memory_space=pltpu.HBM)],
+        out_specs=vmem,
+        out_shape=jax.ShapeDtypeStruct((2 * z_count, y_count // 4 * rows, width), kind),
+        scratch_shapes=[
+            pltpu.VMEM((y_count // 2, z_count, batch_count, rows, cols), jnp.bfloat16),
+            pltpu.SemaphoreType.DMA((4,)),
+        ],
         compiler_params=params(48),
-    )(side, inner, units, units)
+    )(ring, flat, units)
 
 
 def reduce_kernel(mask_ref, part_ref, kept_ref, same_ref, other_ref):
@@ -325,10 +320,9 @@
 
     early = early_call(factors, (near, back, ahead))
     late = late_call(factors, (left, right), early)
-    core = lax.axis_index("core").reshape(1)
-    send, inner = send_call(1 - core, factors, late, units)
-    swapped = lax.ppermute(send, "core", turn(2, 1))
-    keep = keep_call(core, inner, units)
+    flat = flat_call(factors, units)
+    swapped = lax.ppermute(ladder_call(1, late, flat, units, jnp.bfloat16), "core", turn(2, 1))
+    keep = ladder_call(0, late, flat, units, jnp.float32)
     partial = (keep + swapped.astype(jnp.float32)).astype(jnp.bfloat16)
     pieces = lax.all_to_all(partial, ("zl", "x"), split_axis=0, concat_axis=0)
     kept, same, other = reduce_call(out_mask, pieces, block_rows)

time: 187 us -> 186 us (level)
  local copies, waits for them, and re-layouts: 4.91 us -> 0.82 us
  waiting for transfers between devices: 31.6 us -> 33.9 us
  blocking collectives: 68 us -> 70.2 us
    all_gather x1, waiting for transfers between devices: 0.02 us -> 3.53 us  [on_device(): lax.all_gather(gate_call(lax.all_gather(first, 'zh', axis=0), near), 'y',...]
    ppermute x1, waiting for transfers between devices: 6.46 us -> 9.53 us  [on_device(): left = lax.ppermute(back[:4], 'zh', turn(4, 1))]
    ppermute x1, waiting for transfers between devices: 3.86 us -> 1.28 us  [on_device(): right = lax.ppermute(ahead[4:], 'zh', turn(4, -1))]
    unnamed x14 -> x6, local copies, waits for them, and re-layouts: 2.46 us -> 0.02 us
    ppermute x1, starting transfers between devices: 4.98 us -> 2.59 us  [on_device(): lax.ppermute(ladder_call(1, late, flat, units, jnp.bfloat16), 'core', tur...]
    pallas_call x2 -> x3, Pallas kernels: 7.09 us -> 7.35 us  [the longest x2 5.33 us: ladder_call(): pl.pallas_call(functools.partial(ladder_kernel, flip), in_specs=[vmem, vm...]
  transfers between devices with their start and end apart: 9 -> 9, of which waited for: 5 -> 6; matrix products, arithmetic and copies ran while one was open for 1% -> 0% of each run, Pallas kernels for 3% -> 3%
where the time goes in v5:
time: 186 us
  blocking collectives  70.2 us (38%)
  starting transfers between devices  51.7 us (28%)
  waiting for transfers between devices  33.9 us (18%)
  Pallas kernels  15 us (8%)
  between operations  13.6 us (7%)
    all_to_all x1, blocking collectives, on_device(): lax.all_to_all(combine_call(partner, kept, same, other), ROW, split_axis=...  24.9 us
    all_gather x1, blocking collectives, on_device(): lax.all_gather(first, 'zh', axis=0)  23 us
    all_to_all x1, blocking collectives, on_device(): pieces = lax.all_to_all(partial, ('zl', 'x'), split_axis=0, concat_axis=0)  22.3 us
    ppermute x1, starting transfers between devices, on_device(): left = lax.ppermute(back[:4], 'zh', turn(4, 1))  17.7 us
    ppermute x1, waiting for transfers between devices, on_device(): back = lax.ppermute(near, 'zh', turn(4, 1))  15.7 us
    ppermute x1, waiting for transfers between devices, on_device(): left = lax.ppermute(back[:4], 'zh', turn(4, 1))  9.53 us
    all_to_all x1, starting transfers between devices, on_device(): near = lax.all_to_all(second, 'y', split_axis=0, concat_axis=0)  7.66 us
    ppermute x1, starting transfers between devices, on_device(): ahead = lax.ppermute(near, 'zh', turn(4, -1))  6.77 us
  transfers between devices with their start and end apart: 9, of which 6 were waited for; matrix products, arithmetic and copies ran while one was open for 0% of the time, Pallas kernels for 3%

profile of v5, /device:TPU:1, one launch (start us, length us, event | category | flops | bytes accessed | tf_op | source)
XLA Modules:
  0.0 185.6 jit_solution(7400087661299841049)
XLA Ops:
  6.5 2.7 %shard_map.55 = (bf16[10,64,128]{2,1,0:T(8,128)(2,1)}, bf16[8,6,64,128]{3,2,1,0:T(8,128)(2,1)}) custom-call(s32[16,16]{1,0:T(8,128)} %mask_ref.2, bf16[8,64,128]{2,1,0:T(8,128)(2,1)} %amps_ref.1, bf16[8,64,2048]{2,1,0:T(8,128)(2,1)} %own_ref.5), custom_call_target="tpu_custom_call" | custom-call | tf_op jit(solution)/shard_map/pallas_call | solution.py:55
  9.3 7.7 %all-to-all-start = ((bf16[8,6,64,128]{3,2,1,0:T(8,128)(2,1)}), bf16[8,6,64,128]{3,2,1,0:T(8,128)(2,1)S(1)}, u32[]{:S(2)}, u32[]{:S(2)}) async-start(bf16[8,6,64,128]{3,2,1,0:T(8,128)(2,1)} %get-tuple-element.10), calls=%async_computation | async-start | bytes 1572864 | tf_op jit(solution)/shard_map/all_to_all | solution.py:313
  16.9 0.0 all-gather.4.cloned.1.call-start
  17.0 23.0 %all-gather = bf16[40,64,128]{2,1,0:T(8,128)(2,1)} all-gather(bf16[10,64,128]{2,1,0:T(8,128)(2,1)} %get-tuple-element.11), channel_id=2, replica_groups=mesh['zl'=2,'x'=4,'core'=2,'zh'=4,'y'=8] {'zh'}, dimensions={0}, use_global_device_ids=true | all-gather | bytes 819200 | tf_op jit(solution)/shard_map/all_gather | solution.py:314
  40.0 0.0 all-to-all-done.near_ref.other_ref
  40.0 0.0 copy-start
  40.0 0.0 all-gather.4.cloned.1.call-update
  40.0 6.4 %collective-permute-start = (bf16[8,6,64,128]{3,2,1,0:T(8,128)(2,1)S(1)}, bf16[8,6,64,128]{3,2,1,0:T(8,128)(2,1)S(1)}, u32[]{:S(2)}, u32[]{:S(2)}) collective-permute-start(bf16[8,6,64,128]{3,2,1,0:T(8,128)(2,1)S(1)} %all-to-all-done.near_ref.other_ref), channel_id=1, source_target_pairs={{0,8},{8,16},{16,24},{24,0},{1,9},{9,17},{17,25},{25,1},{2,10},{10... | collective-permute-start | bytes 2359304 | tf_op jit(solution)/shard_map/ppermute | solution.py:316
  46.5 6.8 %collective-permute-start.2 = (bf16[8,6,64,128]{3,2,1,0:T(8,128)(2,1)S(1)}, bf16[8,6,64,128]{3,2,1,0:T(8,128)(2,1)S(1)}, u32[]{:S(2)}, u32[]{:S(2)}) collective-permute-start(bf16[8,6,64,128]{3,2,1,0:T(8,128)(2,1)S(1)} %all-to-all-done.near_ref.other_ref), channel_id=1, source_target_pairs={{0,24},{8,0},{16,8},{24,16},{1,25},{9,1},{17,9},{25,17},{2,26},{10... | collective-permute-start | bytes 2359304 | tf_op jit(solution)/shard_map/ppermute | solution.py:317
  53.3 15.7 %collective-permute-done.back_ref = bf16[8,6,64,128]{3,2,1,0:T(8,128)(2,1)S(1)} collective-permute-done((bf16[8,6,64,128]{3,2,1,0:T(8,128)(2,1)S(1)}, bf16[8,6,64,128]{3,2,1,0:T(8,128)(2,1)S(1)}, u32[]{:S(2)}, u32[]{:S(2)}) %collective-permute-start) | collective-permute-done | bytes 786464 | tf_op jit(solution)/shard_map/ppermute | solution.py:316
  69.0 17.7 %collective-permute-start.1 = (bf16[4,6,64,128]{3,2,1,0:T(8,128)(2,1)S(1)}, bf16[4,6,64,128]{3,2,1,0:T(8,128)(2,1)S(1)}, u32[]{:S(2)}, u32[]{:S(2)}) collective-permute-start(bf16[4,6,64,128]{3,2,1,0:T(8,128)(2,1)S(1)} %slice.8), channel_id=1, source_target_pairs={{0,8},{8,16},{16,24},{24,0},{1,9},{9,17},{17,25},{25,1},{2,10},{10... | collective-permute-start | bytes 1179656 | tf_op jit(solution)/shard_map/ppermute | solution.py:318
  86.7 0.0 collective-permute-done.2.ahead_ref
  86.8 4.9 %collective-permute-start.3 = (bf16[4,6,64,128]{3,2,1,0:T(8,128)(2,1)S(1)}, bf16[4,6,64,128]{3,2,1,0:T(8,128)(2,1)S(1)}, u32[]{:S(2)}, u32[]{:S(2)}) collective-permute-start(bf16[4,6,64,128]{3,2,1,0:T(8,128)(2,1)S(1)} %slice.9), channel_id=1, source_target_pairs={{0,24},{8,0},{16,8},{24,16},{1,25},{9,1},{17,9},{25,17},{2,26},{10... | collective-permute-start | bytes 1179656 | tf_op jit(solution)/shard_map/ppermute | solution.py:319
  91.7 0.0 copy-done
  91.7 2.0 %shard_map.56.early_ref = f32[512,768]{1,0:T(8,128)S(1)} custom-call(bf16[8,64,2048]{2,1,0:T(8,128)(2,1)S(1)} %copy-done, bf16[8,6,64,128]{3,2,1,0:T(8,128)(2,1)S(1)} %all-to-all-done.near_ref.other_ref, bf16[8,6,64,128]{3,2,1,0:T(8,128)(2,1)S(1)} %collective-permute-done.back_ref, bf16[8,6,64,128]{3,2,1,0:T(8,128)(2,1)S(1)} %collective-permute-done.2.ahead_ref), custom_call_target="tpu_custom_call" | custom-call | tf_op jit(solution)/shard_map/pallas_call | solution.py:119
  93.8 9.5 %collective-permute-done.1.left_ref = bf16[4,6,64,128]{3,2,1,0:T(8,128)(2,1)S(1)} collective-permute-done((bf16[4,6,64,128]{3,2,1,0:T(8,128)(2,1)S(1)}, bf16[4,6,64,128]{3,2,1,0:T(8,128)(2,1)S(1)}, u32[]{:S(2)}, u32[]{:S(2)}) %collective-permute-start.1) | collective-permute-done | bytes 393248 | tf_op jit(solution)/shard_map/ppermute | solution.py:318
  103.3 1.3 collective-permute-done.3.right_ref
  104.6 0.7 shard_map.57.ring_ref
  105.3 3.5 %all-gather.4.cloned.1.call-done = bf16[32,10,64,128]{3,2,1,0:T(8,128)(2,1)} async-done(((bf16[4,10,64,128]{3,2,1,0:T(8,128)(2,1)}), bf16[32,10,64,128]{3,2,1,0:T(8,128)(2,1)}) %all-gather.4.cloned.1.call-update) | async-done | bytes 5242896 | tf_op jit(solution)/shard_map/all_gather | solution.py:314
  108.8 2.0 %shard_map.59.flat_ref = bf16[1024,128]{1,0:T(8,128)(2,1)S(1)} custom-call(bf16[8,64,2048]{2,1,0:T(8,128)(2,1)S(1)} %copy-done, bf16[8,4,10,64,128]{4,3,2,1,0:T(8,128)(2,1)} %bitcast.9), custom_call_target="tpu_custom_call" | custom-call | tf_op jit(solution)/shard_map/pallas_call | solution.py:171
  110.8 2.7 %shard_map.61 = bf16[8,128,512]{2,1,0:T(8,128)(2,1)S(1)} custom-call(bf16[1024,384]{1,0:T(8,128)(2,1)S(1)} %shard_map.57.ring_ref, bf16[1024,128]{1,0:T(8,128)(2,1)S(1)} %shard_map.59.flat_ref, bf16[8,4,10,64,128]{4,3,2,1,0:T(8,128)(2,1)} %bitcast.10), custom_call_target="tpu_custom_call" | custom-call | tf_op jit(solution)/shard_map/pallas_call | solution.py:213
  113.5 2.6 %collective-permute-start.4 = (bf16[8,128,512]{2,1,0:T(8,128)(2,1)S(1)}, bf16[8,128,512]{2,1,0:T(8,128)(2,1)S(1)}, u32[]{:S(2)}, u32[]{:S(2)}) collective-permute-start(bf16[8,128,512]{2,1,0:T(8,128)(2,1)S(1)} %shard_map.61), channel_id=1, source_target_pairs={{0,32},{32,0},{1,33},{33,1},{2,34},{34,2},{3,35},{35,3},{4,36},{36... | collective-permute-start | bytes 3145736 | tf_op jit(solution)/shard_map/ppermute | solution.py:324
  116.1 2.7 %shard_map.60 = f32[8,128,512]{2,1,0:T(8,128)S(1)} custom-call(bf16[1024,384]{1,0:T(8,128)(2,1)S(1)} %shard_map.57.ring_ref, bf16[1024,128]{1,0:T(8,128)(2,1)S(1)} %shard_map.59.flat_ref, bf16[8,4,10,64,128]{4,3,2,1,0:T(8,128)(2,1)} %bitcast.11), custom_call_target="tpu_custom_call" | custom-call | tf_op jit(solution)/shard_map/pallas_call | solution.py:213
  118.8 0.0 collective-permute-done.4
  118.8 0.3 add_convert_fusion
  119.2 0.0 copy-start.1
  119.2 0.0 copy-start.2
  119.2 22.3 %all_to_all.15.part_ref = bf16[8,128,512]{2,1,0:T(8,128)(2,1)S(1)} all-to-all(bf16[8,128,512]{2,1,0:T(8,128)(2,1)S(1)} %add_convert_fusion), channel_id=1, replica_groups=mesh['zl'=2,'x'=4,'core'=2,'zh'=4,'y'=8] {'zl','x'}, dimensions={0} | all-to-all | bytes 2097152 | tf_op jit(solution)/shard_map/all_to_all | solution.py:327
  141.5 0.0 copy-done.1
  141.5 1.4 shard_map.62
  142.9 1.9 %collective-permute-start.5 = (bf16[4,64,128]{2,1,0:T(8,128)(2,1)S(1)}, bf16[4,64,128]{2,1,0:T(8,128)(2,1)S(1)}, u32[]{:S(2)}, u32[]{:S(2)}) collective-permute-start(bf16[4,64,128]{2,1,0:T(8,128)(2,1)S(1)} %get-tuple-element.13), channel_id=1, source_target_pairs={{0,0},{1,1},{2,32},{3,33},{4,64},{5,65},{6,96},{7,97},{8,128},{9,1... | collective-permute-start | bytes 196616 | tf_op jit(solution)/shard_map/ppermute | solution.py:329
  144.8 3.7 %collective-permute-start.6 = (bf16[4,64,128]{2,1,0:T(8,128)(2,1)S(1)}, bf16[4,64,128]{2,1,0:T(8,128)(2,1)S(1)}, u32[]{:S(2)}, u32[]{:S(2)}) collective-permute-start(bf16[4,64,128]{2,1,0:T(8,128)(2,1)S(1)} %get-tuple-element.14), channel_id=1, source_target_pairs={{0,1},{1,0},{2,33},{3,32},{4,65},{5,64},{6,97},{7,96},{8,129},{9,1... | collective-permute-start | bytes 196616 | tf_op jit(solution)/shard_map/ppermute | solution.py:330
  148.5 0.9 collective-permute-done.5.same_ref
  149.4 2.9 %collective-permute-done.6.other_ref = bf16[4,64,128]{2,1,0:T(8,128)(2,1)S(1)} collective-permute-done((bf16[4,64,128]{2,1,0:T(8,128)(2,1)S(1)}, bf16[4,64,128]{2,1,0:T(8,128)(2,1)S(1)}, u32[]{:S(2)}, u32[]{:S(2)}) %collective-permute-start.6) | collective-permute-done | bytes 65568 | tf_op jit(solution)/shard_map/ppermute | solution.py:330
  152.3 0.0 copy-done.2
  152.3 0.8 shard_map.63
  153.1 24.9 %all_to_all.16 = f32[16,32,128]{2,1,0:T(8,128)S(1)} all-to-all(f32[16,32,128]{2,1,0:T(8,128)S(1)} %shard_map.63), channel_id=1, replica_groups=mesh['zl'=2,'x'=4,'core'=2,'zh'=4,'y'=8] {'zl','x','core'}, dimensions={0} | all-to-all | bytes 524288 | tf_op jit(solution)/shard_map/all_to_all | solution.py:331
  178.0 0.8 copy.11
  (3 shorter events, 0.1 us)
Async XLA Ops:
  9.3 30.7 %all-to-all-start = ((bf16[8,6,64,128]{3,2,1,0:T(8,128)(2,1)}), bf16[8,6,64,128]{3,2,1,0:T(8,128)(2,1)S(1)}, u32[]{:S(2)}, u32[]{:S(2)}) async-start(bf16[8,6,64,128]{3,2,1,0:T(8,128)(2,1)} %get-tuple-element.10), calls=%async_computation | async-start | bytes 1572864 | tf_op jit(solution)/shard_map/all_to_all | solution.py:313
  16.9 91.9 %all-gather.4.cloned.1.call-start = ((), (), s32[]{:S(2)}) async-start(), calls=%async_computation.3 | async-start | bytes 5898240 | tf_op jit(solution)/shard_map/all_gather | solution.py:314
  40.0 51.7 %copy-start = (bf16[8,64,2048]{2,1,0:T(8,128)(2,1)S(1)}, bf16[8,64,2048]{2,1,0:T(8,128)(2,1)}, u32[]{:S(2)}) copy-start(bf16[8,64,2048]{2,1,0:T(8,128)(2,1)} %own_ref.5) | copy-start | bytes 6291460
  40.0 29.0 %collective-permute-start = (bf16[8,6,64,128]{3,2,1,0:T(8,128)(2,1)S(1)}, bf16[8,6,64,128]{3,2,1,0:T(8,128)(2,1)S(1)}, u32[]{:S(2)}, u32[]{:S(2)}) collective-permute-start(bf16[8,6,64,128]{3,2,1,0:T(8,128)(2,1)S(1)} %all-to-all-done.near_ref.other_ref), channel_id=1, source_target_pairs={{0,8},{8,16},{16,24},{24,0},{1,9},{9,17},{17,25},{25,1},{2,10},{10... | collective-permute-start | bytes 2359304 | tf_op jit(solution)/shard_map/ppermute | solution.py:316
  46.5 40.3 %collective-permute-start.2 = (bf16[8,6,64,128]{3,2,1,0:T(8,128)(2,1)S(1)}, bf16[8,6,64,128]{3,2,1,0:T(8,128)(2,1)S(1)}, u32[]{:S(2)}, u32[]{:S(2)}) collective-permute-start(bf16[8,6,64,128]{3,2,1,0:T(8,128)(2,1)S(1)} %all-to-all-done.near_ref.other_ref), channel_id=1, source_target_pairs={{0,24},{8,0},{16,8},{24,16},{1,25},{9,1},{17,9},{25,17},{2,26},{10... | collective-permute-start | bytes 2359304 | tf_op jit(solution)/shard_map/ppermute | solution.py:317
  69.0 34.3 %collective-permute-start.1 = (bf16[4,6,64,128]{3,2,1,0:T(8,128)(2,1)S(1)}, bf16[4,6,64,128]{3,2,1,0:T(8,128)(2,1)S(1)}, u32[]{:S(2)}, u32[]{:S(2)}) collective-permute-start(bf16[4,6,64,128]{3,2,1,0:T(8,128)(2,1)S(1)} %slice.8), channel_id=1, source_target_pairs={{0,8},{8,16},{16,24},{24,0},{1,9},{9,17},{17,25},{25,1},{2,10},{10... | collective-permute-start | bytes 1179656 | tf_op jit(solution)/shard_map/ppermute | solution.py:318
  86.8 17.8 %collective-permute-start.3 = (bf16[4,6,64,128]{3,2,1,0:T(8,128)(2,1)S(1)}, bf16[4,6,64,128]{3,2,1,0:T(8,128)(2,1)S(1)}, u32[]{:S(2)}, u32[]{:S(2)}) collective-permute-start(bf16[4,6,64,128]{3,2,1,0:T(8,128)(2,1)S(1)} %slice.9), channel_id=1, source_target_pairs={{0,24},{8,0},{16,8},{24,16},{1,25},{9,1},{17,9},{25,17},{2,26},{10... | collective-permute-start | bytes 1179656 | tf_op jit(solution)/shard_map/ppermute | solution.py:319
  113.5 5.3 %collective-permute-start.4 = (bf16[8,128,512]{2,1,0:T(8,128)(2,1)S(1)}, bf16[8,128,512]{2,1,0:T(8,128)(2,1)S(1)}, u32[]{:S(2)}, u32[]{:S(2)}) collective-permute-start(bf16[8,128,512]{2,1,0:T(8,128)(2,1)S(1)} %shard_map.61), channel_id=1, source_target_pairs={{0,32},{32,0},{1,33},{33,1},{2,34},{34,2},{3,35},{35,3},{4,36},{36... | collective-permute-start | bytes 3145736 | tf_op jit(solution)/shard_map/ppermute | solution.py:324
  119.2 22.3 %copy-start.1 = (s32[16,16]{1,0:T(8,128)S(1)}, s32[16,16]{1,0:T(8,128)}, u32[]{:S(2)}) copy-start(s32[16,16]{1,0:T(8,128)} %mask_ref.3) | copy-start | bytes 3076
  119.2 33.1 %copy-start.2 = (s32[8]{0:T(128)S(1)}, s32[8]{0:T(128)}, u32[]{:S(2)}) copy-start(s32[8]{0:T(128)} %partner_ref.1) | copy-start | bytes 100
  142.9 6.5 %collective-permute-start.5 = (bf16[4,64,128]{2,1,0:T(8,128)(2,1)S(1)}, bf16[4,64,128]{2,1,0:T(8,128)(2,1)S(1)}, u32[]{:S(2)}, u32[]{:S(2)}) collective-permute-start(bf16[4,64,128]{2,1,0:T(8,128)(2,1)S(1)} %get-tuple-element.13), channel_id=1, source_target_pairs={{0,0},{1,1},{2,32},{3,33},{4,64},{5,65},{6,96},{7,97},{8,128},{9,1... | collective-permute-start | bytes 196616 | tf_op jit(solution)/shard_map/ppermute | solution.py:329
  144.8 7.5 %collective-permute-start.6 = (bf16[4,64,128]{2,1,0:T(8,128)(2,1)S(1)}, bf16[4,64,128]{2,1,0:T(8,128)(2,1)S(1)}, u32[]{:S(2)}, u32[]{:S(2)}) collective-permute-start(bf16[4,64,128]{2,1,0:T(8,128)(2,1)S(1)} %get-tuple-element.14), channel_id=1, source_target_pairs={{0,1},{1,0},{2,33},{3,32},{4,65},{5,64},{6,97},{7,96},{8,129},{9,1... | collective-permute-start | bytes 196616 | tf_op jit(solution)/shard_map/ppermute | solution.py:330
Sparse Core Ops, SparseCore 0:
  40.2 68.6 all-gather.3

commit v6 on v5

--- a/solution.py
+++ b/solution.py
@@ -24,7 +24,7 @@
     return at
 
 
-def prepare_kernel(mask_ref, amps_ref, factor_ref, first_ref, second_ref, masked_ref, slice_ref, sems):
+def prepare_kernel(mask_ref, amps_ref, factor_ref, first_ref, second_ref, masked_ref, slice_ref, order_ref, sems):
     batch_count, (copies, ring) = factor_ref.shape[0], second_ref.shape[:2]
     r = place(ROW)
     cols = amps_ref.shape[2]
@@ -42,6 +42,13 @@
     for store in stores:
         store.start()
     fetch.wait()
+    rows = slice_ref[...].astype(jnp.float32)
+    half = rows.shape[1] // 2
+    for k in range(half // 4):
+        for core in range(2):
+            at = core * half + k * 4
+            order_ref[:, at : at + 4, :] = rows[:, (2 * k + core) * 4 : (2 * k + core + 1) * 4, :]
+    slice_ref[...] = order_ref[...].astype(jnp.bfloat16)
     stores.append(pltpu.make_async_copy(slice_ref, first_ref.at[:batch_count], sems.at[3]))
     stores[-1].start()
     for store in stores:
@@ -63,6 +70,7 @@
         scratch_shapes=[
             pltpu.VMEM(amplitudes.shape, jnp.bfloat16),
             pltpu.VMEM((factors.shape[0], rows, cols), jnp.bfloat16),
+            pltpu.VMEM((factors.shape[0], rows, cols), jnp.float32),
             pltpu.SemaphoreType.DMA((4 + copies,)),
         ],
         compiler_params=params(60),
@@ -184,125 +192,180 @@
 def ladder_kernel(flip, ring_ref, flat_ref, units_ref, out_ref, block_ref, sems):
     y_count, z_count, batch_count, rows, cols = block_ref.shape
     side = lax.rem(lax.axis_index("core") + flip, 2)
-    pair, step = y_count // 2, z_count // 2
+    step = z_count // 2
+    here = pl.ds(pl.multiple_of(side * rows, rows), rows)
     loads = []
     for k in range(2):
-        for half in range(2):
-            source = units_ref.at[pl.ds((side + 2 * half) * pair, pair), pl.ds(k * step, step), pl.ds(0, batch_count)]
-            target = block_ref.at[pl.ds(half * pair, pair), pl.ds(k * step, step)]
-            loads.append(pltpu.make_async_copy(source, target, sems.at[2 * k + half]))
-            loads[-1].start()
+        span = pl.ds(k * step, step)
+        source = units_ref.at[:, span, pl.ds(0, batch_count), here]
+        loads.append(pltpu.make_async_copy(source, block_ref.at[:, span], sems.at[k]))
+        loads[-1].start()
     inner = jnp.concatenate([ring_ref[...], flat_ref[...]], axis=1)
-    height = pair * rows
+    height = step * y_count * rows
     for k in range(2):
-        loads[2 * k].wait()
-        loads[2 * k + 1].wait()
+        loads[k].wait()
         places = [(z, y) for z in range(k * step, (k + 1) * step) for y in range(y_count)]
         lanes = [jnp.concatenate([block_ref[y, z, q] for z, y in places], axis=0) for q in range(batch_count)]
         factor = jnp.concatenate(lanes, axis=1)
-        product = jnp.dot(factor, inner, preferred_element_type=jnp.float32).astype(out_ref.dtype)
-        for m in range(2 * step):
-            out_ref[2 * step * k + m] = product[m * height : (m + 1) * height]
+        product = jnp.dot(factor, inner, preferred_element_type=jnp.float32)
+        out_ref[k * height : (k + 1) * height] = product.astype(out_ref.dtype)
 
 
 def ladder_call(flip, ring, flat, units, kind):
     depth, width = ring.shape[0], ring.shape[1] + flat.shape[1]
     y_count, z_count, unit_count, rows, cols = units.shape
-    batch_count = depth // cols
     vmem = pl.BlockSpec(memory_space=pltpu.VMEM)
     return pl.pallas_call(
         functools.partial(ladder_kernel, flip),
         in_specs=[vmem, vmem, pl.BlockSpec(memory_space=pltpu.HBM)],
         out_specs=vmem,
-        out_shape=jax.ShapeDtypeStruct((2 * z_count, y_count // 4 * rows, width), kind),
+        out_shape=jax.ShapeDtypeStruct((y_count * z_count * rows // 2, width), kind),
         scratch_shapes=[
-            pltpu.VMEM((y_count // 2, z_count, batch_count, rows, cols), jnp.bfloat16),
-            pltpu.SemaphoreType.DMA((4,)),
+            pltpu.VMEM((y_count, z_count, depth // cols, rows // 2, cols), jnp.bfloat16),
+            pltpu.SemaphoreType.DMA((2,)),
         ],
         compiler_params=params(48),
     )(ring, flat, units)
 
 
-def reduce_kernel(mask_ref, part_ref, kept_ref, same_ref, other_ref):
-    c = place(COL)
-    weight = mask_ref[c // 2, place(ROW)].astype(jnp.float32)
-    side = lax.rem(c, 2)
-    half = kept_ref.shape[1]
-    total = part_ref[0].astype(jnp.float32)
-    for k in range(1, part_ref.shape[0]):
-        total = total + part_ref[k].astype(jnp.float32)
-    total = total * weight
-    straight = total.T
-    kept_ref[0], kept_ref[1] = straight[:half], straight[half:]
-    turned = total.astype(jnp.bfloat16)
-    low, high = turned[:half], turned[half:]
-    same_ref[0] = jnp.where(side == 0, low, high)
-    other_ref[0] = jnp.where(side == 0, high, low)
-
-
-def reduce_call(mask, pieces, rows):
-    sources, cols, inner_width = pieces.shape
-    pair_count = inner_width // rows
-    half_spec = pl.BlockSpec((1, rows, cols), lambda i: (i, 0, 0))
+def swing(block, axis):
+    half = block.shape[axis] // 2
+    first = lax.slice_in_dim(block, 0, half, axis=axis)
+    return jnp.concatenate([lax.slice_in_dim(block, half, 2 * half, axis=axis), first], axis=axis)
+
+
+def gather_kernel(keep_ref, other_ref, out_ref):
+    groups, height, cols = out_ref.shape
+    total = keep_ref[...] + other_ref[...].astype(jnp.float32)
+    tiles = total.reshape(height // 8, 2, groups // 2, 8, cols)
+    top = lax.broadcasted_iota(jnp.int32, (height // 8, 8, cols), 1) < 4
+    for k in range(groups // 2):
+        first, second = tiles[:, 0, k], tiles[:, 1, k]
+        even = jnp.where(top, first, swing(second, 1))
+        odd = jnp.where(top, swing(first, 1), second)
+        out_ref[2 * k] = even.reshape(height, cols).astype(jnp.bfloat16)
+        out_ref[2 * k + 1] = odd.reshape(height, cols).astype(jnp.bfloat16)
+
+
+def gather_call(keep, other, groups):
+    height, width = keep.shape
+    cols = 128
+    return pl.pallas_call(
+        gather_kernel,
+        grid=(width // cols,),
+        in_specs=[pl.BlockSpec((height, cols), lambda i: (0, i))] * 2,
+        out_specs=pl.BlockSpec((groups, height // groups, cols), lambda i: (0, 0, i)),
+        out_shape=jax.ShapeDtypeStruct((groups, height // groups, width), jnp.bfloat16),
+        compiler_params=params(),
+    )(keep, other)
+
+
+def reduce_kernel(mask_ref, part_ref, direct_ref, mirror_ref, stage_ref):
+    sources, height, width = part_ref.shape
+    cols = direct_ref.shape[3]
+    half = cols // 2
+    row = place(COL) // 2
+    for k in range(width // cols):
+        span = slice(k * cols, (k + 1) * cols)
+        total = part_ref[0, :, span].astype(jnp.float32)
+        for m in range(1, sources):
+            total = total + part_ref[m, :, span].astype(jnp.float32)
+        tiles = [total[t * 8 : (t + 1) * 8] * mask_ref[row, t].astype(jnp.float32) for t in range(height // 8)]
+        total = jnp.concatenate(tiles, axis=0)
+        tall = total.reshape(height // 8, 8, cols)
+        stage_ref[:, 0, k * 4 : (k + 1) * 4, :] = tall[:, :4]
+        stage_ref[:, 1, k * 4 : (k + 1) * 4, :] = tall[:, 4:]
+        straight = total.T
+        for m in range(2):
+            p = 2 * k + m
+            wide = straight[m * half : (m + 1) * half].reshape(half // 8, 8, height)
+            direct_ref[:, 0, p * 4 : (p + 1) * 4, :] = wide[:, :4]
+            direct_ref[:, 1, p * 4 : (p + 1) * 4, :] = wide[:, 4:]
+    mirror_ref[...] = stage_ref[...].astype(jnp.bfloat16)
+
+
+def reduce_call(mask, pieces):
+    sources, height, width = pieces.shape
+    cols = 128
+    vmem = pl.BlockSpec(memory_space=pltpu.VMEM)
+    groups = width // cols
     return pl.pallas_call(
         reduce_kernel,
-        grid=(pair_count // 2,),
-        in_specs=[
-            pl.BlockSpec(memory_space=pltpu.SMEM),
-            pl.BlockSpec((sources, cols, 2 * rows), lambda i: (0, 0, i)),
+        in_specs=[pl.BlockSpec(memory_space=pltpu.SMEM), vmem],
+        out_specs=[vmem, vmem],
+        out_shape=[
+            jax.ShapeDtypeStruct((cols // 16, 2, groups * 8, height), jnp.float32),
+            jax.ShapeDtypeStruct((height // 8, 2, groups * 4, cols), jnp.bfloat16),
         ],
-        out_specs=[pl.BlockSpec((2, rows, cols), lambda i: (i, 0, 0)), half_spec, half_spec],
-        out_shape=[
-            jax.ShapeDtypeStruct((pair_count, rows, cols), jnp.float32),
-            jax.ShapeDtypeStruct((pair_count // 2, rows, cols), jnp.bfloat16),
-            jax.ShapeDtypeStruct((pair_count // 2, rows, cols), jnp.bfloat16),
-        ],
+        scratch_shapes=[pltpu.VMEM((height // 8, 2, groups * 4, cols), jnp.float32)],
         compiler_params=params(),
     )(mask, pieces)
 
 
-def combine_kernel(partner_ref, kept_ref, same_ref, other_ref, out_ref):
-    side = lax.rem(place(COL), 2)
-    pair_count, rows, cols = kept_ref.shape
-    half = cols // 2
+def align_kernel(direct_ref, out_ref, rows_ref):
+    height, width = out_ref.shape
+    sources, _, cols = direct_ref.shape
+    blocks, pack = width // cols, cols // height
+    own_rows = cols // (2 * sources)
+    for g in range(sources // pack):
+        turned = direct_ref[g * pack : (g + 1) * pack].reshape(cols, cols).T
+        for m in range(pack):
+            at = (g * pack + m) * own_rows
+            tall = turned[:, m * height : (m + 1) * height].reshape(blocks, 2 * own_rows, height)
+            rows_ref[:, 0, at : at + own_rows, :] = tall[:, :own_rows]
+            rows_ref[:, 1, at : at + own_rows, :] = tall[:, own_rows:]
+    for k in range(blocks):
+        out_ref[:, k * cols : (k + 1) * cols] = rows_ref[k].reshape(cols, height).T
+
+
+def align_call(direct):
+    sources, height, cols = direct.shape
+    width = sources * cols
+    vmem = pl.BlockSpec(memory_space=pltpu.VMEM)
+    return pl.pallas_call(
+        align_kernel,
+        in_specs=[vmem],
+        out_specs=vmem,
+        out_shape=jax.ShapeDtypeStruct((height, width), jnp.float32),
+        scratch_shapes=[pltpu.VMEM((width // cols, 2, cols // 2, height), jnp.float32)],
+        compiler_params=params(),
+    )(direct)
+
+
+def combine_kernel(partner_ref, direct_ref, mirror_ref, out_ref):
+    pair_count, own_rows, width = out_ref.shape
+    cols = mirror_ref.shape[2]
+    blocks = width // cols
+    mirror = mirror_ref[...].astype(jnp.float32).reshape(blocks, 2, mirror_ref.shape[1], cols)
+    early, late = mirror[:, 0], mirror[:, 1]
+    front = lax.broadcasted_iota(jnp.int32, early.shape, 2) < cols // 2
+    plain = jnp.where(front, early, swing(late, 2))
+    moved = jnp.where(front, swing(early, 2), late)
     for p in range(pair_count):
         mate = partner_ref[p]
-        odd = lax.rem(mate, 2) == 1
-        same = same_ref[mate // 2].astype(jnp.float32)
-        other = other_ref[mate // 2].astype(jnp.float32)
-        same = jnp.where(odd, same[:, half:], same[:, :half])
-        other = jnp.where(odd, other[:, half:], other[:, :half])
-        first = jnp.where(side == 0, same, other)
-        second = jnp.where(side == 0, other, same)
-        total = kept_ref[p] + jnp.concatenate([first, second], axis=1)
-        for k in range(16):
-            out_ref[k, p * 4 : (p + 1) * 4, :] = total[k * 4 : (k + 1) * 4]
-
-
-def combine_call(partner, kept, same, other):
-    pair_count, rows, cols = kept.shape
-    smem = pl.BlockSpec(memory_space=pltpu.SMEM)
+        chosen = jnp.where(lax.rem(mate, 2) == 1, moved, plain)
+        picked = chosen[:, :own_rows]
+        for k in range(1, pair_count // 2):
+            picked = jnp.where(mate // 2 == k, chosen[:, k * own_rows : (k + 1) * own_rows], picked)
+        for k in range(blocks):
+            span = slice(k * cols, (k + 1) * cols)
+            out_ref[p, :, span] = direct_ref[p * own_rows : (p + 1) * own_rows, span] + picked[k]
+
+
+def combine_call(partner, direct, mirror, pair_count):
+    height, width = direct.shape
     vmem = pl.BlockSpec(memory_space=pltpu.VMEM)
     return pl.pallas_call(
         combine_kernel,
-        in_specs=[smem, vmem, vmem, vmem],
+        in_specs=[pl.BlockSpec(memory_space=pltpu.SMEM), vmem, vmem],
         out_specs=vmem,
-        out_shape=jax.ShapeDtypeStruct((16, pair_count * rows // 16, cols), jnp.float32),
-        compiler_params=params(),
-    )(partner, kept, same, other)
+        out_shape=jax.ShapeDtypeStruct((pair_count, height // pair_count, width), jnp.float32),
+        compiler_params=params(),
+    )(partner, direct, mirror)
 
 
 def turn(count, step):
     return [(i, (i + step) % count) for i in range(count)]
-
-
-def mirror_pairs(other):
-    pairs = []
-    for r in range(16):
-        for c in range(32):
-            side = 1 - c % 2 if other else c % 2
-            pairs.append((r * 32 + c, (c // 2) * 32 + 2 * r + side))
-    return pairs
 
 
 def on_device(amplitudes, factors, amp_mask, out_mask, partner):
@@ -323,14 +386,12 @@
     flat = flat_call(factors, units)
     swapped = lax.ppermute(ladder_call(1, late, flat, units, jnp.bfloat16), "core", turn(2, 1))
     keep = ladder_call(0, late, flat, units, jnp.float32)
-    partial = (keep + swapped.astype(jnp.float32)).astype(jnp.bfloat16)
+    partial = gather_call(keep, swapped, 8)
     pieces = lax.all_to_all(partial, ("zl", "x"), split_axis=0, concat_axis=0)
-    kept, same, other = reduce_call(out_mask, pieces, block_rows)
-    same = lax.ppermute(same, ALL, mirror_pairs(False))
-    other = lax.ppermute(other, ALL, mirror_pairs(True))
-    rows = lax.all_to_all(combine_call(partner, kept, same, other), ROW, split_axis=0, concat_axis=0)
-    rows = rows.reshape(16, pair_count, 4, 128).transpose(1, 2, 0, 3)
-    return rows.reshape(pair_count, 4, full_width)
+    direct, mirror = reduce_call(out_mask, pieces)
+    mirror = lax.all_to_all(mirror.reshape(32, 16, 128), COL, split_axis=0, concat_axis=0)
+    direct = lax.all_to_all(direct.reshape(16, 32, 128), ROW, split_axis=0, concat_axis=0)
+    return combine_call(partner, align_call(direct), mirror, pair_count)
 
 
 def solution(mesh):

time: 186 us -> 183 us (0.984)
  blocking collectives: 70.2 us -> 57.2 us
  waiting for transfers between devices: 33.9 us -> 41 us
  Pallas kernels: 15 us -> 17.7 us
    all_to_all x1, blocking collectives: 24.9 us -> 11.8 us  [on_device(): lax.all_to_all(direct.reshape(16, 32, 128), ROW, split_axis=0, concat_axi...]
    all_to_all x0 -> x1, waiting for transfers between devices: none -> 10.9 us  [on_device(): lax.all_to_all(mirror.reshape(32, 16, 128), COL, split_axis=0, concat_axi...]
    all_to_all x0 -> x1, starting transfers between devices: none -> 6.29 us  [on_device(): lax.all_to_all(mirror.reshape(32, 16, 128), COL, split_axis=0, concat_axi...]
    ppermute x2 -> x0, starting transfers between devices: 5.58 us -> none  [the longest x1 3.66 us: on_device(): other = lax.ppermute(other, ALL, mirror_pairs(True))]
    ppermute x2 -> x0, waiting for transfers between devices: 3.82 us -> none  [the longest x1 2.93 us: on_device(): other = lax.ppermute(other, ALL, mirror_pairs(True))]
    pallas_call x2 -> x4, Pallas kernels: 2.2 us -> 4.81 us  [the longest x1 1.55 us: combine_call(): pl.pallas_call(combine_kernel, in_specs=[pl.BlockSpec(memory_space=pltpu....]
  transfers between devices with their start and end apart: 9 -> 8, of which waited for: 6 -> 5; matrix products, arithmetic and copies ran while one was open for 0% -> 0% of each run, Pallas kernels for 3% -> 3%
where the time goes in v6:
time: 183 us; the launch traced here: 182 us
  blocking collectives  57.2 us (31%)
  starting transfers between devices  52.4 us (29%)
  waiting for transfers between devices  41 us (22%)
  Pallas kernels  17.7 us (10%)
  between operations  13.6 us (7%)
    all_gather x1, blocking collectives, on_device(): lax.all_gather(first, 'zh', axis=0)  23 us
    all_to_all x1, blocking collectives, on_device(): pieces = lax.all_to_all(partial, ('zl', 'x'), split_axis=0, concat_axis=0)  22.3 us
    ppermute x1, starting transfers between devices, on_device(): left = lax.ppermute(back[:4], 'zh', turn(4, 1))  17.7 us
    ppermute x1, waiting for transfers between devices, on_device(): back = lax.ppermute(near, 'zh', turn(4, 1))  15.7 us
    all_to_all x1, blocking collectives, on_device(): lax.all_to_all(direct.reshape(16, 32, 128), ROW, split_axis=0, concat_axi...  11.8 us
    all_to_all x1, waiting for transfers between devices, on_device(): lax.all_to_all(mirror.reshape(32, 16, 128), COL, split_axis=0, concat_axi...  10.9 us
    ppermute x1, waiting for transfers between devices, on_device(): left = lax.ppermute(back[:4], 'zh', turn(4, 1))  9.53 us
    all_to_all x1, starting transfers between devices, on_device(): near = lax.all_to_all(second, 'y', split_axis=0, concat_axis=0)  7.66 us
  transfers between devices with their start and end apart: 8, of which 5 were waited for; matrix products, arithmetic and copies ran while one was open for 0% of the time, Pallas kernels for 3%

profile of v6, /device:TPU:1, one launch (start us, length us, event | category | flops | bytes accessed | tf_op | source)
XLA Modules:
  0.0 181.9 jit_solution(161450860949687478)
XLA Ops:
  6.5 2.7 %shard_map.55 = (bf16[10,64,128]{2,1,0:T(8,128)(2,1)}, bf16[8,6,64,128]{3,2,1,0:T(8,128)(2,1)}) custom-call(s32[16,16]{1,0:T(8,128)} %mask_ref.2, bf16[8,64,128]{2,1,0:T(8,128)(2,1)} %amps_ref.1, bf16[8,64,2048]{2,1,0:T(8,128)(2,1)} %own_ref.5), custom_call_target="tpu_custom_call" | custom-call | tf_op jit(solution)/shard_map/pallas_call | solution.py:62
  9.3 7.7 %all-to-all-start = ((bf16[8,6,64,128]{3,2,1,0:T(8,128)(2,1)}), bf16[8,6,64,128]{3,2,1,0:T(8,128)(2,1)S(1)}, u32[]{:S(2)}, u32[]{:S(2)}) async-start(bf16[8,6,64,128]{3,2,1,0:T(8,128)(2,1)} %get-tuple-element.9), calls=%async_computation | async-start | bytes 1572864 | tf_op jit(solution)/shard_map/all_to_all | solution.py:376
  16.9 0.0 all-gather.4.cloned.1.call-start
  17.0 23.0 %all-gather = bf16[40,64,128]{2,1,0:T(8,128)(2,1)} all-gather(bf16[10,64,128]{2,1,0:T(8,128)(2,1)} %get-tuple-element.10), channel_id=2, replica_groups=mesh['zl'=2,'x'=4,'core'=2,'zh'=4,'y'=8] {'zh'}, dimensions={0}, use_global_device_ids=true | all-gather | bytes 819200 | tf_op jit(solution)/shard_map/all_gather | solution.py:377
  40.0 0.0 all-to-all-done.near_ref.other_ref
  40.0 0.0 copy-start
  40.0 0.0 all-gather.4.cloned.1.call-update
  40.0 6.4 %collective-permute-start = (bf16[8,6,64,128]{3,2,1,0:T(8,128)(2,1)S(1)}, bf16[8,6,64,128]{3,2,1,0:T(8,128)(2,1)S(1)}, u32[]{:S(2)}, u32[]{:S(2)}) collective-permute-start(bf16[8,6,64,128]{3,2,1,0:T(8,128)(2,1)S(1)} %all-to-all-done.near_ref.other_ref), channel_id=1, source_target_pairs={{0,8},{8,16},{16,24},{24,0},{1,9},{9,17},{17,25},{25,1},{2,10},{10... | collective-permute-start | bytes 2359304 | tf_op jit(solution)/shard_map/ppermute | solution.py:379
  46.5 6.8 %collective-permute-start.2 = (bf16[8,6,64,128]{3,2,1,0:T(8,128)(2,1)S(1)}, bf16[8,6,64,128]{3,2,1,0:T(8,128)(2,1)S(1)}, u32[]{:S(2)}, u32[]{:S(2)}) collective-permute-start(bf16[8,6,64,128]{3,2,1,0:T(8,128)(2,1)S(1)} %all-to-all-done.near_ref.other_ref), channel_id=1, source_target_pairs={{0,24},{8,0},{16,8},{24,16},{1,25},{9,1},{17,9},{25,17},{2,26},{10... | collective-permute-start | bytes 2359304 | tf_op jit(solution)/shard_map/ppermute | solution.py:380
  53.3 15.7 %collective-permute-done.back_ref = bf16[8,6,64,128]{3,2,1,0:T(8,128)(2,1)S(1)} collective-permute-done((bf16[8,6,64,128]{3,2,1,0:T(8,128)(2,1)S(1)}, bf16[8,6,64,128]{3,2,1,0:T(8,128)(2,1)S(1)}, u32[]{:S(2)}, u32[]{:S(2)}) %collective-permute-start) | collective-permute-done | bytes 786464 | tf_op jit(solution)/shard_map/ppermute | solution.py:379
  69.0 17.7 %collective-permute-start.1 = (bf16[4,6,64,128]{3,2,1,0:T(8,128)(2,1)S(1)}, bf16[4,6,64,128]{3,2,1,0:T(8,128)(2,1)S(1)}, u32[]{:S(2)}, u32[]{:S(2)}) collective-permute-start(bf16[4,6,64,128]{3,2,1,0:T(8,128)(2,1)S(1)} %slice.8), channel_id=1, source_target_pairs={{0,8},{8,16},{16,24},{24,0},{1,9},{9,17},{17,25},{25,1},{2,10},{10... | collective-permute-start | bytes 1179656 | tf_op jit(solution)/shard_map/ppermute | solution.py:381
  86.7 0.0 collective-permute-done.2.ahead_ref
  86.8 4.9 %collective-permute-start.3 = (bf16[4,6,64,128]{3,2,1,0:T(8,128)(2,1)S(1)}, bf16[4,6,64,128]{3,2,1,0:T(8,128)(2,1)S(1)}, u32[]{:S(2)}, u32[]{:S(2)}) collective-permute-start(bf16[4,6,64,128]{3,2,1,0:T(8,128)(2,1)S(1)} %slice.9), channel_id=1, source_target_pairs={{0,24},{8,0},{16,8},{24,16},{1,25},{9,1},{17,9},{25,17},{2,26},{10... | collective-permute-start | bytes 1179656 | tf_op jit(solution)/shard_map/ppermute | solution.py:382
  91.7 0.0 copy-done
  91.7 2.0 %shard_map.56.early_ref = f32[512,768]{1,0:T(8,128)S(1)} custom-call(bf16[8,64,2048]{2,1,0:T(8,128)(2,1)S(1)} %copy-done, bf16[8,6,64,128]{3,2,1,0:T(8,128)(2,1)S(1)} %all-to-all-done.near_ref.other_ref, bf16[8,6,64,128]{3,2,1,0:T(8,128)(2,1)S(1)} %collective-permute-done.back_ref, bf16[8,6,64,128]{3,2,1,0:T(8,128)(2,1)S(1)} %collective-permute-done.2.ahead_ref), custom_call_target="tpu_custom_call" | custom-call | tf_op jit(solution)/shard_map/pallas_call | solution.py:127
  93.8 9.5 %collective-permute-done.1.left_ref = bf16[4,6,64,128]{3,2,1,0:T(8,128)(2,1)S(1)} collective-permute-done((bf16[4,6,64,128]{3,2,1,0:T(8,128)(2,1)S(1)}, bf16[4,6,64,128]{3,2,1,0:T(8,128)(2,1)S(1)}, u32[]{:S(2)}, u32[]{:S(2)}) %collective-permute-start.1) | collective-permute-done | bytes 393248 | tf_op jit(solution)/shard_map/ppermute | solution.py:381
  103.3 1.3 collective-permute-done.3.right_ref
  104.6 0.7 shard_map.57.ring_ref
  105.3 3.5 %all-gather.4.cloned.1.call-done = bf16[32,10,64,128]{3,2,1,0:T(8,128)(2,1)} async-done(((bf16[4,10,64,128]{3,2,1,0:T(8,128)(2,1)}), bf16[32,10,64,128]{3,2,1,0:T(8,128)(2,1)}) %all-gather.4.cloned.1.call-update) | async-done | bytes 5242896 | tf_op jit(solution)/shard_map/all_gather | solution.py:377
  108.8 2.0 %shard_map.59.flat_ref = bf16[1024,128]{1,0:T(8,128)(2,1)S(1)} custom-call(bf16[8,64,2048]{2,1,0:T(8,128)(2,1)S(1)} %copy-done, bf16[8,4,10,64,128]{4,3,2,1,0:T(8,128)(2,1)} %bitcast.5), custom_call_target="tpu_custom_call" | custom-call | tf_op jit(solution)/shard_map/pallas_call | solution.py:179
  110.8 2.7 %shard_map.61 = bf16[1024,512]{1,0:T(8,128)(2,1)S(1)} custom-call(bf16[1024,384]{1,0:T(8,128)(2,1)S(1)} %shard_map.57.ring_ref, bf16[1024,128]{1,0:T(8,128)(2,1)S(1)} %shard_map.59.flat_ref, bf16[8,4,10,64,128]{4,3,2,1,0:T(8,128)(2,1)} %bitcast.6), custom_call_target="tpu_custom_call" | custom-call | tf_op jit(solution)/shard_map/pallas_call | solution.py:218
  113.5 2.6 %collective-permute-start.4 = (bf16[1024,512]{1,0:T(8,128)(2,1)S(1)}, bf16[1024,512]{1,0:T(8,128)(2,1)S(1)}, u32[]{:S(2)}, u32[]{:S(2)}) collective-permute-start(bf16[1024,512]{1,0:T(8,128)(2,1)S(1)} %shard_map.61), channel_id=1, source_target_pairs={{0,32},{32,0},{1,33},{33,1},{2,34},{34,2},{3,35},{35,3},{4,36},{36... | collective-permute-start | bytes 3145736 | tf_op jit(solution)/shard_map/ppermute | solution.py:387
  116.1 2.7 %shard_map.60.keep_ref = f32[1024,512]{1,0:T(8,128)S(1)} custom-call(bf16[1024,384]{1,0:T(8,128)(2,1)S(1)} %shard_map.57.ring_ref, bf16[1024,128]{1,0:T(8,128)(2,1)S(1)} %shard_map.59.flat_ref, bf16[8,4,10,64,128]{4,3,2,1,0:T(8,128)(2,1)} %bitcast.7), custom_call_target="tpu_custom_call" | custom-call | tf_op jit(solution)/shard_map/pallas_call | solution.py:218
  118.8 0.0 collective-permute-done.4.other_ref
  118.8 1.1 shard_map.62
  119.9 0.0 copy-start.1
  119.9 0.0 copy-start.2
  119.9 22.3 %all_to_all.20.part_ref = bf16[8,128,512]{2,1,0:T(8,128)(2,1)S(1)} all-to-all(bf16[8,128,512]{2,1,0:T(8,128)(2,1)S(1)} %shard_map.62), channel_id=1, replica_groups=mesh['zl'=2,'x'=4,'core'=2,'zh'=4,'y'=8] {'zl','x'}, dimensions={0} | all-to-all | bytes 2097152 | tf_op jit(solution)/shard_map/all_to_all | solution.py:390
  142.3 0.0 copy-done.1
  142.3 1.5 shard_map.63
  143.8 11.8 %all_to_all.21.direct_ref = f32[16,32,128]{2,1,0:T(8,128)S(1)} all-to-all(f32[16,32,128]{2,1,0:T(8,128)S(1)} %bitcast.4), channel_id=1, replica_groups=mesh['zl'=2,'x'=4,'core'=2,'zh'=4,'y'=8] {'zl','x','core'}, dimensions={0} | all-to-all | bytes 524288 | tf_op jit(solution)/shard_map/all_to_all | solution.py:393
  155.6 6.3 %all-to-all-start.3 = ((bf16[32,16,128]{2,1,0:T(8,128)(2,1)}), bf16[32,16,128]{2,1,0:T(8,128)(2,1)S(1)}, u32[]{:S(2)}, u32[]{:S(2)}) async-start(bf16[32,16,128]{2,1,0:T(8,128)(2,1)} %bitcast.3), calls=%async_computation.3 | async-start | bytes 262144 | tf_op jit(solution)/shard_map/all_to_all | solution.py:392
  161.9 0.7 shard_map.64.direct_ref
  162.6 10.9 %all-to-all-done.3.mirror_ref = bf16[32,16,128]{2,1,0:T(8,128)(2,1)S(1)} async-done(((bf16[32,16,128]{2,1,0:T(8,128)(2,1)}), bf16[32,16,128]{2,1,0:T(8,128)(2,1)S(1)}, u32[]{:S(2)}, u32[]{:S(2)}) %all-to-all-start.3) | async-done | bytes 131104 | tf_op jit(solution)/shard_map/all_to_all | solution.py:392
  173.5 0.0 copy-done.2
  173.5 1.6 shard_map.65
  (3 shorter events, 0.1 us)
Async XLA Ops:
  9.3 30.7 %all-to-all-start = ((bf16[8,6,64,128]{3,2,1,0:T(8,128)(2,1)}), bf16[8,6,64,128]{3,2,1,0:T(8,128)(2,1)S(1)}, u32[]{:S(2)}, u32[]{:S(2)}) async-start(bf16[8,6,64,128]{3,2,1,0:T(8,128)(2,1)} %get-tuple-element.9), calls=%async_computation | async-start | bytes 1572864 | tf_op jit(solution)/shard_map/all_to_all | solution.py:376
  16.9 91.9 %all-gather.4.cloned.1.call-start = ((), (), s32[]{:S(2)}) async-start(), calls=%async_computation.4 | async-start | bytes 5898240 | tf_op jit(solution)/shard_map/all_gather | solution.py:377
  40.0 51.7 %copy-start = (bf16[8,64,2048]{2,1,0:T(8,128)(2,1)S(1)}, bf16[8,64,2048]{2,1,0:T(8,128)(2,1)}, u32[]{:S(2)}) copy-start(bf16[8,64,2048]{2,1,0:T(8,128)(2,1)} %own_ref.5) | copy-start | bytes 6291460
  40.0 29.0 %collective-permute-start = (bf16[8,6,64,128]{3,2,1,0:T(8,128)(2,1)S(1)}, bf16[8,6,64,128]{3,2,1,0:T(8,128)(2,1)S(1)}, u32[]{:S(2)}, u32[]{:S(2)}) collective-permute-start(bf16[8,6,64,128]{3,2,1,0:T(8,128)(2,1)S(1)} %all-to-all-done.near_ref.other_ref), channel_id=1, source_target_pairs={{0,8},{8,16},{16,24},{24,0},{1,9},{9,17},{17,25},{25,1},{2,10},{10... | collective-permute-start | bytes 2359304 | tf_op jit(solution)/shard_map/ppermute | solution.py:379
  46.5 40.3 %collective-permute-start.2 = (bf16[8,6,64,128]{3,2,1,0:T(8,128)(2,1)S(1)}, bf16[8,6,64,128]{3,2,1,0:T(8,128)(2,1)S(1)}, u32[]{:S(2)}, u32[]{:S(2)}) collective-permute-start(bf16[8,6,64,128]{3,2,1,0:T(8,128)(2,1)S(1)} %all-to-all-done.near_ref.other_ref), channel_id=1, source_target_pairs={{0,24},{8,0},{16,8},{24,16},{1,25},{9,1},{17,9},{25,17},{2,26},{10... | collective-permute-start | bytes 2359304 | tf_op jit(solution)/shard_map/ppermute | solution.py:380
  69.0 34.3 %collective-permute-start.1 = (bf16[4,6,64,128]{3,2,1,0:T(8,128)(2,1)S(1)}, bf16[4,6,64,128]{3,2,1,0:T(8,128)(2,1)S(1)}, u32[]{:S(2)}, u32[]{:S(2)}) collective-permute-start(bf16[4,6,64,128]{3,2,1,0:T(8,128)(2,1)S(1)} %slice.8), channel_id=1, source_target_pairs={{0,8},{8,16},{16,24},{24,0},{1,9},{9,17},{17,25},{25,1},{2,10},{10... | collective-permute-start | bytes 1179656 | tf_op jit(solution)/shard_map/ppermute | solution.py:381
  86.8 17.8 %collective-permute-start.3 = (bf16[4,6,64,128]{3,2,1,0:T(8,128)(2,1)S(1)}, bf16[4,6,64,128]{3,2,1,0:T(8,128)(2,1)S(1)}, u32[]{:S(2)}, u32[]{:S(2)}) collective-permute-start(bf16[4,6,64,128]{3,2,1,0:T(8,128)(2,1)S(1)} %slice.9), channel_id=1, source_target_pairs={{0,24},{8,0},{16,8},{24,16},{1,25},{9,1},{17,9},{25,17},{2,26},{10... | collective-permute-start | bytes 1179656 | tf_op jit(solution)/shard_map/ppermute | solution.py:382
  113.5 5.3 %collective-permute-start.4 = (bf16[1024,512]{1,0:T(8,128)(2,1)S(1)}, bf16[1024,512]{1,0:T(8,128)(2,1)S(1)}, u32[]{:S(2)}, u32[]{:S(2)}) collective-permute-start(bf16[1024,512]{1,0:T(8,128)(2,1)S(1)} %shard_map.61), channel_id=1, source_target_pairs={{0,32},{32,0},{1,33},{33,1},{2,34},{34,2},{3,35},{35,3},{4,36},{36... | collective-permute-start | bytes 3145736 | tf_op jit(solution)/shard_map/ppermute | solution.py:387
  119.9 22.4 %copy-start.1 = (s32[16,16]{1,0:T(8,128)S(1)}, s32[16,16]{1,0:T(8,128)}, u32[]{:S(2)}) copy-start(s32[16,16]{1,0:T(8,128)} %mask_ref.3) | copy-start | bytes 3076
  119.9 53.6 %copy-start.2 = (s32[8]{0:T(128)S(1)}, s32[8]{0:T(128)}, u32[]{:S(2)}) copy-start(s32[8]{0:T(128)} %partner_ref.1) | copy-start | bytes 100
  155.6 17.9 %all-to-all-start.3 = ((bf16[32,16,128]{2,1,0:T(8,128)(2,1)}), bf16[32,16,128]{2,1,0:T(8,128)(2,1)S(1)}, u32[]{:S(2)}, u32[]{:S(2)}) async-start(bf16[32,16,128]{2,1,0:T(8,128)(2,1)} %bitcast.3), calls=%async_computation.3 | async-start | bytes 262144 | tf_op jit(solution)/shard_map/all_to_all | solution.py:392
Sparse Core Ops, SparseCore 0:
  40.2 68.6 all-gather.3

commit v7 on v6

--- a/solution.py
+++ b/solution.py
@@ -116,9 +116,10 @@
 
 
 def early_kernel(own_ref, near_ref, back_ref, ahead_ref, out_ref):
+    step = 1 + 2 * lax.axis_index("zl")
     product = ring_term(own_ref, [near_ref], 0)
-    product = product + ring_term(own_ref, [back_ref], 3)
-    out_ref[...] = product + ring_term(own_ref, [ahead_ref], 1)
+    product = product + ring_term(own_ref, [back_ref], 4 - step)
+    out_ref[...] = product + ring_term(own_ref, [ahead_ref], step)
 
 
 def early_call(own, parts):
@@ -368,6 +369,10 @@
     return [(i, (i + step) % count) for i in range(count)]
 
 
+def cross(step):
+    return [(k, k // 4 * 4 + (k % 4 + (1 - k // 4 * 2) * step) % 4) for k in range(8)]
+
+
 def on_device(amplitudes, factors, amp_mask, out_mask, partner):
     pair_count, amp_rows, amp_cols = amplitudes.shape
     batch_count, block_rows, full_width = factors.shape
@@ -376,10 +381,10 @@
     near = lax.all_to_all(second, "y", split_axis=0, concat_axis=0)
     units = lax.all_gather(gate_call(lax.all_gather(first, "zh", axis=0), near), "y", axis=0)
 
-    back = lax.ppermute(near, "zh", turn(4, 1))
-    ahead = lax.ppermute(near, "zh", turn(4, -1))
-    left = lax.ppermute(back[:4], "zh", turn(4, 1))
-    right = lax.ppermute(ahead[4:], "zh", turn(4, -1))
+    back = lax.ppermute(near, ("zl", "zh"), cross(1))
+    ahead = lax.ppermute(near, ("zl", "zh"), cross(-1))
+    left = lax.ppermute(back[:4], ("zl", "zh"), cross(1))
+    right = lax.ppermute(ahead[4:], ("zl", "zh"), cross(-1))
 
     early = early_call(factors, (near, back, ahead))
     late = late_call(factors, (left, right), early)

time: 183 us -> 183 us (level)
  blocking collectives: 57.2 us -> 54.2 us
  starting transfers between devices: 52.4 us -> 55.3 us
    ppermute x4, waiting for transfers between devices: 26.6 us -> 29.9 us  [the longest x1 15.8 us: on_device(): back = lax.ppermute(near, ('zl', 'zh'), cross(1))]
    all_gather x1, waiting for transfers between devices: 3.53 us -> 0.19 us  [on_device(): lax.all_gather(gate_call(lax.all_gather(first, 'zh', axis=0), near), 'y',...]
    all_to_all x1, blocking collectives: 22.3 us -> 19.4 us  [on_device(): pieces = lax.all_to_all(partial, ('zl', 'x'), split_axis=0, concat_axis=0)]
    all_to_all x1, starting transfers between devices: 6.29 us -> 9.22 us  [on_device(): lax.all_to_all(mirror.reshape(32, 16, 128), COL, split_axis=0, concat_axi...]
where the time goes in v7:
time: 183 us; the launch traced here: 182 us
  starting transfers between devices  55.3 us (30%)
  blocking collectives  54.2 us (30%)
  waiting for transfers between devices  41.1 us (22%)
  Pallas kernels  17.7 us (10%)
  between operations  13.6 us (7%)
    all_gather x1, blocking collectives, on_device(): lax.all_gather(first, 'zh', axis=0)  23 us
    all_to_all x1, blocking collectives, on_device(): pieces = lax.all_to_all(partial, ('zl', 'x'), split_axis=0, concat_axis=0)  19.4 us
    ppermute x1, starting transfers between devices, on_device(): left = lax.ppermute(back[:4], ('zl', 'zh'), cross(1))  17.7 us
    ppermute x1, waiting for transfers between devices, on_device(): back = lax.ppermute(near, ('zl', 'zh'), cross(1))  15.8 us
    all_to_all x1, blocking collectives, on_device(): lax.all_to_all(direct.reshape(16, 32, 128), ROW, split_axis=0, concat_axi...  11.8 us
    all_to_all x1, waiting for transfers between devices, on_device(): lax.all_to_all(mirror.reshape(32, 16, 128), COL, split_axis=0, concat_axi...  10.9 us
    ppermute x1, waiting for transfers between devices, on_device(): right = lax.ppermute(ahead[4:], ('zl', 'zh'), cross(-1))  9.91 us
    all_to_all x1, starting transfers between devices, on_device(): lax.all_to_all(mirror.reshape(32, 16, 128), COL, split_axis=0, concat_axi...  9.22 us
  transfers between devices with their start and end apart: 8, of which 5 were waited for; matrix products, arithmetic and copies ran while one was open for 0% of the time, Pallas kernels for 3%

profile of v7, /device:TPU:1, one launch (start us, length us, event | category | flops | bytes accessed | tf_op | source)
XLA Modules:
  0.0 181.9 jit_solution(14894423703165006555)
XLA Ops:
  6.5 2.7 %shard_map.55 = (bf16[10,64,128]{2,1,0:T(8,128)(2,1)}, bf16[8,6,64,128]{3,2,1,0:T(8,128)(2,1)}) custom-call(s32[16,16]{1,0:T(8,128)} %mask_ref.2, bf16[8,64,128]{2,1,0:T(8,128)(2,1)} %amps_ref.1, bf16[8,64,2048]{2,1,0:T(8,128)(2,1)} %own_ref.5), custom_call_target="tpu_custom_call" | custom-call | tf_op jit(solution)/shard_map/pallas_call | solution.py:62
  9.3 7.7 %all-to-all-start = ((bf16[8,6,64,128]{3,2,1,0:T(8,128)(2,1)}), bf16[8,6,64,128]{3,2,1,0:T(8,128)(2,1)S(1)}, u32[]{:S(2)}, u32[]{:S(2)}) async-start(bf16[8,6,64,128]{3,2,1,0:T(8,128)(2,1)} %get-tuple-element.9), calls=%async_computation | async-start | bytes 1572864 | tf_op jit(solution)/shard_map/all_to_all | solution.py:381
  16.9 0.0 all-gather.4.cloned.1.call-start
  17.0 23.0 %all-gather = bf16[40,64,128]{2,1,0:T(8,128)(2,1)} all-gather(bf16[10,64,128]{2,1,0:T(8,128)(2,1)} %get-tuple-element.10), channel_id=2, replica_groups=mesh['zl'=2,'x'=4,'core'=2,'zh'=4,'y'=8] {'zh'}, dimensions={0}, use_global_device_ids=true | all-gather | bytes 819200 | tf_op jit(solution)/shard_map/all_gather | solution.py:382
  40.0 0.0 all-to-all-done.near_ref.other_ref
  40.0 0.0 copy-start
  40.0 0.0 all-gather.4.cloned.1.call-update
  40.0 6.4 %collective-permute-start = (bf16[8,6,64,128]{3,2,1,0:T(8,128)(2,1)S(1)}, bf16[8,6,64,128]{3,2,1,0:T(8,128)(2,1)S(1)}, u32[]{:S(2)}, u32[]{:S(2)}) collective-permute-start(bf16[8,6,64,128]{3,2,1,0:T(8,128)(2,1)S(1)} %all-to-all-done.near_ref.other_ref), channel_id=1, source_target_pairs={{0,8},{8,16},{16,24},{24,0},{256,280},{264,256},{272,264},{280,272... | collective-permute-start | bytes 2359304 | tf_op jit(solution)/shard_map/ppermute | solution.py:384
  46.5 6.8 %collective-permute-start.2 = (bf16[8,6,64,128]{3,2,1,0:T(8,128)(2,1)S(1)}, bf16[8,6,64,128]{3,2,1,0:T(8,128)(2,1)S(1)}, u32[]{:S(2)}, u32[]{:S(2)}) collective-permute-start(bf16[8,6,64,128]{3,2,1,0:T(8,128)(2,1)S(1)} %all-to-all-done.near_ref.other_ref), channel_id=1, source_target_pairs={{0,24},{8,0},{16,8},{24,16},{256,264},{264,272},{272,280},{280,256... | collective-permute-start | bytes 2359304 | tf_op jit(solution)/shard_map/ppermute | solution.py:385
  53.3 15.8 %collective-permute-done.back_ref = bf16[8,6,64,128]{3,2,1,0:T(8,128)(2,1)S(1)} collective-permute-done((bf16[8,6,64,128]{3,2,1,0:T(8,128)(2,1)S(1)}, bf16[8,6,64,128]{3,2,1,0:T(8,128)(2,1)S(1)}, u32[]{:S(2)}, u32[]{:S(2)}) %collective-permute-start) | collective-permute-done | bytes 786464 | tf_op jit(solution)/shard_map/ppermute | solution.py:384
  69.1 17.7 %collective-permute-start.1 = (bf16[4,6,64,128]{3,2,1,0:T(8,128)(2,1)S(1)}, bf16[4,6,64,128]{3,2,1,0:T(8,128)(2,1)S(1)}, u32[]{:S(2)}, u32[]{:S(2)}) collective-permute-start(bf16[4,6,64,128]{3,2,1,0:T(8,128)(2,1)S(1)} %slice.8), channel_id=1, source_target_pairs={{0,8},{8,16},{16,24},{24,0},{256,280},{264,256},{272,264},{280,272... | collective-permute-start | bytes 1179656 | tf_op jit(solution)/shard_map/ppermute | solution.py:386
  86.8 0.0 collective-permute-done.2.ahead_ref
  86.9 4.8 %collective-permute-start.3 = (bf16[4,6,64,128]{3,2,1,0:T(8,128)(2,1)S(1)}, bf16[4,6,64,128]{3,2,1,0:T(8,128)(2,1)S(1)}, u32[]{:S(2)}, u32[]{:S(2)}) collective-permute-start(bf16[4,6,64,128]{3,2,1,0:T(8,128)(2,1)S(1)} %slice.9), channel_id=1, source_target_pairs={{0,24},{8,0},{16,8},{24,16},{256,264},{264,272},{272,280},{280,256... | collective-permute-start | bytes 1179656 | tf_op jit(solution)/shard_map/ppermute | solution.py:387
  91.7 0.0 copy-done
  91.7 2.0 %shard_map.56.early_ref = f32[512,768]{1,0:T(8,128)S(1)} custom-call(bf16[8,64,2048]{2,1,0:T(8,128)(2,1)S(1)} %copy-done, bf16[8,6,64,128]{3,2,1,0:T(8,128)(2,1)S(1)} %all-to-all-done.near_ref.other_ref, bf16[8,6,64,128]{3,2,1,0:T(8,128)(2,1)S(1)} %collective-permute-done.back_ref, bf16[8,6,64,128]{3,2,1,0:T(8,128)(2,1)S(1)} %collective-permute-done.2.ahead_ref), custom_call_target="tpu_custom_call" | custom-call | tf_op jit(solution)/shard_map/pallas_call | solution.py:128
  93.8 4.2 %collective-permute-done.1.left_ref = bf16[4,6,64,128]{3,2,1,0:T(8,128)(2,1)S(1)} collective-permute-done((bf16[4,6,64,128]{3,2,1,0:T(8,128)(2,1)S(1)}, bf16[4,6,64,128]{3,2,1,0:T(8,128)(2,1)S(1)}, u32[]{:S(2)}, u32[]{:S(2)}) %collective-permute-start.1) | collective-permute-done | bytes 393248 | tf_op jit(solution)/shard_map/ppermute | solution.py:386
  98.0 9.9 %collective-permute-done.3.right_ref = bf16[4,6,64,128]{3,2,1,0:T(8,128)(2,1)S(1)} collective-permute-done((bf16[4,6,64,128]{3,2,1,0:T(8,128)(2,1)S(1)}, bf16[4,6,64,128]{3,2,1,0:T(8,128)(2,1)S(1)}, u32[]{:S(2)}, u32[]{:S(2)}) %collective-permute-start.3) | collective-permute-done | bytes 393248 | tf_op jit(solution)/shard_map/ppermute | solution.py:387
  107.9 0.7 shard_map.57.ring_ref
  108.6 0.2 all-gather.4.cloned.1.call-done
  108.8 2.0 %shard_map.59.flat_ref = bf16[1024,128]{1,0:T(8,128)(2,1)S(1)} custom-call(bf16[8,64,2048]{2,1,0:T(8,128)(2,1)S(1)} %copy-done, bf16[8,4,10,64,128]{4,3,2,1,0:T(8,128)(2,1)} %bitcast.5), custom_call_target="tpu_custom_call" | custom-call | tf_op jit(solution)/shard_map/pallas_call | solution.py:180
  110.8 2.7 %shard_map.61 = bf16[1024,512]{1,0:T(8,128)(2,1)S(1)} custom-call(bf16[1024,384]{1,0:T(8,128)(2,1)S(1)} %shard_map.57.ring_ref, bf16[1024,128]{1,0:T(8,128)(2,1)S(1)} %shard_map.59.flat_ref, bf16[8,4,10,64,128]{4,3,2,1,0:T(8,128)(2,1)} %bitcast.6), custom_call_target="tpu_custom_call" | custom-call | tf_op jit(solution)/shard_map/pallas_call | solution.py:219
  113.5 2.6 %collective-permute-start.4 = (bf16[1024,512]{1,0:T(8,128)(2,1)S(1)}, bf16[1024,512]{1,0:T(8,128)(2,1)S(1)}, u32[]{:S(2)}, u32[]{:S(2)}) collective-permute-start(bf16[1024,512]{1,0:T(8,128)(2,1)S(1)} %shard_map.61), channel_id=1, source_target_pairs={{0,32},{32,0},{1,33},{33,1},{2,34},{34,2},{3,35},{35,3},{4,36},{36... | collective-permute-start | bytes 3145736 | tf_op jit(solution)/shard_map/ppermute | solution.py:392
  116.1 2.7 %shard_map.60.keep_ref = f32[1024,512]{1,0:T(8,128)S(1)} custom-call(bf16[1024,384]{1,0:T(8,128)(2,1)S(1)} %shard_map.57.ring_ref, bf16[1024,128]{1,0:T(8,128)(2,1)S(1)} %shard_map.59.flat_ref, bf16[8,4,10,64,128]{4,3,2,1,0:T(8,128)(2,1)} %bitcast.7), custom_call_target="tpu_custom_call" | custom-call | tf_op jit(solution)/shard_map/pallas_call | solution.py:219
  118.8 0.0 collective-permute-done.4.other_ref
  118.8 1.1 shard_map.62
  119.9 0.0 copy-start.1
  119.9 0.0 copy-start.2
  119.9 19.4 %all_to_all.20.part_ref = bf16[8,128,512]{2,1,0:T(8,128)(2,1)S(1)} all-to-all(bf16[8,128,512]{2,1,0:T(8,128)(2,1)S(1)} %shard_map.62), channel_id=1, replica_groups=mesh['zl'=2,'x'=4,'core'=2,'zh'=4,'y'=8] {'zl','x'}, dimensions={0} | all-to-all | bytes 2097152 | tf_op jit(solution)/shard_map/all_to_all | solution.py:395
  139.3 0.0 copy-done.1
  139.3 1.5 shard_map.63
  140.9 11.8 %all_to_all.21.direct_ref = f32[16,32,128]{2,1,0:T(8,128)S(1)} all-to-all(f32[16,32,128]{2,1,0:T(8,128)S(1)} %bitcast.4), channel_id=1, replica_groups=mesh['zl'=2,'x'=4,'core'=2,'zh'=4,'y'=8] {'zl','x','core'}, dimensions={0} | all-to-all | bytes 524288 | tf_op jit(solution)/shard_map/all_to_all | solution.py:398
  152.7 9.2 %all-to-all-start.3 = ((bf16[32,16,128]{2,1,0:T(8,128)(2,1)}), bf16[32,16,128]{2,1,0:T(8,128)(2,1)S(1)}, u32[]{:S(2)}, u32[]{:S(2)}) async-start(bf16[32,16,128]{2,1,0:T(8,128)(2,1)} %bitcast.3), calls=%async_computation.3 | async-start | bytes 262144 | tf_op jit(solution)/shard_map/all_to_all | solution.py:397
  161.9 0.7 shard_map.64.direct_ref
  162.6 10.9 %all-to-all-done.3.mirror_ref = bf16[32,16,128]{2,1,0:T(8,128)(2,1)S(1)} async-done(((bf16[32,16,128]{2,1,0:T(8,128)(2,1)}), bf16[32,16,128]{2,1,0:T(8,128)(2,1)S(1)}, u32[]{:S(2)}, u32[]{:S(2)}) %all-to-all-start.3) | async-done | bytes 131104 | tf_op jit(solution)/shard_map/all_to_all | solution.py:397
  173.5 0.0 copy-done.2
  173.5 1.6 shard_map.65
  (3 shorter events, 0.1 us)
Async XLA Ops:
  9.3 30.7 %all-to-all-start = ((bf16[8,6,64,128]{3,2,1,0:T(8,128)(2,1)}), bf16[8,6,64,128]{3,2,1,0:T(8,128)(2,1)S(1)}, u32[]{:S(2)}, u32[]{:S(2)}) async-start(bf16[8,6,64,128]{3,2,1,0:T(8,128)(2,1)} %get-tuple-element.9), calls=%async_computation | async-start | bytes 1572864 | tf_op jit(solution)/shard_map/all_to_all | solution.py:381
  16.9 91.9 %all-gather.4.cloned.1.call-start = ((), (), s32[]{:S(2)}) async-start(), calls=%async_computation.4 | async-start | bytes 5898240 | tf_op jit(solution)/shard_map/all_gather | solution.py:382
  40.0 51.7 %copy-start = (bf16[8,64,2048]{2,1,0:T(8,128)(2,1)S(1)}, bf16[8,64,2048]{2,1,0:T(8,128)(2,1)}, u32[]{:S(2)}) copy-start(bf16[8,64,2048]{2,1,0:T(8,128)(2,1)} %own_ref.5) | copy-start | bytes 6291460
  40.0 29.0 %collective-permute-start = (bf16[8,6,64,128]{3,2,1,0:T(8,128)(2,1)S(1)}, bf16[8,6,64,128]{3,2,1,0:T(8,128)(2,1)S(1)}, u32[]{:S(2)}, u32[]{:S(2)}) collective-permute-start(bf16[8,6,64,128]{3,2,1,0:T(8,128)(2,1)S(1)} %all-to-all-done.near_ref.other_ref), channel_id=1, source_target_pairs={{0,8},{8,16},{16,24},{24,0},{256,280},{264,256},{272,264},{280,272... | collective-permute-start | bytes 2359304 | tf_op jit(solution)/shard_map/ppermute | solution.py:384
  46.5 40.3 %collective-permute-start.2 = (bf16[8,6,64,128]{3,2,1,0:T(8,128)(2,1)S(1)}, bf16[8,6,64,128]{3,2,1,0:T(8,128)(2,1)S(1)}, u32[]{:S(2)}, u32[]{:S(2)}) collective-permute-start(bf16[8,6,64,128]{3,2,1,0:T(8,128)(2,1)S(1)} %all-to-all-done.near_ref.other_ref), channel_id=1, source_target_pairs={{0,24},{8,0},{16,8},{24,16},{256,264},{264,272},{272,280},{280,256... | collective-permute-start | bytes 2359304 | tf_op jit(solution)/shard_map/ppermute | solution.py:385
  69.1 28.9 %collective-permute-start.1 = (bf16[4,6,64,128]{3,2,1,0:T(8,128)(2,1)S(1)}, bf16[4,6,64,128]{3,2,1,0:T(8,128)(2,1)S(1)}, u32[]{:S(2)}, u32[]{:S(2)}) collective-permute-start(bf16[4,6,64,128]{3,2,1,0:T(8,128)(2,1)S(1)} %slice.8), channel_id=1, source_target_pairs={{0,8},{8,16},{16,24},{24,0},{256,280},{264,256},{272,264},{280,272... | collective-permute-start | bytes 1179656 | tf_op jit(solution)/shard_map/ppermute | solution.py:386
  86.9 21.1 %collective-permute-start.3 = (bf16[4,6,64,128]{3,2,1,0:T(8,128)(2,1)S(1)}, bf16[4,6,64,128]{3,2,1,0:T(8,128)(2,1)S(1)}, u32[]{:S(2)}, u32[]{:S(2)}) collective-permute-start(bf16[4,6,64,128]{3,2,1,0:T(8,128)(2,1)S(1)} %slice.9), channel_id=1, source_target_pairs={{0,24},{8,0},{16,8},{24,16},{256,264},{264,272},{272,280},{280,256... | collective-permute-start | bytes 1179656 | tf_op jit(solution)/shard_map/ppermute | solution.py:387
  113.5 5.3 %collective-permute-start.4 = (bf16[1024,512]{1,0:T(8,128)(2,1)S(1)}, bf16[1024,512]{1,0:T(8,128)(2,1)S(1)}, u32[]{:S(2)}, u32[]{:S(2)}) collective-permute-start(bf16[1024,512]{1,0:T(8,128)(2,1)S(1)} %shard_map.61), channel_id=1, source_target_pairs={{0,32},{32,0},{1,33},{33,1},{2,34},{34,2},{3,35},{35,3},{4,36},{36... | collective-permute-start | bytes 3145736 | tf_op jit(solution)/shard_map/ppermute | solution.py:392
  119.9 19.4 %copy-start.1 = (s32[16,16]{1,0:T(8,128)S(1)}, s32[16,16]{1,0:T(8,128)}, u32[]{:S(2)}) copy-start(s32[16,16]{1,0:T(8,128)} %mask_ref.3) | copy-start | bytes 3076
  119.9 53.6 %copy-start.2 = (s32[8]{0:T(128)S(1)}, s32[8]{0:T(128)}, u32[]{:S(2)}) copy-start(s32[8]{0:T(128)} %partner_ref.1) | copy-start | bytes 100
  152.7 20.8 %all-to-all-start.3 = ((bf16[32,16,128]{2,1,0:T(8,128)(2,1)}), bf16[32,16,128]{2,1,0:T(8,128)(2,1)S(1)}, u32[]{:S(2)}, u32[]{:S(2)}) async-start(bf16[32,16,128]{2,1,0:T(8,128)(2,1)} %bitcast.3), calls=%async_computation.3 | async-start | bytes 262144 | tf_op jit(solution)/shard_map/all_to_all | solution.py:397
Sparse Core Ops, SparseCore 0:
  40.2 68.6 all-gather.3

commit v8 on v7

--- a/solution.py
+++ b/solution.py
@@ -142,7 +142,7 @@
     spread_product(product, out_ref, 0, batch_count, block_rows)
 
 
-def late_call(own, parts, early):
+def late_call(own, parts, early, total):
     batch_count, block_rows, width = own.shape
     pair_count, rows, cols = parts[0].shape[1:]
     vmem = pl.BlockSpec(memory_space=pltpu.VMEM)
@@ -150,83 +150,98 @@
         late_kernel,
         in_specs=[vmem] * 4,
         out_specs=vmem,
-        out_shape=jax.ShapeDtypeStruct((batch_count * cols, pair_count * block_rows), jnp.bfloat16),
+        out_shape=jax.ShapeDtypeStruct((batch_count * cols, total * block_rows), jnp.bfloat16),
         compiler_params=params(),
     )(own, *parts, early)
 
 
-def flat_kernel(own_ref, units_ref, out_ref, amps_ref, sems):
+GATED = 1
+RING = ((0, 0, 4), (-1, 0, 4), (1, 0, 4), (-2, 0, 4), (2, 0, 4), (-3, 0, 4), (3, 0, 4), (4, 0, 2), (4, 2, 4))
+
+
+def ring_place(move):
+    return lax.rem(lax.axis_index("y") + 8 + move, 8)
+
+
+def flat_kernel(own_ref, held_ref, *refs):
+    pieces, (out_ref, amps_ref, sems) = refs[: len(RING)], refs[len(RING) :]
     batch_count, block_rows, width = own_ref.shape
     y_count, z_count, pairs, rows, cols = amps_ref.shape
     loads = []
-    for p in range(pairs):
-        block = units_ref.at[:, :, batch_count + p]
-        loads.append(pltpu.make_async_copy(block, amps_ref.at[:, :, p], sems.at[p]))
-        loads[p].start()
-    lanes = []
-    for p in range(pairs):
-        loads[p].wait()
-        lanes.append(jnp.concatenate([amps_ref[y, z, p] for z in range(z_count) for y in range(y_count)], axis=0))
+    for k, (move, first, last) in enumerate(RING):
+        target = amps_ref.at[ring_place(move), pl.ds(first, last - first)]
+        loads.append(pltpu.make_async_copy(pieces[k].at[:, pl.ds(batch_count, pairs)], target, sems.at[k]))
+        loads[k].start()
+    for load in loads:
+        load.wait()
+    lanes = [
+        jnp.concatenate([amps_ref[y, z, p] for z in range(z_count) for y in range(y_count)], axis=0)
+        for p in range(pairs)
+    ]
     own = own_ref[...].reshape(batch_count * block_rows, width)
     product = jnp.dot(own, jnp.concatenate(lanes, axis=1), preferred_element_type=jnp.float32)
-    spread_product(product, out_ref, 0, batch_count, block_rows)
-
-
-def flat_call(own, units):
+    spread_product(product, out_ref, out_ref.shape[1] - pairs * block_rows, batch_count, block_rows)
+
+
+def flat_call(own, pieces, inner):
     batch_count, block_rows, width = own.shape
-    y_count, z_count, unit_count, rows, cols = units.shape
+    z_count, unit_count, rows, cols = pieces[0].shape
     pairs = unit_count - batch_count
     vmem = pl.BlockSpec(memory_space=pltpu.VMEM)
     return pl.pallas_call(
         flat_kernel,
-        in_specs=[vmem, pl.BlockSpec(memory_space=pltpu.HBM)],
+        in_specs=[vmem, vmem] + [pl.BlockSpec(memory_space=pl.ANY)] * len(pieces),
         out_specs=vmem,
-        out_shape=jax.ShapeDtypeStruct((batch_count * cols, pairs * block_rows), jnp.bfloat16),
+        out_shape=jax.ShapeDtypeStruct(inner.shape, jnp.bfloat16),
+        input_output_aliases={1: 0},
         scratch_shapes=[
-            pltpu.VMEM((y_count, z_count, pairs, rows, cols), jnp.bfloat16),
-            pltpu.SemaphoreType.DMA((pairs,)),
+            pltpu.VMEM((8, z_count, pairs, rows, cols), jnp.bfloat16),
+            pltpu.SemaphoreType.DMA((len(pieces),)),
         ],
-        compiler_params=params(48),
-    )(own, units)
-
-
-def ladder_kernel(flip, ring_ref, flat_ref, units_ref, out_ref, block_ref, sems):
+        compiler_params=params(),
+    )(own, inner, *pieces)
+
+
+def ladder_kernel(flip, inner_ref, *refs):
+    pieces, (out_ref, block_ref, sems) = refs[: len(RING)], refs[len(RING) :]
     y_count, z_count, batch_count, rows, cols = block_ref.shape
     side = lax.rem(lax.axis_index("core") + flip, 2)
     step = z_count // 2
     here = pl.ds(pl.multiple_of(side * rows, rows), rows)
-    loads = []
+    loads = ([], [])
     for k in range(2):
-        span = pl.ds(k * step, step)
-        source = units_ref.at[:, span, pl.ds(0, batch_count), here]
-        loads.append(pltpu.make_async_copy(source, block_ref.at[:, span], sems.at[k]))
-        loads[-1].start()
-    inner = jnp.concatenate([ring_ref[...], flat_ref[...]], axis=1)
+        for m, (move, first, last) in enumerate(RING):
+            if first <= k * step < last:
+                source = pieces[m].at[pl.ds(k * step - first, step), pl.ds(0, batch_count), here]
+                target = block_ref.at[ring_place(move), pl.ds(k * step, step)]
+                loads[k].append(pltpu.make_async_copy(source, target, sems.at[k, m]))
+                loads[k][-1].start()
     height = step * y_count * rows
     for k in range(2):
-        loads[k].wait()
+        for load in loads[k]:
+            load.wait()
         places = [(z, y) for z in range(k * step, (k + 1) * step) for y in range(y_count)]
         lanes = [jnp.concatenate([block_ref[y, z, q] for z, y in places], axis=0) for q in range(batch_count)]
         factor = jnp.concatenate(lanes, axis=1)
-        product = jnp.dot(factor, inner, preferred_element_type=jnp.float32)
+        product = jnp.dot(factor, inner_ref[...], preferred_element_type=jnp.float32)
         out_ref[k * height : (k + 1) * height] = product.astype(out_ref.dtype)
 
 
-def ladder_call(flip, ring, flat, units, kind):
-    depth, width = ring.shape[0], ring.shape[1] + flat.shape[1]
-    y_count, z_count, unit_count, rows, cols = units.shape
+def ladder_call(flip, inner, pieces, kind):
+    depth, width = inner.shape
+    z_count, unit_count, rows, cols = pieces[0].shape
     vmem = pl.BlockSpec(memory_space=pltpu.VMEM)
     return pl.pallas_call(
         functools.partial(ladder_kernel, flip),
-        in_specs=[vmem, vmem, pl.BlockSpec(memory_space=pltpu.HBM)],
+        in_specs=[vmem] + [pl.BlockSpec(memory_space=pl.ANY)] * len(pieces),
         out_specs=vmem,
-        out_shape=jax.ShapeDtypeStruct((y_count * z_count * rows // 2, width), kind),
+        out_shape=jax.ShapeDtypeStruct((8 * z_count * rows // 2, width), kind),
         scratch_shapes=[
-            pltpu.VMEM((y_count, z_count, depth // cols, rows // 2, cols), jnp.bfloat16),
-            pltpu.SemaphoreType.DMA((2,)),
+            pltpu.VMEM((8, z_count, depth // cols, rows // 2, cols), jnp.bfloat16),
+            pltpu.SemaphoreType.DMA((2, len(pieces))),
         ],
-        compiler_params=params(48),
-    )(ring, flat, units)
+        compiler_params=params(),
+    )(inner, *pieces)
 
 
 def swing(block, axis):
@@ -379,18 +394,29 @@
     ring = 6
     first, second = prepare_call(amp_mask, amplitudes, factors, ring, 8)
     near = lax.all_to_all(second, "y", split_axis=0, concat_axis=0)
-    units = lax.all_gather(gate_call(lax.all_gather(first, "zh", axis=0), near), "y", axis=0)
+    held = gate_call(lax.all_gather(first, "zh", axis=0), near)
 
     back = lax.ppermute(near, ("zl", "zh"), cross(1))
     ahead = lax.ppermute(near, ("zl", "zh"), cross(-1))
     left = lax.ppermute(back[:4], ("zl", "zh"), cross(1))
     right = lax.ppermute(ahead[4:], ("zl", "zh"), cross(-1))
 
+    up, down = held, held
+    units = [held]
+    for k in range(3):
+        up = lax.ppermute(up, "y", turn(8, 1))
+        down = lax.ppermute(down, "y", turn(8, -1))
+        if k == GATED:
+            up, down = gate_call(up, back), gate_call(down, ahead)
+        units += [up, down]
+    units.append(lax.ppermute(up[:2], "y", turn(8, 1)))
+    units.append(lax.ppermute(down[2:], "y", turn(8, -1)))
+
     early = early_call(factors, (near, back, ahead))
-    late = late_call(factors, (left, right), early)
-    flat = flat_call(factors, units)
-    swapped = lax.ppermute(ladder_call(1, late, flat, units, jnp.bfloat16), "core", turn(2, 1))
-    keep = ladder_call(0, late, flat, units, jnp.float32)
+    late = late_call(factors, (left, right), early, pair_count)
+    inner = flat_call(factors, units, late)
+    swapped = lax.ppermute(ladder_call(1, inner, units, jnp.bfloat16), "core", turn(2, 1))
+    keep = ladder_call(0, inner, units, jnp.float32)
     partial = gather_call(keep, swapped, 8)
     pieces = lax.all_to_all(partial, ("zl", "x"), split_axis=0, concat_axis=0)
     direct, mirror = reduce_call(out_mask, pieces)

time: 183 us -> 179 us (0.978)
  between operations: 13.6 us -> 0.29 us
  starting transfers between devices: 55.3 us -> 65.9 us
  waiting for transfers between devices: 41.1 us -> 43.9 us
  blocking collectives: 54.2 us -> 51.7 us
  Pallas kernels: 17.7 us -> 15.5 us
    ppermute x1 -> x9, starting transfers between devices: 2.58 us -> 28.8 us  [the longest x3 10.2 us: on_device(): down = lax.ppermute(down, 'y', turn(8, -1))]
    ppermute x1, waiting for transfers between devices: 0.01 us -> 25.4 us  [on_device(): ahead = lax.ppermute(near, ('zl', 'zh'), cross(-1))]
    ppermute x1, starting transfers between devices: 17.7 us -> 1.92 us  [on_device(): left = lax.ppermute(back[:4], ('zl', 'zh'), cross(1))]
    ppermute x1, waiting for transfers between devices: 15.8 us -> 0.01 us  [on_device(): back = lax.ppermute(near, ('zl', 'zh'), cross(1))]
    ppermute x1, waiting for transfers between devices: 9.91 us -> 0.01 us  [on_device(): right = lax.ppermute(ahead[4:], ('zl', 'zh'), cross(-1))]
    ppermute x1, starting transfers between devices: 6.77 us -> 12.5 us  [on_device(): ahead = lax.ppermute(near, ('zl', 'zh'), cross(-1))]
    ppermute x1, starting transfers between devices: 6.45 us -> 1.92 us  [on_device(): back = lax.ppermute(near, ('zl', 'zh'), cross(1))]
    ppermute x1 -> x9, waiting for transfers between devices: 0.01 us -> 3.1 us  [the longest x3 2.51 us: on_device(): down = lax.ppermute(down, 'y', turn(8, -1))]
  transfers between devices with their start and end apart: 8 -> 15, of which waited for: 5 -> 6; matrix products, arithmetic and copies ran while one was open for 0% -> 0% of each run, Pallas kernels for 3% -> 3%
where the time goes in v8:
time: 179 us; the launch traced here: 177 us
  starting transfers between devices  65.9 us (37%)
  blocking collectives  51.7 us (29%)
  waiting for transfers between devices  43.9 us (25%)
  Pallas kernels  15.5 us (9%)
    ppermute x1, waiting for transfers between devices, on_device(): ahead = lax.ppermute(near, ('zl', 'zh'), cross(-1))  25.4 us
    all_gather x1, blocking collectives, on_device(): held = gate_call(lax.all_gather(first, 'zh', axis=0), near)  21.6 us
    all_to_all x1, blocking collectives, on_device(): pieces = lax.all_to_all(partial, ('zl', 'x'), split_axis=0, concat_axis=0)  18.2 us
    ppermute x1, starting transfers between devices, on_device(): ahead = lax.ppermute(near, ('zl', 'zh'), cross(-1))  12.5 us
    all_to_all x1, blocking collectives, on_device(): lax.all_to_all(direct.reshape(16, 32, 128), ROW, split_axis=0, concat_axi...  11.9 us
    all_to_all x1, waiting for transfers between devices, on_device(): lax.all_to_all(mirror.reshape(32, 16, 128), COL, split_axis=0, concat_axi...  10.9 us
    ppermute x3, starting transfers between devices, on_device(): down = lax.ppermute(down, 'y', turn(8, -1))  10.2 us
    all_to_all x1, starting transfers between devices, on_device(): near = lax.all_to_all(second, 'y', split_axis=0, concat_axis=0)  7.66 us
  transfers between devices with their start and end apart: 15, of which 6 were waited for; matrix products, arithmetic and copies ran while one was open for 0% of the time, Pallas kernels for 3%

profile of v8, /device:TPU:1, one launch (start us, length us, event | category | flops | bytes accessed | tf_op | source)
XLA Modules:
  0.0 177.3 jit_solution(3339460748809843176)
XLA Ops:
  0.0 2.7 %shard_map.55 = (bf16[10,64,128]{2,1,0:T(8,128)(2,1)}, bf16[8,6,64,128]{3,2,1,0:T(8,128)(2,1)}) custom-call(s32[16,16]{1,0:T(8,128)} %mask_ref.2, bf16[8,64,128]{2,1,0:T(8,128)(2,1)} %amps_ref.1, bf16[8,64,2048]{2,1,0:T(8,128)(2,1)} %own_ref.5), custom_call_target="tpu_custom_call" | custom-call | tf_op jit(solution)/shard_map/pallas_call | solution.py:62
  2.7 7.7 %all-to-all-start = ((bf16[8,6,64,128]{3,2,1,0:T(8,128)(2,1)}), bf16[8,6,64,128]{3,2,1,0:T(8,128)(2,1)S(1)}, u32[]{:S(2)}, u32[]{:S(2)}) async-start(bf16[8,6,64,128]{3,2,1,0:T(8,128)(2,1)} %get-tuple-element.9), calls=%async_computation | async-start | bytes 1572864 | tf_op jit(solution)/shard_map/all_to_all | solution.py:396
  10.4 21.6 %all-gather = bf16[40,64,128]{2,1,0:T(8,128)(2,1)S(1)} all-gather(bf16[10,64,128]{2,1,0:T(8,128)(2,1)} %get-tuple-element.10), channel_id=2, replica_groups=mesh['zl'=2,'x'=4,'core'=2,'zh'=4,'y'=8] {'zh'}, dimensions={0}, use_global_device_ids=true | all-gather | bytes 819200 | tf_op jit(solution)/shard_map/all_gather | solution.py:397
  32.0 0.0 all-to-all-done.near_ref.other_ref
  32.0 3.5 %collective-permute-start.5 = (bf16[4,10,64,128]{3,2,1,0:T(8,128)(2,1)S(1)}, bf16[4,10,64,128]{3,2,1,0:T(8,128)(2,1)S(1)}, u32[]{:S(2)}, u32[]{:S(2)}) collective-permute-start(bf16[4,10,64,128]{3,2,1,0:T(8,128)(2,1)S(1)} %shard_map.58.refs_0_), channel_id=1, source_target_pairs={{0,7},{1,0},{2,1},{3,2},{4,3},{5,4},{6,5},{7,6},{8,15},{9,8},{10,9... | collective-permute-start | bytes 1966088 | tf_op jit(solution)/shard_map/ppermute | solution.py:408
  35.5 1.9 %collective-permute-start.4 = (bf16[4,10,64,128]{3,2,1,0:T(8,128)(2,1)S(1)}, bf16[4,10,64,128]{3,2,1,0:T(8,128)(2,1)S(1)}, u32[]{:S(2)}, u32[]{:S(2)}) collective-permute-start(bf16[4,10,64,128]{3,2,1,0:T(8,128)(2,1)S(1)} %shard_map.58.refs_0_), channel_id=1, source_target_pairs={{0,1},{1,2},{2,3},{3,4},{4,5},{5,6},{6,7},{7,0},{8,9},{9,10},{10,1... | collective-permute-start | bytes 1966088 | tf_op jit(solution)/shard_map/ppermute | solution.py:407
  37.4 12.5 %collective-permute-start.2 = (bf16[8,6,64,128]{3,2,1,0:T(8,128)(2,1)S(1)}, bf16[8,6,64,128]{3,2,1,0:T(8,128)(2,1)S(1)}, u32[]{:S(2)}, u32[]{:S(2)}) collective-permute-start(bf16[8,6,64,128]{3,2,1,0:T(8,128)(2,1)S(1)} %all-to-all-done.near_ref.other_ref), channel_id=1, source_target_pairs={{0,24},{8,0},{16,8},{24,16},{256,264},{264,272},{272,280},{280,256... | collective-permute-start | bytes 2359304 | tf_op jit(solution)/shard_map/ppermute | solution.py:400
  49.9 1.9 %collective-permute-start = (bf16[8,6,64,128]{3,2,1,0:T(8,128)(2,1)S(1)}, bf16[8,6,64,128]{3,2,1,0:T(8,128)(2,1)S(1)}, u32[]{:S(2)}, u32[]{:S(2)}) collective-permute-start(bf16[8,6,64,128]{3,2,1,0:T(8,128)(2,1)S(1)} %all-to-all-done.near_ref.other_ref), channel_id=1, source_target_pairs={{0,8},{8,16},{16,24},{24,0},{256,280},{264,256},{272,264},{280,272... | collective-permute-start | bytes 2359304 | tf_op jit(solution)/shard_map/ppermute | solution.py:399
  51.9 0.0 collective-permute-done.5.refs_2_
  51.9 3.1 %collective-permute-start.7 = (bf16[4,10,64,128]{3,2,1,0:T(8,128)(2,1)S(1)}, bf16[4,10,64,128]{3,2,1,0:T(8,128)(2,1)S(1)}, u32[]{:S(2)}, u32[]{:S(2)}) collective-permute-start(bf16[4,10,64,128]{3,2,1,0:T(8,128)(2,1)S(1)} %collective-permute-done.5.refs_2_), channel_id=1, source_target_pairs={{0,7},{1,0},{2,1},{3,2},{4,3},{5,4},{6,5},{7,6},{8,15},{9,8},{10,9... | collective-permute-start | bytes 1966088 | tf_op jit(solution)/shard_map/ppermute | solution.py:408
  55.0 0.0 collective-permute-done.4.refs_1_
  55.0 2.2 %collective-permute-start.6 = (bf16[4,10,64,128]{3,2,1,0:T(8,128)(2,1)S(1)}, bf16[4,10,64,128]{3,2,1,0:T(8,128)(2,1)S(1)}, u32[]{:S(2)}, u32[]{:S(2)}) collective-permute-start(bf16[4,10,64,128]{3,2,1,0:T(8,128)(2,1)S(1)} %collective-permute-done.4.refs_1_), channel_id=1, source_target_pairs={{0,1},{1,2},{2,3},{3,4},{4,5},{5,6},{6,7},{7,0},{8,9},{9,10},{10,1... | collective-permute-start | bytes 1966088 | tf_op jit(solution)/shard_map/ppermute | solution.py:407
  57.2 25.4 %collective-permute-done.2.ahead_ref.other_ref = bf16[8,6,64,128]{3,2,1,0:T(8,128)(2,1)S(1)} collective-permute-done((bf16[8,6,64,128]{3,2,1,0:T(8,128)(2,1)S(1)}, bf16[8,6,64,128]{3,2,1,0:T(8,128)(2,1)S(1)}, u32[]{:S(2)}, u32[]{:S(2)}) %collective-permute-start.2) | collective-permute-done | bytes 786464 | tf_op jit(solution)/shard_map/ppermute | solution.py:400
  82.5 0.0 collective-permute-done.7.held_ref
  82.6 3.6 %collective-permute-start.9 = (bf16[4,10,64,128]{3,2,1,0:T(8,128)(2,1)S(1)}, bf16[4,10,64,128]{3,2,1,0:T(8,128)(2,1)S(1)}, u32[]{:S(2)}, u32[]{:S(2)}) collective-permute-start(bf16[4,10,64,128]{3,2,1,0:T(8,128)(2,1)S(1)} %shard_map.60.refs_4_), channel_id=1, source_target_pairs={{0,7},{1,0},{2,1},{3,2},{4,3},{5,4},{6,5},{7,6},{8,15},{9,8},{10,9... | collective-permute-start | bytes 1966088 | tf_op jit(solution)/shard_map/ppermute | solution.py:408
  86.1 0.0 collective-permute-done.back_ref.other_ref
  86.1 0.0 collective-permute-done.6.held_ref
  86.2 1.9 %collective-permute-start.8 = (bf16[4,10,64,128]{3,2,1,0:T(8,128)(2,1)S(1)}, bf16[4,10,64,128]{3,2,1,0:T(8,128)(2,1)S(1)}, u32[]{:S(2)}, u32[]{:S(2)}) collective-permute-start(bf16[4,10,64,128]{3,2,1,0:T(8,128)(2,1)S(1)} %shard_map.59.refs_3_), channel_id=1, source_target_pairs={{0,1},{1,2},{2,3},{3,4},{4,5},{5,6},{6,7},{7,0},{8,9},{9,10},{10,1... | collective-permute-start | bytes 1966088 | tf_op jit(solution)/shard_map/ppermute | solution.py:407
  88.1 6.2 %collective-permute-start.3 = (bf16[4,6,64,128]{3,2,1,0:T(8,128)(2,1)S(1)}, bf16[4,6,64,128]{3,2,1,0:T(8,128)(2,1)S(1)}, u32[]{:S(2)}, u32[]{:S(2)}) collective-permute-start(bf16[4,6,64,128]{3,2,1,0:T(8,128)(2,1)S(1)} %slice.17), channel_id=1, source_target_pairs={{0,24},{8,0},{16,8},{24,16},{256,264},{264,272},{272,280},{280,256... | collective-permute-start | bytes 1179656 | tf_op jit(solution)/shard_map/ppermute | solution.py:402
  94.4 1.9 %collective-permute-start.1 = (bf16[4,6,64,128]{3,2,1,0:T(8,128)(2,1)S(1)}, bf16[4,6,64,128]{3,2,1,0:T(8,128)(2,1)S(1)}, u32[]{:S(2)}, u32[]{:S(2)}) collective-permute-start(bf16[4,6,64,128]{3,2,1,0:T(8,128)(2,1)S(1)} %slice.16), channel_id=1, source_target_pairs={{0,8},{8,16},{16,24},{24,0},{256,280},{264,256},{272,264},{280,272... | collective-permute-start | bytes 1179656 | tf_op jit(solution)/shard_map/ppermute | solution.py:401
  96.3 2.5 %collective-permute-done.9.refs_6_ = bf16[4,10,64,128]{3,2,1,0:T(8,128)(2,1)S(1)} collective-permute-done((bf16[4,10,64,128]{3,2,1,0:T(8,128)(2,1)S(1)}, bf16[4,10,64,128]{3,2,1,0:T(8,128)(2,1)S(1)}, u32[]{:S(2)}, u32[]{:S(2)}) %collective-permute-start.9) | collective-permute-done | bytes 655392 | tf_op jit(solution)/shard_map/ppermute | solution.py:408
  98.8 5.0 %collective-permute-start.11 = (bf16[2,10,64,128]{3,2,1,0:T(8,128)(2,1)S(1)}, bf16[2,10,64,128]{3,2,1,0:T(8,128)(2,1)S(1)}, u32[]{:S(2)}, u32[]{:S(2)}) collective-permute-start(bf16[2,10,64,128]{3,2,1,0:T(8,128)(2,1)S(1)} %slice.19), channel_id=1, source_target_pairs={{0,7},{1,0},{2,1},{3,2},{4,3},{5,4},{6,5},{7,6},{8,15},{9,8},{10,9... | collective-permute-start | bytes 983048 | tf_op jit(solution)/shard_map/ppermute | solution.py:413
  103.8 0.0 collective-permute-done.8.refs_5_
  103.9 1.9 %collective-permute-start.10 = (bf16[2,10,64,128]{3,2,1,0:T(8,128)(2,1)S(1)}, bf16[2,10,64,128]{3,2,1,0:T(8,128)(2,1)S(1)}, u32[]{:S(2)}, u32[]{:S(2)}) collective-permute-start(bf16[2,10,64,128]{3,2,1,0:T(8,128)(2,1)S(1)} %slice.18), channel_id=1, source_target_pairs={{0,1},{1,2},{2,3},{3,4},{4,5},{5,6},{6,7},{7,0},{8,9},{9,10},{10,1... | collective-permute-start | bytes 983048 | tf_op jit(solution)/shard_map/ppermute | solution.py:412
  105.8 0.0 copy-done
  105.8 2.1 %shard_map.56.early_ref = f32[512,768]{1,0:T(8,128)S(1)} custom-call(bf16[8,64,2048]{2,1,0:T(8,128)(2,1)S(1)} %copy-done, bf16[8,6,64,128]{3,2,1,0:T(8,128)(2,1)S(1)} %all-to-all-done.near_ref.other_ref, bf16[8,6,64,128]{3,2,1,0:T(8,128)(2,1)S(1)} %collective-permute-done.back_ref.other_ref, ...), custom_call_target="tpu_custom_call" | custom-call | tf_op jit(solution)/shard_map/pallas_call | solution.py:128
  107.9 0.0 collective-permute-done.3.right_ref
  107.9 4.5 %collective-permute-done.1.left_ref = bf16[4,6,64,128]{3,2,1,0:T(8,128)(2,1)S(1)} collective-permute-done((bf16[4,6,64,128]{3,2,1,0:T(8,128)(2,1)S(1)}, bf16[4,6,64,128]{3,2,1,0:T(8,128)(2,1)S(1)}, u32[]{:S(2)}, u32[]{:S(2)}) %collective-permute-start.1) | collective-permute-done | bytes 393248 | tf_op jit(solution)/shard_map/ppermute | solution.py:401
  112.3 0.7 shard_map.57.held_ref
  113.0 0.0 collective-permute-done.11.refs_8_
  113.0 0.3 collective-permute-done.10.refs_7_
  113.3 1.3 shard_map.61.inner_ref
  114.6 1.9 %shard_map.63 = bf16[1024,512]{1,0:T(8,128)(2,1)S(1)} custom-call(bf16[1024,512]{1,0:T(8,128)(2,1)S(1)} %shard_map.61.inner_ref, bf16[4,10,64,128]{3,2,1,0:T(8,128)(2,1)S(1)} %shard_map.58.refs_0_, bf16[4,10,64,128]{3,2,1,0:T(8,128)(2,1)S(1)} %collective-permute-done.4.refs_1_, bf16[4,10,64,128]{3,2,1,0:T(8,128)(2,1)S(1)} %collective-permute-done.5.refs_2_, ...), custom_call_target="tpu_custom_call" | custom-call | tf_op jit(solution)/shard_map/pallas_call | solution.py:234
  116.6 5.7 %collective-permute-start.12 = (bf16[1024,512]{1,0:T(8,128)(2,1)S(1)}, bf16[1024,512]{1,0:T(8,128)(2,1)S(1)}, u32[]{:S(2)}, u32[]{:S(2)}) collective-permute-start(bf16[1024,512]{1,0:T(8,128)(2,1)S(1)} %shard_map.63), channel_id=1, source_target_pairs={{0,32},{32,0},{1,33},{33,1},{2,34},{34,2},{3,35},{35,3},{4,36},{36... | collective-permute-start | bytes 3145736 | tf_op jit(solution)/shard_map/ppermute | solution.py:418
  122.3 1.9 %shard_map.62.keep_ref = f32[1024,512]{1,0:T(8,128)S(1)} custom-call(bf16[1024,512]{1,0:T(8,128)(2,1)S(1)} %shard_map.61.inner_ref, bf16[4,10,64,128]{3,2,1,0:T(8,128)(2,1)S(1)} %shard_map.58.refs_0_, bf16[4,10,64,128]{3,2,1,0:T(8,128)(2,1)S(1)} %collective-permute-done.4.refs_1_, bf16[4,10,64,128]{3,2,1,0:T(8,128)(2,1)S(1)} %collective-permute-done.5.refs_2_, ...), custom_call_target="tpu_custom_call" | custom-call | tf_op jit(solution)/shard_map/pallas_call | solution.py:234
  124.2 0.0 copy-start.1
  124.2 0.3 collective-permute-done.12.other_ref
  124.5 1.1 shard_map.64
  125.6 0.0 copy-start.2
  125.6 18.2 %all_to_all.20.part_ref = bf16[8,128,512]{2,1,0:T(8,128)(2,1)S(1)} all-to-all(bf16[8,128,512]{2,1,0:T(8,128)(2,1)S(1)} %shard_map.64), channel_id=1, replica_groups=mesh['zl'=2,'x'=4,'core'=2,'zh'=4,'y'=8] {'zl','x'}, dimensions={0} | all-to-all | bytes 2097152 | tf_op jit(solution)/shard_map/all_to_all | solution.py:421
  143.8 0.0 copy-done.1
  143.9 1.5 shard_map.65
  145.4 11.9 %all_to_all.21.direct_ref = f32[16,32,128]{2,1,0:T(8,128)S(1)} all-to-all(f32[16,32,128]{2,1,0:T(8,128)S(1)} %bitcast.4), channel_id=1, replica_groups=mesh['zl'=2,'x'=4,'core'=2,'zh'=4,'y'=8] {'zl','x','core'}, dimensions={0} | all-to-all | bytes 524288 | tf_op jit(solution)/shard_map/all_to_all | solution.py:424
  157.3 6.9 %all-to-all-start.3 = ((bf16[32,16,128]{2,1,0:T(8,128)(2,1)}), bf16[32,16,128]{2,1,0:T(8,128)(2,1)S(1)}, u32[]{:S(2)}, u32[]{:S(2)}) async-start(bf16[32,16,128]{2,1,0:T(8,128)(2,1)} %bitcast.2), calls=%async_computation.3 | async-start | bytes 262144 | tf_op jit(solution)/shard_map/all_to_all | solution.py:423
  164.2 0.7 shard_map.66.direct_ref
  164.8 10.9 %all-to-all-done.3.mirror_ref = bf16[32,16,128]{2,1,0:T(8,128)(2,1)S(1)} async-done(((bf16[32,16,128]{2,1,0:T(8,128)(2,1)}), bf16[32,16,128]{2,1,0:T(8,128)(2,1)S(1)}, u32[]{:S(2)}, u32[]{:S(2)}) %all-to-all-start.3) | async-done | bytes 131104 | tf_op jit(solution)/shard_map/all_to_all | solution.py:423
  175.8 0.0 copy-done.2
  175.8 1.6 shard_map.67
  (8 shorter events, 0.1 us)
Async XLA Ops:
  2.7 29.2 %all-to-all-start = ((bf16[8,6,64,128]{3,2,1,0:T(8,128)(2,1)}), bf16[8,6,64,128]{3,2,1,0:T(8,128)(2,1)S(1)}, u32[]{:S(2)}, u32[]{:S(2)}) async-start(bf16[8,6,64,128]{3,2,1,0:T(8,128)(2,1)} %get-tuple-element.9), calls=%async_computation | async-start | bytes 1572864 | tf_op jit(solution)/shard_map/all_to_all | solution.py:396
  32.0 19.9 %collective-permute-start.5 = (bf16[4,10,64,128]{3,2,1,0:T(8,128)(2,1)S(1)}, bf16[4,10,64,128]{3,2,1,0:T(8,128)(2,1)S(1)}, u32[]{:S(2)}, u32[]{:S(2)}) collective-permute-start(bf16[4,10,64,128]{3,2,1,0:T(8,128)(2,1)S(1)} %shard_map.58.refs_0_), channel_id=1, source_target_pairs={{0,7},{1,0},{2,1},{3,2},{4,3},{5,4},{6,5},{7,6},{8,15},{9,8},{10,9... | collective-permute-start | bytes 1966088 | tf_op jit(solution)/shard_map/ppermute | solution.py:408
  35.5 19.5 %collective-permute-start.4 = (bf16[4,10,64,128]{3,2,1,0:T(8,128)(2,1)S(1)}, bf16[4,10,64,128]{3,2,1,0:T(8,128)(2,1)S(1)}, u32[]{:S(2)}, u32[]{:S(2)}) collective-permute-start(bf16[4,10,64,128]{3,2,1,0:T(8,128)(2,1)S(1)} %shard_map.58.refs_0_), channel_id=1, source_target_pairs={{0,1},{1,2},{2,3},{3,4},{4,5},{5,6},{6,7},{7,0},{8,9},{9,10},{10,1... | collective-permute-start | bytes 1966088 | tf_op jit(solution)/shard_map/ppermute | solution.py:407
  37.4 45.1 %collective-permute-start.2 = (bf16[8,6,64,128]{3,2,1,0:T(8,128)(2,1)S(1)}, bf16[8,6,64,128]{3,2,1,0:T(8,128)(2,1)S(1)}, u32[]{:S(2)}, u32[]{:S(2)}) collective-permute-start(bf16[8,6,64,128]{3,2,1,0:T(8,128)(2,1)S(1)} %all-to-all-done.near_ref.other_ref), channel_id=1, source_target_pairs={{0,24},{8,0},{16,8},{24,16},{256,264},{264,272},{272,280},{280,256... | collective-permute-start | bytes 2359304 | tf_op jit(solution)/shard_map/ppermute | solution.py:400
  49.9 36.2 %collective-permute-start = (bf16[8,6,64,128]{3,2,1,0:T(8,128)(2,1)S(1)}, bf16[8,6,64,128]{3,2,1,0:T(8,128)(2,1)S(1)}, u32[]{:S(2)}, u32[]{:S(2)}) collective-permute-start(bf16[8,6,64,128]{3,2,1,0:T(8,128)(2,1)S(1)} %all-to-all-done.near_ref.other_ref), channel_id=1, source_target_pairs={{0,8},{8,16},{16,24},{24,0},{256,280},{264,256},{272,264},{280,272... | collective-permute-start | bytes 2359304 | tf_op jit(solution)/shard_map/ppermute | solution.py:399
  51.9 30.7 %collective-permute-start.7 = (bf16[4,10,64,128]{3,2,1,0:T(8,128)(2,1)S(1)}, bf16[4,10,64,128]{3,2,1,0:T(8,128)(2,1)S(1)}, u32[]{:S(2)}, u32[]{:S(2)}) collective-permute-start(bf16[4,10,64,128]{3,2,1,0:T(8,128)(2,1)S(1)} %collective-permute-done.5.refs_2_), channel_id=1, source_target_pairs={{0,7},{1,0},{2,1},{3,2},{4,3},{5,4},{6,5},{7,6},{8,15},{9,8},{10,9... | collective-permute-start | bytes 1966088 | tf_op jit(solution)/shard_map/ppermute | solution.py:408
  55.0 31.1 %collective-permute-start.6 = (bf16[4,10,64,128]{3,2,1,0:T(8,128)(2,1)S(1)}, bf16[4,10,64,128]{3,2,1,0:T(8,128)(2,1)S(1)}, u32[]{:S(2)}, u32[]{:S(2)}) collective-permute-start(bf16[4,10,64,128]{3,2,1,0:T(8,128)(2,1)S(1)} %collective-permute-done.4.refs_1_), channel_id=1, source_target_pairs={{0,1},{1,2},{2,3},{3,4},{4,5},{5,6},{6,7},{7,0},{8,9},{9,10},{10,1... | collective-permute-start | bytes 1966088 | tf_op jit(solution)/shard_map/ppermute | solution.py:407
  82.6 23.2 %copy-start = (bf16[8,64,2048]{2,1,0:T(8,128)(2,1)S(1)}, bf16[8,64,2048]{2,1,0:T(8,128)(2,1)}, u32[]{:S(2)}) copy-start(bf16[8,64,2048]{2,1,0:T(8,128)(2,1)} %own_ref.5) | copy-start | bytes 6291460
  82.6 16.3 %collective-permute-start.9 = (bf16[4,10,64,128]{3,2,1,0:T(8,128)(2,1)S(1)}, bf16[4,10,64,128]{3,2,1,0:T(8,128)(2,1)S(1)}, u32[]{:S(2)}, u32[]{:S(2)}) collective-permute-start(bf16[4,10,64,128]{3,2,1,0:T(8,128)(2,1)S(1)} %shard_map.60.refs_4_), channel_id=1, source_target_pairs={{0,7},{1,0},{2,1},{3,2},{4,3},{5,4},{6,5},{7,6},{8,15},{9,8},{10,9... | collective-permute-start | bytes 1966088 | tf_op jit(solution)/shard_map/ppermute | solution.py:408
  86.2 17.7 %collective-permute-start.8 = (bf16[4,10,64,128]{3,2,1,0:T(8,128)(2,1)S(1)}, bf16[4,10,64,128]{3,2,1,0:T(8,128)(2,1)S(1)}, u32[]{:S(2)}, u32[]{:S(2)}) collective-permute-start(bf16[4,10,64,128]{3,2,1,0:T(8,128)(2,1)S(1)} %shard_map.59.refs_3_), channel_id=1, source_target_pairs={{0,1},{1,2},{2,3},{3,4},{4,5},{5,6},{6,7},{7,0},{8,9},{9,10},{10,1... | collective-permute-start | bytes 1966088 | tf_op jit(solution)/shard_map/ppermute | solution.py:407
  88.1 19.7 %collective-permute-start.3 = (bf16[4,6,64,128]{3,2,1,0:T(8,128)(2,1)S(1)}, bf16[4,6,64,128]{3,2,1,0:T(8,128)(2,1)S(1)}, u32[]{:S(2)}, u32[]{:S(2)}) collective-permute-start(bf16[4,6,64,128]{3,2,1,0:T(8,128)(2,1)S(1)} %slice.17), channel_id=1, source_target_pairs={{0,24},{8,0},{16,8},{24,16},{256,264},{264,272},{272,280},{280,256... | collective-permute-start | bytes 1179656 | tf_op jit(solution)/shard_map/ppermute | solution.py:402
  94.4 17.9 %collective-permute-start.1 = (bf16[4,6,64,128]{3,2,1,0:T(8,128)(2,1)S(1)}, bf16[4,6,64,128]{3,2,1,0:T(8,128)(2,1)S(1)}, u32[]{:S(2)}, u32[]{:S(2)}) collective-permute-start(bf16[4,6,64,128]{3,2,1,0:T(8,128)(2,1)S(1)} %slice.16), channel_id=1, source_target_pairs={{0,8},{8,16},{16,24},{24,0},{256,280},{264,256},{272,264},{280,272... | collective-permute-start | bytes 1179656 | tf_op jit(solution)/shard_map/ppermute | solution.py:401
  98.8 14.2 %collective-permute-start.11 = (bf16[2,10,64,128]{3,2,1,0:T(8,128)(2,1)S(1)}, bf16[2,10,64,128]{3,2,1,0:T(8,128)(2,1)S(1)}, u32[]{:S(2)}, u32[]{:S(2)}) collective-permute-start(bf16[2,10,64,128]{3,2,1,0:T(8,128)(2,1)S(1)} %slice.19), channel_id=1, source_target_pairs={{0,7},{1,0},{2,1},{3,2},{4,3},{5,4},{6,5},{7,6},{8,15},{9,8},{10,9... | collective-permute-start | bytes 983048 | tf_op jit(solution)/shard_map/ppermute | solution.py:413
  103.9 9.4 %collective-permute-start.10 = (bf16[2,10,64,128]{3,2,1,0:T(8,128)(2,1)S(1)}, bf16[2,10,64,128]{3,2,1,0:T(8,128)(2,1)S(1)}, u32[]{:S(2)}, u32[]{:S(2)}) collective-permute-start(bf16[2,10,64,128]{3,2,1,0:T(8,128)(2,1)S(1)} %slice.18), channel_id=1, source_target_pairs={{0,1},{1,2},{2,3},{3,4},{4,5},{5,6},{6,7},{7,0},{8,9},{9,10},{10,1... | collective-permute-start | bytes 983048 | tf_op jit(solution)/shard_map/ppermute | solution.py:412
  116.6 8.0 %collective-permute-start.12 = (bf16[1024,512]{1,0:T(8,128)(2,1)S(1)}, bf16[1024,512]{1,0:T(8,128)(2,1)S(1)}, u32[]{:S(2)}, u32[]{:S(2)}) collective-permute-start(bf16[1024,512]{1,0:T(8,128)(2,1)S(1)} %shard_map.63), channel_id=1, source_target_pairs={{0,32},{32,0},{1,33},{33,1},{2,34},{34,2},{3,35},{35,3},{4,36},{36... | collective-permute-start | bytes 3145736 | tf_op jit(solution)/shard_map/ppermute | solution.py:418
  124.2 19.6 %copy-start.1 = (s32[16,16]{1,0:T(8,128)S(1)}, s32[16,16]{1,0:T(8,128)}, u32[]{:S(2)}) copy-start(s32[16,16]{1,0:T(8,128)} %mask_ref.3) | copy-start | bytes 3076
  125.6 50.2 %copy-start.2 = (s32[8]{0:T(128)S(1)}, s32[8]{0:T(128)}, u32[]{:S(2)}) copy-start(s32[8]{0:T(128)} %partner_ref.1) | copy-start | bytes 100
  157.3 18.5 %all-to-all-start.3 = ((bf16[32,16,128]{2,1,0:T(8,128)(2,1)}), bf16[32,16,128]{2,1,0:T(8,128)(2,1)S(1)}, u32[]{:S(2)}, u32[]{:S(2)}) async-start(bf16[32,16,128]{2,1,0:T(8,128)(2,1)} %bitcast.2), calls=%async_computation.3 | async-start | bytes 262144 | tf_op jit(solution)/shard_map/all_to_all | solution.py:423

commit v9 on v8

--- a/solution.py
+++ b/solution.py
@@ -155,12 +155,11 @@
     )(own, *parts, early)
 
 
-GATED = 1
 RING = ((0, 0, 4), (-1, 0, 4), (1, 0, 4), (-2, 0, 4), (2, 0, 4), (-3, 0, 4), (3, 0, 4), (4, 0, 2), (4, 2, 4))
 
 
 def ring_place(move):
-    return lax.rem(lax.axis_index("y") + 8 + move, 8)
+    return lax.rem(lax.axis_index("y") + 8 + move * (1 - 2 * lax.axis_index("core")), 8)
 
 
 def flat_kernel(own_ref, held_ref, *refs):
@@ -384,8 +383,8 @@
     return [(i, (i + step) % count) for i in range(count)]
 
 
-def cross(step):
-    return [(k, k // 4 * 4 + (k % 4 + (1 - k // 4 * 2) * step) % 4) for k in range(8)]
+def cross(count, step):
+    return [(k, k // count * count + (k % count + (1 - k // count * 2) * step) % count) for k in range(2 * count)]
 
 
 def on_device(amplitudes, factors, amp_mask, out_mask, partner):
@@ -396,21 +395,23 @@
     near = lax.all_to_all(second, "y", split_axis=0, concat_axis=0)
     held = gate_call(lax.all_gather(first, "zh", axis=0), near)
 
-    back = lax.ppermute(near, ("zl", "zh"), cross(1))
-    ahead = lax.ppermute(near, ("zl", "zh"), cross(-1))
-    left = lax.ppermute(back[:4], ("zl", "zh"), cross(1))
-    right = lax.ppermute(ahead[4:], ("zl", "zh"), cross(-1))
+    back = lax.ppermute(near, ("zl", "zh"), cross(4, 1))
+    ahead = lax.ppermute(near, ("zl", "zh"), cross(4, -1))
+    left = lax.ppermute(back[:4], ("zl", "zh"), cross(4, 1))
+    right = lax.ppermute(ahead[4:], ("zl", "zh"), cross(4, -1))
 
     up, down = held, held
     units = [held]
     for k in range(3):
-        up = lax.ppermute(up, "y", turn(8, 1))
-        down = lax.ppermute(down, "y", turn(8, -1))
-        if k == GATED:
-            up, down = gate_call(up, back), gate_call(down, ahead)
+        up = lax.ppermute(up, ("core", "y"), cross(8, 1))
+        down = lax.ppermute(down, ("core", "y"), cross(8, -1))
+        if k == 1:
+            up = gate_call(up, ahead)
+        if k == 2:
+            up = gate_call(up, back)
         units += [up, down]
-    units.append(lax.ppermute(up[:2], "y", turn(8, 1)))
-    units.append(lax.ppermute(down[2:], "y", turn(8, -1)))
+    units.append(lax.ppermute(up[:2], ("core", "y"), cross(8, 1)))
+    units.append(lax.ppermute(down[2:], ("core", "y"), cross(8, -1)))
 
     early = early_call(factors, (near, back, ahead))
     late = late_call(factors, (left, right), early, pair_count)

time: 179 us -> 173 us (0.966)
  waiting for transfers between devices: 43.9 us -> 26.1 us
  blocking collectives: 51.7 us -> 59.5 us
  starting transfers between devices: 65.9 us -> 70.8 us
    ppermute x12, waiting for transfers between devices: 32.6 us -> 14.9 us  [the longest x1 7.46 us: on_device(): left = lax.ppermute(back[:4], ('zl', 'zh'), cross(4, 1))]
    ppermute x12, starting transfers between devices: 45.7 us -> 56.9 us  [the longest x3 13.7 us: on_device(): up = lax.ppermute(up, ('core', 'y'), cross(8, 1))]
    all_to_all x1, blocking collectives: 18.2 us -> 26 us  [on_device(): pieces = lax.all_to_all(partial, ('zl', 'x'), split_axis=0, concat_axis=0)]
    ppermute x1, starting transfers between devices: 5.69 us -> 2.41 us  [on_device(): lax.ppermute(ladder_call(1, inner, units, jnp.bfloat16), 'core', turn(2, 1))]
    all_to_all x1, starting transfers between devices: 6.86 us -> 3.86 us  [on_device(): lax.all_to_all(mirror.reshape(32, 16, 128), COL, split_axis=0, concat_axi...]
where the time goes in v9:
time: 173 us; the launch traced here: 172 us
  starting transfers between devices  70.8 us (41%)
  blocking collectives  59.5 us (34%)
  waiting for transfers between devices  26.1 us (15%)
  Pallas kernels  15.5 us (9%)
    all_to_all x1, blocking collectives, on_device(): pieces = lax.all_to_all(partial, ('zl', 'x'), split_axis=0, concat_axis=0)  26 us
    all_gather x1, blocking collectives, on_device(): held = gate_call(lax.all_gather(first, 'zh', axis=0), near)  21.6 us
    ppermute x3, starting transfers between devices, on_device(): up = lax.ppermute(up, ('core', 'y'), cross(8, 1))  13.7 us
    ppermute x1, starting transfers between devices, on_device(): ahead = lax.ppermute(near, ('zl', 'zh'), cross(4, -1))  12.7 us
    all_to_all x1, blocking collectives, on_device(): lax.all_to_all(direct.reshape(16, 32, 128), ROW, split_axis=0, concat_axi...  11.9 us
    all_to_all x1, waiting for transfers between devices, on_device(): lax.all_to_all(mirror.reshape(32, 16, 128), COL, split_axis=0, concat_axi...  10.9 us
    ppermute x1, starting transfers between devices, on_device(): right = lax.ppermute(ahead[4:], ('zl', 'zh'), cross(4, -1))  9.61 us
    all_to_all x1, starting transfers between devices, on_device(): near = lax.all_to_all(second, 'y', split_axis=0, concat_axis=0)  7.66 us
  transfers between devices with their start and end apart: 15, of which 6 were waited for; matrix products, arithmetic and copies ran while one was open for 0% of the time, Pallas kernels for 3%

profile of v9, /device:TPU:1, one launch (start us, length us, event | category | flops | bytes accessed | tf_op | source)
XLA Modules:
  0.0 172.4 jit_solution(12675056229272296826)
XLA Ops:
  0.0 2.7 %shard_map.55 = (bf16[10,64,128]{2,1,0:T(8,128)(2,1)}, bf16[8,6,64,128]{3,2,1,0:T(8,128)(2,1)}) custom-call(s32[16,16]{1,0:T(8,128)} %mask_ref.2, bf16[8,64,128]{2,1,0:T(8,128)(2,1)} %amps_ref.1, bf16[8,64,2048]{2,1,0:T(8,128)(2,1)} %own_ref.5), custom_call_target="tpu_custom_call" | custom-call | tf_op jit(solution)/shard_map/pallas_call | solution.py:62
  2.7 7.7 %all-to-all-start = ((bf16[8,6,64,128]{3,2,1,0:T(8,128)(2,1)}), bf16[8,6,64,128]{3,2,1,0:T(8,128)(2,1)S(1)}, u32[]{:S(2)}, u32[]{:S(2)}) async-start(bf16[8,6,64,128]{3,2,1,0:T(8,128)(2,1)} %get-tuple-element.9), calls=%async_computation | async-start | bytes 1572864 | tf_op jit(solution)/shard_map/all_to_all | solution.py:395
  10.4 21.6 %all-gather = bf16[40,64,128]{2,1,0:T(8,128)(2,1)S(1)} all-gather(bf16[10,64,128]{2,1,0:T(8,128)(2,1)} %get-tuple-element.10), channel_id=2, replica_groups=mesh['zl'=2,'x'=4,'core'=2,'zh'=4,'y'=8] {'zh'}, dimensions={0}, use_global_device_ids=true | all-gather | bytes 819200 | tf_op jit(solution)/shard_map/all_gather | solution.py:396
  32.0 0.0 all-to-all-done.near_ref.other_ref
  32.0 2.3 %collective-permute-start.5 = (bf16[4,10,64,128]{3,2,1,0:T(8,128)(2,1)S(1)}, bf16[4,10,64,128]{3,2,1,0:T(8,128)(2,1)S(1)}, u32[]{:S(2)}, u32[]{:S(2)}) collective-permute-start(bf16[4,10,64,128]{3,2,1,0:T(8,128)(2,1)S(1)} %shard_map.58.refs_0_), channel_id=1, source_target_pairs={{0,7},{1,0},{2,1},{3,2},{4,3},{5,4},{6,5},{7,6},{32,33},{33,34},{3... | collective-permute-start | bytes 1966088 | tf_op jit(solution)/shard_map/ppermute | solution.py:407
  34.3 4.2 %collective-permute-start.4 = (bf16[4,10,64,128]{3,2,1,0:T(8,128)(2,1)S(1)}, bf16[4,10,64,128]{3,2,1,0:T(8,128)(2,1)S(1)}, u32[]{:S(2)}, u32[]{:S(2)}) collective-permute-start(bf16[4,10,64,128]{3,2,1,0:T(8,128)(2,1)S(1)} %shard_map.58.refs_0_), channel_id=1, source_target_pairs={{0,1},{1,2},{2,3},{3,4},{4,5},{5,6},{6,7},{7,0},{32,39},{33,32},{3... | collective-permute-start | bytes 1966088 | tf_op jit(solution)/shard_map/ppermute | solution.py:406
  38.5 12.7 %collective-permute-start.2 = (bf16[8,6,64,128]{3,2,1,0:T(8,128)(2,1)S(1)}, bf16[8,6,64,128]{3,2,1,0:T(8,128)(2,1)S(1)}, u32[]{:S(2)}, u32[]{:S(2)}) collective-permute-start(bf16[8,6,64,128]{3,2,1,0:T(8,128)(2,1)S(1)} %all-to-all-done.near_ref.other_ref), channel_id=1, source_target_pairs={{0,24},{8,0},{16,8},{24,16},{256,264},{264,272},{272,280},{280,256... | collective-permute-start | bytes 2359304 | tf_op jit(solution)/shard_map/ppermute | solution.py:399
  51.1 0.0 collective-permute-done.5.refs_2_
  51.2 1.9 %collective-permute-start.7 = (bf16[4,10,64,128]{3,2,1,0:T(8,128)(2,1)S(1)}, bf16[4,10,64,128]{3,2,1,0:T(8,128)(2,1)S(1)}, u32[]{:S(2)}, u32[]{:S(2)}) collective-permute-start(bf16[4,10,64,128]{3,2,1,0:T(8,128)(2,1)S(1)} %collective-permute-done.5.refs_2_), channel_id=1, source_target_pairs={{0,7},{1,0},{2,1},{3,2},{4,3},{5,4},{6,5},{7,6},{32,33},{33,34},{3... | collective-permute-start | bytes 1966088 | tf_op jit(solution)/shard_map/ppermute | solution.py:407
  53.1 0.0 collective-permute-done.4.refs_1_
  53.1 4.6 %collective-permute-start.6 = (bf16[4,10,64,128]{3,2,1,0:T(8,128)(2,1)S(1)}, bf16[4,10,64,128]{3,2,1,0:T(8,128)(2,1)S(1)}, u32[]{:S(2)}, u32[]{:S(2)}) collective-permute-start(bf16[4,10,64,128]{3,2,1,0:T(8,128)(2,1)S(1)} %collective-permute-done.4.refs_1_), channel_id=1, source_target_pairs={{0,1},{1,2},{2,3},{3,4},{4,5},{5,6},{6,7},{7,0},{32,39},{33,32},{3... | collective-permute-start | bytes 1966088 | tf_op jit(solution)/shard_map/ppermute | solution.py:406
  57.7 6.4 %collective-permute-start = (bf16[8,6,64,128]{3,2,1,0:T(8,128)(2,1)S(1)}, bf16[8,6,64,128]{3,2,1,0:T(8,128)(2,1)S(1)}, u32[]{:S(2)}, u32[]{:S(2)}) collective-permute-start(bf16[8,6,64,128]{3,2,1,0:T(8,128)(2,1)S(1)} %all-to-all-done.near_ref.other_ref), channel_id=1, source_target_pairs={{0,8},{8,16},{16,24},{24,0},{256,280},{264,256},{272,264},{280,272... | collective-permute-start | bytes 2359304 | tf_op jit(solution)/shard_map/ppermute | solution.py:398
  64.1 0.0 collective-permute-done.7.refs_4_
  64.1 1.9 %collective-permute-start.9 = (bf16[4,10,64,128]{3,2,1,0:T(8,128)(2,1)S(1)}, bf16[4,10,64,128]{3,2,1,0:T(8,128)(2,1)S(1)}, u32[]{:S(2)}, u32[]{:S(2)}) collective-permute-start(bf16[4,10,64,128]{3,2,1,0:T(8,128)(2,1)S(1)} %collective-permute-done.7.refs_4_), channel_id=1, source_target_pairs={{0,7},{1,0},{2,1},{3,2},{4,3},{5,4},{6,5},{7,6},{32,33},{33,34},{3... | collective-permute-start | bytes 1966088 | tf_op jit(solution)/shard_map/ppermute | solution.py:407
  66.0 2.2 %collective-permute-done.2.ahead_ref.other_ref = bf16[8,6,64,128]{3,2,1,0:T(8,128)(2,1)S(1)} collective-permute-done((bf16[8,6,64,128]{3,2,1,0:T(8,128)(2,1)S(1)}, bf16[8,6,64,128]{3,2,1,0:T(8,128)(2,1)S(1)}, u32[]{:S(2)}, u32[]{:S(2)}) %collective-permute-start.2) | collective-permute-done | bytes 786464 | tf_op jit(solution)/shard_map/ppermute | solution.py:399
  68.2 2.9 %collective-permute-done.6.held_ref = bf16[4,10,64,128]{3,2,1,0:T(8,128)(2,1)S(1)} collective-permute-done((bf16[4,10,64,128]{3,2,1,0:T(8,128)(2,1)S(1)}, bf16[4,10,64,128]{3,2,1,0:T(8,128)(2,1)S(1)}, u32[]{:S(2)}, u32[]{:S(2)}) %collective-permute-start.6) | collective-permute-done | bytes 655392 | tf_op jit(solution)/shard_map/ppermute | solution.py:406
  71.0 4.9 %collective-permute-start.8 = (bf16[4,10,64,128]{3,2,1,0:T(8,128)(2,1)S(1)}, bf16[4,10,64,128]{3,2,1,0:T(8,128)(2,1)S(1)}, u32[]{:S(2)}, u32[]{:S(2)}) collective-permute-start(bf16[4,10,64,128]{3,2,1,0:T(8,128)(2,1)S(1)} %shard_map.59.refs_3_), channel_id=1, source_target_pairs={{0,1},{1,2},{2,3},{3,4},{4,5},{5,6},{6,7},{7,0},{32,39},{33,32},{3... | collective-permute-start | bytes 1966088 | tf_op jit(solution)/shard_map/ppermute | solution.py:406
  76.0 0.0 copy-start
  76.0 9.6 %collective-permute-start.3 = (bf16[4,6,64,128]{3,2,1,0:T(8,128)(2,1)S(1)}, bf16[4,6,64,128]{3,2,1,0:T(8,128)(2,1)S(1)}, u32[]{:S(2)}, u32[]{:S(2)}) collective-permute-start(bf16[4,6,64,128]{3,2,1,0:T(8,128)(2,1)S(1)} %slice.17), channel_id=1, source_target_pairs={{0,24},{8,0},{16,8},{24,16},{256,264},{264,272},{272,280},{280,256... | collective-permute-start | bytes 1179656 | tf_op jit(solution)/shard_map/ppermute | solution.py:401
  85.6 2.4 %collective-permute-done.back_ref.other_ref = bf16[8,6,64,128]{3,2,1,0:T(8,128)(2,1)S(1)} collective-permute-done((bf16[8,6,64,128]{3,2,1,0:T(8,128)(2,1)S(1)}, bf16[8,6,64,128]{3,2,1,0:T(8,128)(2,1)S(1)}, u32[]{:S(2)}, u32[]{:S(2)}) %collective-permute-start) | collective-permute-done | bytes 786464 | tf_op jit(solution)/shard_map/ppermute | solution.py:398
  88.1 1.9 %collective-permute-start.1 = (bf16[4,6,64,128]{3,2,1,0:T(8,128)(2,1)S(1)}, bf16[4,6,64,128]{3,2,1,0:T(8,128)(2,1)S(1)}, u32[]{:S(2)}, u32[]{:S(2)}) collective-permute-start(bf16[4,6,64,128]{3,2,1,0:T(8,128)(2,1)S(1)} %slice.16), channel_id=1, source_target_pairs={{0,8},{8,16},{16,24},{24,0},{256,280},{264,256},{272,264},{280,272... | collective-permute-start | bytes 1179656 | tf_op jit(solution)/shard_map/ppermute | solution.py:400
  90.0 0.0 collective-permute-done.9.refs_6_
  90.1 1.9 %collective-permute-start.11 = (bf16[2,10,64,128]{3,2,1,0:T(8,128)(2,1)S(1)}, bf16[2,10,64,128]{3,2,1,0:T(8,128)(2,1)S(1)}, u32[]{:S(2)}, u32[]{:S(2)}) collective-permute-start(bf16[2,10,64,128]{3,2,1,0:T(8,128)(2,1)S(1)} %slice.19), channel_id=1, source_target_pairs={{0,7},{1,0},{2,1},{3,2},{4,3},{5,4},{6,5},{7,6},{32,33},{33,34},{3... | collective-permute-start | bytes 983048 | tf_op jit(solution)/shard_map/ppermute | solution.py:414
  92.0 0.0 collective-permute-done.8.held_ref
  92.0 4.6 %collective-permute-start.10 = (bf16[2,10,64,128]{3,2,1,0:T(8,128)(2,1)S(1)}, bf16[2,10,64,128]{3,2,1,0:T(8,128)(2,1)S(1)}, u32[]{:S(2)}, u32[]{:S(2)}) collective-permute-start(bf16[2,10,64,128]{3,2,1,0:T(8,128)(2,1)S(1)} %slice.18), channel_id=1, source_target_pairs={{0,1},{1,2},{2,3},{3,4},{4,5},{5,6},{6,7},{7,0},{32,39},{33,32},{3... | collective-permute-start | bytes 983048 | tf_op jit(solution)/shard_map/ppermute | solution.py:413
  96.6 0.0 copy-done
  96.6 2.1 %shard_map.56.early_ref = f32[512,768]{1,0:T(8,128)S(1)} custom-call(bf16[8,64,2048]{2,1,0:T(8,128)(2,1)S(1)} %copy-done, bf16[8,6,64,128]{3,2,1,0:T(8,128)(2,1)S(1)} %all-to-all-done.near_ref.other_ref, bf16[8,6,64,128]{3,2,1,0:T(8,128)(2,1)S(1)} %collective-permute-done.back_ref.other_ref, ...), custom_call_target="tpu_custom_call" | custom-call | tf_op jit(solution)/shard_map/pallas_call | solution.py:128
  98.7 0.0 collective-permute-done.3.right_ref
  98.7 7.5 %collective-permute-done.1.left_ref = bf16[4,6,64,128]{3,2,1,0:T(8,128)(2,1)S(1)} collective-permute-done((bf16[4,6,64,128]{3,2,1,0:T(8,128)(2,1)S(1)}, bf16[4,6,64,128]{3,2,1,0:T(8,128)(2,1)S(1)}, u32[]{:S(2)}, u32[]{:S(2)}) %collective-permute-start.1) | collective-permute-done | bytes 393248 | tf_op jit(solution)/shard_map/ppermute | solution.py:400
  106.2 0.7 shard_map.57.held_ref
  106.9 0.0 collective-permute-done.11.refs_8_
  106.9 0.0 collective-permute-done.10.refs_7_
  106.9 1.3 shard_map.61.inner_ref
  108.2 2.0 %shard_map.63 = bf16[1024,512]{1,0:T(8,128)(2,1)S(1)} custom-call(bf16[1024,512]{1,0:T(8,128)(2,1)S(1)} %shard_map.61.inner_ref, bf16[4,10,64,128]{3,2,1,0:T(8,128)(2,1)S(1)} %shard_map.58.refs_0_, bf16[4,10,64,128]{3,2,1,0:T(8,128)(2,1)S(1)} %collective-permute-done.4.refs_1_, bf16[4,10,64,128]{3,2,1,0:T(8,128)(2,1)S(1)} %collective-permute-done.5.refs_2_, ...), custom_call_target="tpu_custom_call" | custom-call | tf_op jit(solution)/shard_map/pallas_call | solution.py:233
  110.2 2.4 %collective-permute-start.12 = (bf16[1024,512]{1,0:T(8,128)(2,1)S(1)}, bf16[1024,512]{1,0:T(8,128)(2,1)S(1)}, u32[]{:S(2)}, u32[]{:S(2)}) collective-permute-start(bf16[1024,512]{1,0:T(8,128)(2,1)S(1)} %shard_map.63), channel_id=1, source_target_pairs={{0,32},{32,0},{1,33},{33,1},{2,34},{34,2},{3,35},{35,3},{4,36},{36... | collective-permute-start | bytes 3145736 | tf_op jit(solution)/shard_map/ppermute | solution.py:419
  112.6 2.0 %shard_map.62.keep_ref = f32[1024,512]{1,0:T(8,128)S(1)} custom-call(bf16[1024,512]{1,0:T(8,128)(2,1)S(1)} %shard_map.61.inner_ref, bf16[4,10,64,128]{3,2,1,0:T(8,128)(2,1)S(1)} %shard_map.58.refs_0_, bf16[4,10,64,128]{3,2,1,0:T(8,128)(2,1)S(1)} %collective-permute-done.4.refs_1_, bf16[4,10,64,128]{3,2,1,0:T(8,128)(2,1)S(1)} %collective-permute-done.5.refs_2_, ...), custom_call_target="tpu_custom_call" | custom-call | tf_op jit(solution)/shard_map/pallas_call | solution.py:233
  114.6 0.0 copy-start.1
  114.6 0.3 collective-permute-done.12.other_ref
  114.9 1.1 shard_map.64
  115.9 0.0 copy-start.2
  116.0 26.0 %all_to_all.20.part_ref = bf16[8,128,512]{2,1,0:T(8,128)(2,1)S(1)} all-to-all(bf16[8,128,512]{2,1,0:T(8,128)(2,1)S(1)} %shard_map.64), channel_id=1, replica_groups=mesh['zl'=2,'x'=4,'core'=2,'zh'=4,'y'=8] {'zl','x'}, dimensions={0} | all-to-all | bytes 2097152 | tf_op jit(solution)/shard_map/all_to_all | solution.py:422
  142.0 0.0 copy-done.1
  142.0 1.5 shard_map.65
  143.5 11.9 %all_to_all.21.direct_ref = f32[16,32,128]{2,1,0:T(8,128)S(1)} all-to-all(f32[16,32,128]{2,1,0:T(8,128)S(1)} %bitcast.4), channel_id=1, replica_groups=mesh['zl'=2,'x'=4,'core'=2,'zh'=4,'y'=8] {'zl','x','core'}, dimensions={0} | all-to-all | bytes 524288 | tf_op jit(solution)/shard_map/all_to_all | solution.py:425
  155.4 3.9 %all-to-all-start.3 = ((bf16[32,16,128]{2,1,0:T(8,128)(2,1)}), bf16[32,16,128]{2,1,0:T(8,128)(2,1)S(1)}, u32[]{:S(2)}, u32[]{:S(2)}) async-start(bf16[32,16,128]{2,1,0:T(8,128)(2,1)} %bitcast.2), calls=%async_computation.3 | async-start | bytes 262144 | tf_op jit(solution)/shard_map/all_to_all | solution.py:424
  159.3 0.7 shard_map.66.direct_ref
  159.9 10.9 %all-to-all-done.3.mirror_ref = bf16[32,16,128]{2,1,0:T(8,128)(2,1)S(1)} async-done(((bf16[32,16,128]{2,1,0:T(8,128)(2,1)}), bf16[32,16,128]{2,1,0:T(8,128)(2,1)S(1)}, u32[]{:S(2)}, u32[]{:S(2)}) %all-to-all-start.3) | async-done | bytes 131104 | tf_op jit(solution)/shard_map/all_to_all | solution.py:424
  170.8 1.6 shard_map.67
  (8 shorter events, 0.1 us)
Async XLA Ops:
  2.7 29.2 %all-to-all-start = ((bf16[8,6,64,128]{3,2,1,0:T(8,128)(2,1)}), bf16[8,6,64,128]{3,2,1,0:T(8,128)(2,1)S(1)}, u32[]{:S(2)}, u32[]{:S(2)}) async-start(bf16[8,6,64,128]{3,2,1,0:T(8,128)(2,1)} %get-tuple-element.9), calls=%async_computation | async-start | bytes 1572864 | tf_op jit(solution)/shard_map/all_to_all | solution.py:395
  32.0 19.2 %collective-permute-start.5 = (bf16[4,10,64,128]{3,2,1,0:T(8,128)(2,1)S(1)}, bf16[4,10,64,128]{3,2,1,0:T(8,128)(2,1)S(1)}, u32[]{:S(2)}, u32[]{:S(2)}) collective-permute-start(bf16[4,10,64,128]{3,2,1,0:T(8,128)(2,1)S(1)} %shard_map.58.refs_0_), channel_id=1, source_target_pairs={{0,7},{1,0},{2,1},{3,2},{4,3},{5,4},{6,5},{7,6},{32,33},{33,34},{3... | collective-permute-start | bytes 1966088 | tf_op jit(solution)/shard_map/ppermute | solution.py:407
  34.3 18.8 %collective-permute-start.4 = (bf16[4,10,64,128]{3,2,1,0:T(8,128)(2,1)S(1)}, bf16[4,10,64,128]{3,2,1,0:T(8,128)(2,1)S(1)}, u32[]{:S(2)}, u32[]{:S(2)}) collective-permute-start(bf16[4,10,64,128]{3,2,1,0:T(8,128)(2,1)S(1)} %shard_map.58.refs_0_), channel_id=1, source_target_pairs={{0,1},{1,2},{2,3},{3,4},{4,5},{5,6},{6,7},{7,0},{32,39},{33,32},{3... | collective-permute-start | bytes 1966088 | tf_op jit(solution)/shard_map/ppermute | solution.py:406
  38.5 29.7 %collective-permute-start.2 = (bf16[8,6,64,128]{3,2,1,0:T(8,128)(2,1)S(1)}, bf16[8,6,64,128]{3,2,1,0:T(8,128)(2,1)S(1)}, u32[]{:S(2)}, u32[]{:S(2)}) collective-permute-start(bf16[8,6,64,128]{3,2,1,0:T(8,128)(2,1)S(1)} %all-to-all-done.near_ref.other_ref), channel_id=1, source_target_pairs={{0,24},{8,0},{16,8},{24,16},{256,264},{264,272},{272,280},{280,256... | collective-permute-start | bytes 2359304 | tf_op jit(solution)/shard_map/ppermute | solution.py:399
  51.2 12.9 %collective-permute-start.7 = (bf16[4,10,64,128]{3,2,1,0:T(8,128)(2,1)S(1)}, bf16[4,10,64,128]{3,2,1,0:T(8,128)(2,1)S(1)}, u32[]{:S(2)}, u32[]{:S(2)}) collective-permute-start(bf16[4,10,64,128]{3,2,1,0:T(8,128)(2,1)S(1)} %collective-permute-done.5.refs_2_), channel_id=1, source_target_pairs={{0,7},{1,0},{2,1},{3,2},{4,3},{5,4},{6,5},{7,6},{32,33},{33,34},{3... | collective-permute-start | bytes 1966088 | tf_op jit(solution)/shard_map/ppermute | solution.py:407
  53.1 17.9 %collective-permute-start.6 = (bf16[4,10,64,128]{3,2,1,0:T(8,128)(2,1)S(1)}, bf16[4,10,64,128]{3,2,1,0:T(8,128)(2,1)S(1)}, u32[]{:S(2)}, u32[]{:S(2)}) collective-permute-start(bf16[4,10,64,128]{3,2,1,0:T(8,128)(2,1)S(1)} %collective-permute-done.4.refs_1_), channel_id=1, source_target_pairs={{0,1},{1,2},{2,3},{3,4},{4,5},{5,6},{6,7},{7,0},{32,39},{33,32},{3... | collective-permute-start | bytes 1966088 | tf_op jit(solution)/shard_map/ppermute | solution.py:406
  57.7 30.4 %collective-permute-start = (bf16[8,6,64,128]{3,2,1,0:T(8,128)(2,1)S(1)}, bf16[8,6,64,128]{3,2,1,0:T(8,128)(2,1)S(1)}, u32[]{:S(2)}, u32[]{:S(2)}) collective-permute-start(bf16[8,6,64,128]{3,2,1,0:T(8,128)(2,1)S(1)} %all-to-all-done.near_ref.other_ref), channel_id=1, source_target_pairs={{0,8},{8,16},{16,24},{24,0},{256,280},{264,256},{272,264},{280,272... | collective-permute-start | bytes 2359304 | tf_op jit(solution)/shard_map/ppermute | solution.py:398
  64.1 25.9 %collective-permute-start.9 = (bf16[4,10,64,128]{3,2,1,0:T(8,128)(2,1)S(1)}, bf16[4,10,64,128]{3,2,1,0:T(8,128)(2,1)S(1)}, u32[]{:S(2)}, u32[]{:S(2)}) collective-permute-start(bf16[4,10,64,128]{3,2,1,0:T(8,128)(2,1)S(1)} %collective-permute-done.7.refs_4_), channel_id=1, source_target_pairs={{0,7},{1,0},{2,1},{3,2},{4,3},{5,4},{6,5},{7,6},{32,33},{33,34},{3... | collective-permute-start | bytes 1966088 | tf_op jit(solution)/shard_map/ppermute | solution.py:407
  71.0 21.0 %collective-permute-start.8 = (bf16[4,10,64,128]{3,2,1,0:T(8,128)(2,1)S(1)}, bf16[4,10,64,128]{3,2,1,0:T(8,128)(2,1)S(1)}, u32[]{:S(2)}, u32[]{:S(2)}) collective-permute-start(bf16[4,10,64,128]{3,2,1,0:T(8,128)(2,1)S(1)} %shard_map.59.refs_3_), channel_id=1, source_target_pairs={{0,1},{1,2},{2,3},{3,4},{4,5},{5,6},{6,7},{7,0},{32,39},{33,32},{3... | collective-permute-start | bytes 1966088 | tf_op jit(solution)/shard_map/ppermute | solution.py:406
  76.0 20.6 %copy-start = (bf16[8,64,2048]{2,1,0:T(8,128)(2,1)S(1)}, bf16[8,64,2048]{2,1,0:T(8,128)(2,1)}, u32[]{:S(2)}) copy-start(bf16[8,64,2048]{2,1,0:T(8,128)(2,1)} %own_ref.5) | copy-start | bytes 6291460
  76.0 22.7 %collective-permute-start.3 = (bf16[4,6,64,128]{3,2,1,0:T(8,128)(2,1)S(1)}, bf16[4,6,64,128]{3,2,1,0:T(8,128)(2,1)S(1)}, u32[]{:S(2)}, u32[]{:S(2)}) collective-permute-start(bf16[4,6,64,128]{3,2,1,0:T(8,128)(2,1)S(1)} %slice.17), channel_id=1, source_target_pairs={{0,24},{8,0},{16,8},{24,16},{256,264},{264,272},{272,280},{280,256... | collective-permute-start | bytes 1179656 | tf_op jit(solution)/shard_map/ppermute | solution.py:401
  88.1 18.1 %collective-permute-start.1 = (bf16[4,6,64,128]{3,2,1,0:T(8,128)(2,1)S(1)}, bf16[4,6,64,128]{3,2,1,0:T(8,128)(2,1)S(1)}, u32[]{:S(2)}, u32[]{:S(2)}) collective-permute-start(bf16[4,6,64,128]{3,2,1,0:T(8,128)(2,1)S(1)} %slice.16), channel_id=1, source_target_pairs={{0,8},{8,16},{16,24},{24,0},{256,280},{264,256},{272,264},{280,272... | collective-permute-start | bytes 1179656 | tf_op jit(solution)/shard_map/ppermute | solution.py:400
  90.1 16.8 %collective-permute-start.11 = (bf16[2,10,64,128]{3,2,1,0:T(8,128)(2,1)S(1)}, bf16[2,10,64,128]{3,2,1,0:T(8,128)(2,1)S(1)}, u32[]{:S(2)}, u32[]{:S(2)}) collective-permute-start(bf16[2,10,64,128]{3,2,1,0:T(8,128)(2,1)S(1)} %slice.19), channel_id=1, source_target_pairs={{0,7},{1,0},{2,1},{3,2},{4,3},{5,4},{6,5},{7,6},{32,33},{33,34},{3... | collective-permute-start | bytes 983048 | tf_op jit(solution)/shard_map/ppermute | solution.py:414
  92.0 14.8 %collective-permute-start.10 = (bf16[2,10,64,128]{3,2,1,0:T(8,128)(2,1)S(1)}, bf16[2,10,64,128]{3,2,1,0:T(8,128)(2,1)S(1)}, u32[]{:S(2)}, u32[]{:S(2)}) collective-permute-start(bf16[2,10,64,128]{3,2,1,0:T(8,128)(2,1)S(1)} %slice.18), channel_id=1, source_target_pairs={{0,1},{1,2},{2,3},{3,4},{4,5},{5,6},{6,7},{7,0},{32,39},{33,32},{3... | collective-permute-start | bytes 983048 | tf_op jit(solution)/shard_map/ppermute | solution.py:413
  110.2 4.7 %collective-permute-start.12 = (bf16[1024,512]{1,0:T(8,128)(2,1)S(1)}, bf16[1024,512]{1,0:T(8,128)(2,1)S(1)}, u32[]{:S(2)}, u32[]{:S(2)}) collective-permute-start(bf16[1024,512]{1,0:T(8,128)(2,1)S(1)} %shard_map.63), channel_id=1, source_target_pairs={{0,32},{32,0},{1,33},{33,1},{2,34},{34,2},{3,35},{35,3},{4,36},{36... | collective-permute-start | bytes 3145736 | tf_op jit(solution)/shard_map/ppermute | solution.py:419
  114.6 27.4 %copy-start.1 = (s32[16,16]{1,0:T(8,128)S(1)}, s32[16,16]{1,0:T(8,128)}, u32[]{:S(2)}) copy-start(s32[16,16]{1,0:T(8,128)} %mask_ref.3) | copy-start | bytes 3076
  115.9 54.9 %copy-start.2 = (s32[8]{0:T(128)S(1)}, s32[8]{0:T(128)}, u32[]{:S(2)}) copy-start(s32[8]{0:T(128)} %partner_ref.1) | copy-start | bytes 100
  155.4 15.4 %all-to-all-start.3 = ((bf16[32,16,128]{2,1,0:T(8,128)(2,1)}), bf16[32,16,128]{2,1,0:T(8,128)(2,1)S(1)}, u32[]{:S(2)}, u32[]{:S(2)}) async-start(bf16[32,16,128]{2,1,0:T(8,128)(2,1)} %bitcast.2), calls=%async_computation.3 | async-start | bytes 262144 | tf_op jit(solution)/shard_map/all_to_all | solution.py:424

commit v10 on v9

--- a/solution.py
+++ b/solution.py
@@ -116,7 +116,7 @@
 
 
 def early_kernel(own_ref, near_ref, back_ref, ahead_ref, out_ref):
-    step = 1 + 2 * lax.axis_index("zl")
+    step = 1 + 2 * lax.axis_index("core")
     product = ring_term(own_ref, [near_ref], 0)
     product = product + ring_term(own_ref, [back_ref], 4 - step)
     out_ref[...] = product + ring_term(own_ref, [ahead_ref], step)
@@ -395,10 +395,10 @@
     near = lax.all_to_all(second, "y", split_axis=0, concat_axis=0)
     held = gate_call(lax.all_gather(first, "zh", axis=0), near)
 
-    back = lax.ppermute(near, ("zl", "zh"), cross(4, 1))
-    ahead = lax.ppermute(near, ("zl", "zh"), cross(4, -1))
-    left = lax.ppermute(back[:4], ("zl", "zh"), cross(4, 1))
-    right = lax.ppermute(ahead[4:], ("zl", "zh"), cross(4, -1))
+    back = lax.ppermute(near, ("core", "zh"), cross(4, 1))
+    ahead = lax.ppermute(near, ("core", "zh"), cross(4, -1))
+    left = lax.ppermute(back[:4], ("core", "zh"), cross(4, 1))
+    right = lax.ppermute(ahead[4:], ("core", "zh"), cross(4, -1))
 
     up, down = held, held
     units = [held]

time: 173 us -> 173 us (level)
  starting transfers between devices: 70.8 us -> 78.3 us
  blocking collectives: 59.5 us -> 53.6 us
  waiting for transfers between devices: 26.1 us -> 24.1 us
    all_to_all x1, blocking collectives: 26 us -> 20.1 us  [on_device(): pieces = lax.all_to_all(partial, ('zl', 'x'), split_axis=0, concat_axis=0)]
    all_to_all x1, starting transfers between devices: 3.86 us -> 8.53 us  [on_device(): lax.all_to_all(mirror.reshape(32, 16, 128), COL, split_axis=0, concat_axi...]
    ppermute x4, waiting for transfers between devices: 12.1 us -> 8.78 us  [the longest x1 4.1 us: on_device(): back = lax.ppermute(near, ('core', 'zh'), cross(4, 1))]
    ppermute x4, starting transfers between devices: 30.6 us -> 32.4 us  [the longest x1 10.7 us: on_device(): back = lax.ppermute(near, ('core', 'zh'), cross(4, 1))]
  transfers between devices with their start and end apart: 15 -> 15, of which waited for: 6 -> 7; matrix products, arithmetic and copies ran while one was open for 0% -> 0% of each run, Pallas kernels for 3% -> 3%
where the time goes in v10:
time: 173 us; the launch traced here: 172 us
  starting transfers between devices  78.3 us (45%)
  blocking collectives  53.6 us (31%)
  waiting for transfers between devices  24.1 us (14%)
  Pallas kernels  15.5 us (9%)
    all_gather x1, blocking collectives, on_device(): held = gate_call(lax.all_gather(first, 'zh', axis=0), near)  21.6 us
    all_to_all x1, blocking collectives, on_device(): pieces = lax.all_to_all(partial, ('zl', 'x'), split_axis=0, concat_axis=0)  20.1 us
    ppermute x3, starting transfers between devices, on_device(): up = lax.ppermute(up, ('core', 'y'), cross(8, 1))  14.6 us
    all_to_all x1, blocking collectives, on_device(): lax.all_to_all(direct.reshape(16, 32, 128), ROW, split_axis=0, concat_axi...  11.9 us
    all_to_all x1, waiting for transfers between devices, on_device(): lax.all_to_all(mirror.reshape(32, 16, 128), COL, split_axis=0, concat_axi...  10.9 us
    ppermute x1, starting transfers between devices, on_device(): back = lax.ppermute(near, ('core', 'zh'), cross(4, 1))  10.7 us
    all_to_all x1, starting transfers between devices, on_device(): lax.all_to_all(mirror.reshape(32, 16, 128), COL, split_axis=0, concat_axi...  8.53 us
    ppermute x1, starting transfers between devices, on_device(): right = lax.ppermute(ahead[4:], ('core', 'zh'), cross(4, -1))  8.03 us
  transfers between devices with their start and end apart: 15, of which 7 were waited for; matrix products, arithmetic and copies ran while one was open for 0% of the time, Pallas kernels for 3%

profile of v10, /device:TPU:1, one launch (start us, length us, event | category | flops | bytes accessed | tf_op | source)
XLA Modules:
  0.0 172.0 jit_solution(6498453291725559458)
XLA Ops:
  0.0 2.7 %shard_map.55 = (bf16[10,64,128]{2,1,0:T(8,128)(2,1)}, bf16[8,6,64,128]{3,2,1,0:T(8,128)(2,1)}) custom-call(s32[16,16]{1,0:T(8,128)} %mask_ref.2, bf16[8,64,128]{2,1,0:T(8,128)(2,1)} %amps_ref.1, bf16[8,64,2048]{2,1,0:T(8,128)(2,1)} %own_ref.5), custom_call_target="tpu_custom_call" | custom-call | tf_op jit(solution)/shard_map/pallas_call | solution.py:62
  2.7 7.7 %all-to-all-start = ((bf16[8,6,64,128]{3,2,1,0:T(8,128)(2,1)}), bf16[8,6,64,128]{3,2,1,0:T(8,128)(2,1)S(1)}, u32[]{:S(2)}, u32[]{:S(2)}) async-start(bf16[8,6,64,128]{3,2,1,0:T(8,128)(2,1)} %get-tuple-element.9), calls=%async_computation | async-start | bytes 1572864 | tf_op jit(solution)/shard_map/all_to_all | solution.py:395
  10.4 21.6 %all-gather = bf16[40,64,128]{2,1,0:T(8,128)(2,1)S(1)} all-gather(bf16[10,64,128]{2,1,0:T(8,128)(2,1)} %get-tuple-element.10), channel_id=2, replica_groups=mesh['zl'=2,'x'=4,'core'=2,'zh'=4,'y'=8] {'zh'}, dimensions={0}, use_global_device_ids=true | all-gather | bytes 819200 | tf_op jit(solution)/shard_map/all_gather | solution.py:396
  32.0 0.0 all-to-all-done.near_ref.other_ref
  32.0 2.3 %collective-permute-start.5 = (bf16[4,10,64,128]{3,2,1,0:T(8,128)(2,1)S(1)}, bf16[4,10,64,128]{3,2,1,0:T(8,128)(2,1)S(1)}, u32[]{:S(2)}, u32[]{:S(2)}) collective-permute-start(bf16[4,10,64,128]{3,2,1,0:T(8,128)(2,1)S(1)} %shard_map.58.refs_0_), channel_id=1, source_target_pairs={{0,7},{1,0},{2,1},{3,2},{4,3},{5,4},{6,5},{7,6},{32,33},{33,34},{3... | collective-permute-start | bytes 1966088 | tf_op jit(solution)/shard_map/ppermute | solution.py:407
  34.3 4.2 %collective-permute-start.4 = (bf16[4,10,64,128]{3,2,1,0:T(8,128)(2,1)S(1)}, bf16[4,10,64,128]{3,2,1,0:T(8,128)(2,1)S(1)}, u32[]{:S(2)}, u32[]{:S(2)}) collective-permute-start(bf16[4,10,64,128]{3,2,1,0:T(8,128)(2,1)S(1)} %shard_map.58.refs_0_), channel_id=1, source_target_pairs={{0,1},{1,2},{2,3},{3,4},{4,5},{5,6},{6,7},{7,0},{32,39},{33,32},{3... | collective-permute-start | bytes 1966088 | tf_op jit(solution)/shard_map/ppermute | solution.py:406
  38.5 7.8 %collective-permute-start.2 = (bf16[8,6,64,128]{3,2,1,0:T(8,128)(2,1)S(1)}, bf16[8,6,64,128]{3,2,1,0:T(8,128)(2,1)S(1)}, u32[]{:S(2)}, u32[]{:S(2)}) collective-permute-start(bf16[8,6,64,128]{3,2,1,0:T(8,128)(2,1)S(1)} %all-to-all-done.near_ref.other_ref), channel_id=1, source_target_pairs={{0,24},{8,0},{16,8},{24,16},{32,40},{40,48},{48,56},{56,32},{1,25}... | collective-permute-start | bytes 2359304 | tf_op jit(solution)/shard_map/ppermute | solution.py:399
  46.3 0.0 collective-permute-done.5.refs_2_
  46.3 1.9 %collective-permute-start.7 = (bf16[4,10,64,128]{3,2,1,0:T(8,128)(2,1)S(1)}, bf16[4,10,64,128]{3,2,1,0:T(8,128)(2,1)S(1)}, u32[]{:S(2)}, u32[]{:S(2)}) collective-permute-start(bf16[4,10,64,128]{3,2,1,0:T(8,128)(2,1)S(1)} %collective-permute-done.5.refs_2_), channel_id=1, source_target_pairs={{0,7},{1,0},{2,1},{3,2},{4,3},{5,4},{6,5},{7,6},{32,33},{33,34},{3... | collective-permute-start | bytes 1966088 | tf_op jit(solution)/shard_map/ppermute | solution.py:407
  48.2 4.1 %collective-permute-done.4.refs_1_ = bf16[4,10,64,128]{3,2,1,0:T(8,128)(2,1)S(1)} collective-permute-done((bf16[4,10,64,128]{3,2,1,0:T(8,128)(2,1)S(1)}, bf16[4,10,64,128]{3,2,1,0:T(8,128)(2,1)S(1)}, u32[]{:S(2)}, u32[]{:S(2)}) %collective-permute-start.4) | collective-permute-done | bytes 655392 | tf_op jit(solution)/shard_map/ppermute | solution.py:406
  52.3 5.1 %collective-permute-start.6 = (bf16[4,10,64,128]{3,2,1,0:T(8,128)(2,1)S(1)}, bf16[4,10,64,128]{3,2,1,0:T(8,128)(2,1)S(1)}, u32[]{:S(2)}, u32[]{:S(2)}) collective-permute-start(bf16[4,10,64,128]{3,2,1,0:T(8,128)(2,1)S(1)} %collective-permute-done.4.refs_1_), channel_id=1, source_target_pairs={{0,1},{1,2},{2,3},{3,4},{4,5},{5,6},{6,7},{7,0},{32,39},{33,32},{3... | collective-permute-start | bytes 1966088 | tf_op jit(solution)/shard_map/ppermute | solution.py:406
  57.4 10.7 %collective-permute-start = (bf16[8,6,64,128]{3,2,1,0:T(8,128)(2,1)S(1)}, bf16[8,6,64,128]{3,2,1,0:T(8,128)(2,1)S(1)}, u32[]{:S(2)}, u32[]{:S(2)}) collective-permute-start(bf16[8,6,64,128]{3,2,1,0:T(8,128)(2,1)S(1)} %all-to-all-done.near_ref.other_ref), channel_id=1, source_target_pairs={{0,8},{8,16},{16,24},{24,0},{32,56},{40,32},{48,40},{56,48},{1,9},... | collective-permute-start | bytes 2359304 | tf_op jit(solution)/shard_map/ppermute | solution.py:398
  68.1 0.0 collective-permute-done.7.refs_4_
  68.1 1.9 %collective-permute-start.9 = (bf16[4,10,64,128]{3,2,1,0:T(8,128)(2,1)S(1)}, bf16[4,10,64,128]{3,2,1,0:T(8,128)(2,1)S(1)}, u32[]{:S(2)}, u32[]{:S(2)}) collective-permute-start(bf16[4,10,64,128]{3,2,1,0:T(8,128)(2,1)S(1)} %collective-permute-done.7.refs_4_), channel_id=1, source_target_pairs={{0,7},{1,0},{2,1},{3,2},{4,3},{5,4},{6,5},{7,6},{32,33},{33,34},{3... | collective-permute-start | bytes 1966088 | tf_op jit(solution)/shard_map/ppermute | solution.py:407
  70.0 0.0 collective-permute-done.2.ahead_ref.other_ref
  70.0 0.1 collective-permute-done.6.held_ref
  70.1 5.3 %collective-permute-start.8 = (bf16[4,10,64,128]{3,2,1,0:T(8,128)(2,1)S(1)}, bf16[4,10,64,128]{3,2,1,0:T(8,128)(2,1)S(1)}, u32[]{:S(2)}, u32[]{:S(2)}) collective-permute-start(bf16[4,10,64,128]{3,2,1,0:T(8,128)(2,1)S(1)} %shard_map.59.refs_3_), channel_id=1, source_target_pairs={{0,1},{1,2},{2,3},{3,4},{4,5},{5,6},{6,7},{7,0},{32,39},{33,32},{3... | collective-permute-start | bytes 1966088 | tf_op jit(solution)/shard_map/ppermute | solution.py:406
  75.4 0.0 copy-start
  75.4 8.0 %collective-permute-start.3 = (bf16[4,6,64,128]{3,2,1,0:T(8,128)(2,1)S(1)}, bf16[4,6,64,128]{3,2,1,0:T(8,128)(2,1)S(1)}, u32[]{:S(2)}, u32[]{:S(2)}) collective-permute-start(bf16[4,6,64,128]{3,2,1,0:T(8,128)(2,1)S(1)} %slice.17), channel_id=1, source_target_pairs={{0,24},{8,0},{16,8},{24,16},{32,40},{40,48},{48,56},{56,32},{1,25}... | collective-permute-start | bytes 1179656 | tf_op jit(solution)/shard_map/ppermute | solution.py:401
  83.5 4.1 %collective-permute-done.back_ref.other_ref = bf16[8,6,64,128]{3,2,1,0:T(8,128)(2,1)S(1)} collective-permute-done((bf16[8,6,64,128]{3,2,1,0:T(8,128)(2,1)S(1)}, bf16[8,6,64,128]{3,2,1,0:T(8,128)(2,1)S(1)}, u32[]{:S(2)}, u32[]{:S(2)}) %collective-permute-start) | collective-permute-done | bytes 786464 | tf_op jit(solution)/shard_map/ppermute | solution.py:398
  87.6 5.9 %collective-permute-start.1 = (bf16[4,6,64,128]{3,2,1,0:T(8,128)(2,1)S(1)}, bf16[4,6,64,128]{3,2,1,0:T(8,128)(2,1)S(1)}, u32[]{:S(2)}, u32[]{:S(2)}) collective-permute-start(bf16[4,6,64,128]{3,2,1,0:T(8,128)(2,1)S(1)} %slice.16), channel_id=1, source_target_pairs={{0,8},{8,16},{16,24},{24,0},{32,56},{40,32},{48,40},{56,48},{1,9},... | collective-permute-start | bytes 1179656 | tf_op jit(solution)/shard_map/ppermute | solution.py:400
  93.5 0.0 collective-permute-done.9.refs_6_
  93.6 2.1 %collective-permute-start.11 = (bf16[2,10,64,128]{3,2,1,0:T(8,128)(2,1)S(1)}, bf16[2,10,64,128]{3,2,1,0:T(8,128)(2,1)S(1)}, u32[]{:S(2)}, u32[]{:S(2)}) collective-permute-start(bf16[2,10,64,128]{3,2,1,0:T(8,128)(2,1)S(1)} %slice.19), channel_id=1, source_target_pairs={{0,7},{1,0},{2,1},{3,2},{4,3},{5,4},{6,5},{7,6},{32,33},{33,34},{3... | collective-permute-start | bytes 983048 | tf_op jit(solution)/shard_map/ppermute | solution.py:414
  95.7 0.0 collective-permute-done.8.held_ref
  95.8 4.4 %collective-permute-start.10 = (bf16[2,10,64,128]{3,2,1,0:T(8,128)(2,1)S(1)}, bf16[2,10,64,128]{3,2,1,0:T(8,128)(2,1)S(1)}, u32[]{:S(2)}, u32[]{:S(2)}) collective-permute-start(bf16[2,10,64,128]{3,2,1,0:T(8,128)(2,1)S(1)} %slice.18), channel_id=1, source_target_pairs={{0,1},{1,2},{2,3},{3,4},{4,5},{5,6},{6,7},{7,0},{32,39},{33,32},{3... | collective-permute-start | bytes 983048 | tf_op jit(solution)/shard_map/ppermute | solution.py:413
  100.1 0.0 copy-done
  100.1 2.1 %shard_map.56.early_ref = f32[512,768]{1,0:T(8,128)S(1)} custom-call(bf16[8,64,2048]{2,1,0:T(8,128)(2,1)S(1)} %copy-done, bf16[8,6,64,128]{3,2,1,0:T(8,128)(2,1)S(1)} %all-to-all-done.near_ref.other_ref, bf16[8,6,64,128]{3,2,1,0:T(8,128)(2,1)S(1)} %collective-permute-done.back_ref.other_ref, ...), custom_call_target="tpu_custom_call" | custom-call | tf_op jit(solution)/shard_map/pallas_call | solution.py:128
  102.2 0.8 collective-permute-done.3.right_ref
  103.0 3.9 %collective-permute-done.1.left_ref = bf16[4,6,64,128]{3,2,1,0:T(8,128)(2,1)S(1)} collective-permute-done((bf16[4,6,64,128]{3,2,1,0:T(8,128)(2,1)S(1)}, bf16[4,6,64,128]{3,2,1,0:T(8,128)(2,1)S(1)}, u32[]{:S(2)}, u32[]{:S(2)}) %collective-permute-start.1) | collective-permute-done | bytes 393248 | tf_op jit(solution)/shard_map/ppermute | solution.py:400
  106.9 0.7 shard_map.57.held_ref
  107.6 0.0 collective-permute-done.11.refs_8_
  107.6 0.0 collective-permute-done.10.refs_7_
  107.6 1.3 shard_map.61.inner_ref
  108.9 2.0 %shard_map.63 = bf16[1024,512]{1,0:T(8,128)(2,1)S(1)} custom-call(bf16[1024,512]{1,0:T(8,128)(2,1)S(1)} %shard_map.61.inner_ref, bf16[4,10,64,128]{3,2,1,0:T(8,128)(2,1)S(1)} %shard_map.58.refs_0_, bf16[4,10,64,128]{3,2,1,0:T(8,128)(2,1)S(1)} %collective-permute-done.4.refs_1_, bf16[4,10,64,128]{3,2,1,0:T(8,128)(2,1)S(1)} %collective-permute-done.5.refs_2_, ...), custom_call_target="tpu_custom_call" | custom-call | tf_op jit(solution)/shard_map/pallas_call | solution.py:233
  110.9 2.5 %collective-permute-start.12 = (bf16[1024,512]{1,0:T(8,128)(2,1)S(1)}, bf16[1024,512]{1,0:T(8,128)(2,1)S(1)}, u32[]{:S(2)}, u32[]{:S(2)}) collective-permute-start(bf16[1024,512]{1,0:T(8,128)(2,1)S(1)} %shard_map.63), channel_id=1, source_target_pairs={{0,32},{32,0},{1,33},{33,1},{2,34},{34,2},{3,35},{35,3},{4,36},{36... | collective-permute-start | bytes 3145736 | tf_op jit(solution)/shard_map/ppermute | solution.py:419
  113.4 2.0 %shard_map.62.keep_ref = f32[1024,512]{1,0:T(8,128)S(1)} custom-call(bf16[1024,512]{1,0:T(8,128)(2,1)S(1)} %shard_map.61.inner_ref, bf16[4,10,64,128]{3,2,1,0:T(8,128)(2,1)S(1)} %shard_map.58.refs_0_, bf16[4,10,64,128]{3,2,1,0:T(8,128)(2,1)S(1)} %collective-permute-done.4.refs_1_, bf16[4,10,64,128]{3,2,1,0:T(8,128)(2,1)S(1)} %collective-permute-done.5.refs_2_, ...), custom_call_target="tpu_custom_call" | custom-call | tf_op jit(solution)/shard_map/pallas_call | solution.py:233
  115.4 0.0 copy-start.1
  115.4 0.3 collective-permute-done.12.other_ref
  115.7 1.1 shard_map.64
  116.8 0.0 copy-start.2
  116.8 20.1 %all_to_all.20.part_ref = bf16[8,128,512]{2,1,0:T(8,128)(2,1)S(1)} all-to-all(bf16[8,128,512]{2,1,0:T(8,128)(2,1)S(1)} %shard_map.64), channel_id=1, replica_groups=mesh['zl'=2,'x'=4,'core'=2,'zh'=4,'y'=8] {'zl','x'}, dimensions={0} | all-to-all | bytes 2097152 | tf_op jit(solution)/shard_map/all_to_all | solution.py:422
  136.9 0.0 copy-done.1
  136.9 1.5 shard_map.65
  138.4 11.9 %all_to_all.21.direct_ref = f32[16,32,128]{2,1,0:T(8,128)S(1)} all-to-all(f32[16,32,128]{2,1,0:T(8,128)S(1)} %bitcast.4), channel_id=1, replica_groups=mesh['zl'=2,'x'=4,'core'=2,'zh'=4,'y'=8] {'zl','x','core'}, dimensions={0} | all-to-all | bytes 524288 | tf_op jit(solution)/shard_map/all_to_all | solution.py:425
  150.3 8.5 %all-to-all-start.3 = ((bf16[32,16,128]{2,1,0:T(8,128)(2,1)}), bf16[32,16,128]{2,1,0:T(8,128)(2,1)S(1)}, u32[]{:S(2)}, u32[]{:S(2)}) async-start(bf16[32,16,128]{2,1,0:T(8,128)(2,1)} %bitcast.2), calls=%async_computation.3 | async-start | bytes 262144 | tf_op jit(solution)/shard_map/all_to_all | solution.py:424
  158.8 0.7 shard_map.66.direct_ref
  159.5 10.9 %all-to-all-done.3.mirror_ref = bf16[32,16,128]{2,1,0:T(8,128)(2,1)S(1)} async-done(((bf16[32,16,128]{2,1,0:T(8,128)(2,1)}), bf16[32,16,128]{2,1,0:T(8,128)(2,1)S(1)}, u32[]{:S(2)}, u32[]{:S(2)}) %all-to-all-start.3) | async-done | bytes 131104 | tf_op jit(solution)/shard_map/all_to_all | solution.py:424
  170.5 1.6 shard_map.67
  (8 shorter events, 0.1 us)
Async XLA Ops:
  2.7 29.2 %all-to-all-start = ((bf16[8,6,64,128]{3,2,1,0:T(8,128)(2,1)}), bf16[8,6,64,128]{3,2,1,0:T(8,128)(2,1)S(1)}, u32[]{:S(2)}, u32[]{:S(2)}) async-start(bf16[8,6,64,128]{3,2,1,0:T(8,128)(2,1)} %get-tuple-element.9), calls=%async_computation | async-start | bytes 1572864 | tf_op jit(solution)/shard_map/all_to_all | solution.py:395
  32.0 14.3 %collective-permute-start.5 = (bf16[4,10,64,128]{3,2,1,0:T(8,128)(2,1)S(1)}, bf16[4,10,64,128]{3,2,1,0:T(8,128)(2,1)S(1)}, u32[]{:S(2)}, u32[]{:S(2)}) collective-permute-start(bf16[4,10,64,128]{3,2,1,0:T(8,128)(2,1)S(1)} %shard_map.58.refs_0_), channel_id=1, source_target_pairs={{0,7},{1,0},{2,1},{3,2},{4,3},{5,4},{6,5},{7,6},{32,33},{33,34},{3... | collective-permute-start | bytes 1966088 | tf_op jit(solution)/shard_map/ppermute | solution.py:407
  34.3 18.0 %collective-permute-start.4 = (bf16[4,10,64,128]{3,2,1,0:T(8,128)(2,1)S(1)}, bf16[4,10,64,128]{3,2,1,0:T(8,128)(2,1)S(1)}, u32[]{:S(2)}, u32[]{:S(2)}) collective-permute-start(bf16[4,10,64,128]{3,2,1,0:T(8,128)(2,1)S(1)} %shard_map.58.refs_0_), channel_id=1, source_target_pairs={{0,1},{1,2},{2,3},{3,4},{4,5},{5,6},{6,7},{7,0},{32,39},{33,32},{3... | collective-permute-start | bytes 1966088 | tf_op jit(solution)/shard_map/ppermute | solution.py:406
  38.5 31.5 %collective-permute-start.2 = (bf16[8,6,64,128]{3,2,1,0:T(8,128)(2,1)S(1)}, bf16[8,6,64,128]{3,2,1,0:T(8,128)(2,1)S(1)}, u32[]{:S(2)}, u32[]{:S(2)}) collective-permute-start(bf16[8,6,64,128]{3,2,1,0:T(8,128)(2,1)S(1)} %all-to-all-done.near_ref.other_ref), channel_id=1, source_target_pairs={{0,24},{8,0},{16,8},{24,16},{32,40},{40,48},{48,56},{56,32},{1,25}... | collective-permute-start | bytes 2359304 | tf_op jit(solution)/shard_map/ppermute | solution.py:399
  46.3 21.7 %collective-permute-start.7 = (bf16[4,10,64,128]{3,2,1,0:T(8,128)(2,1)S(1)}, bf16[4,10,64,128]{3,2,1,0:T(8,128)(2,1)S(1)}, u32[]{:S(2)}, u32[]{:S(2)}) collective-permute-start(bf16[4,10,64,128]{3,2,1,0:T(8,128)(2,1)S(1)} %collective-permute-done.5.refs_2_), channel_id=1, source_target_pairs={{0,7},{1,0},{2,1},{3,2},{4,3},{5,4},{6,5},{7,6},{32,33},{33,34},{3... | collective-permute-start | bytes 1966088 | tf_op jit(solution)/shard_map/ppermute | solution.py:407
  52.3 17.8 %collective-permute-start.6 = (bf16[4,10,64,128]{3,2,1,0:T(8,128)(2,1)S(1)}, bf16[4,10,64,128]{3,2,1,0:T(8,128)(2,1)S(1)}, u32[]{:S(2)}, u32[]{:S(2)}) collective-permute-start(bf16[4,10,64,128]{3,2,1,0:T(8,128)(2,1)S(1)} %collective-permute-done.4.refs_1_), channel_id=1, source_target_pairs={{0,1},{1,2},{2,3},{3,4},{4,5},{5,6},{6,7},{7,0},{32,39},{33,32},{3... | collective-permute-start | bytes 1966088 | tf_op jit(solution)/shard_map/ppermute | solution.py:406
  57.4 30.2 %collective-permute-start = (bf16[8,6,64,128]{3,2,1,0:T(8,128)(2,1)S(1)}, bf16[8,6,64,128]{3,2,1,0:T(8,128)(2,1)S(1)}, u32[]{:S(2)}, u32[]{:S(2)}) collective-permute-start(bf16[8,6,64,128]{3,2,1,0:T(8,128)(2,1)S(1)} %all-to-all-done.near_ref.other_ref), channel_id=1, source_target_pairs={{0,8},{8,16},{16,24},{24,0},{32,56},{40,32},{48,40},{56,48},{1,9},... | collective-permute-start | bytes 2359304 | tf_op jit(solution)/shard_map/ppermute | solution.py:398
  68.1 25.5 %collective-permute-start.9 = (bf16[4,10,64,128]{3,2,1,0:T(8,128)(2,1)S(1)}, bf16[4,10,64,128]{3,2,1,0:T(8,128)(2,1)S(1)}, u32[]{:S(2)}, u32[]{:S(2)}) collective-permute-start(bf16[4,10,64,128]{3,2,1,0:T(8,128)(2,1)S(1)} %collective-permute-done.7.refs_4_), channel_id=1, source_target_pairs={{0,7},{1,0},{2,1},{3,2},{4,3},{5,4},{6,5},{7,6},{32,33},{33,34},{3... | collective-permute-start | bytes 1966088 | tf_op jit(solution)/shard_map/ppermute | solution.py:407
  70.1 25.6 %collective-permute-start.8 = (bf16[4,10,64,128]{3,2,1,0:T(8,128)(2,1)S(1)}, bf16[4,10,64,128]{3,2,1,0:T(8,128)(2,1)S(1)}, u32[]{:S(2)}, u32[]{:S(2)}) collective-permute-start(bf16[4,10,64,128]{3,2,1,0:T(8,128)(2,1)S(1)} %shard_map.59.refs_3_), channel_id=1, source_target_pairs={{0,1},{1,2},{2,3},{3,4},{4,5},{5,6},{6,7},{7,0},{32,39},{33,32},{3... | collective-permute-start | bytes 1966088 | tf_op jit(solution)/shard_map/ppermute | solution.py:406
  75.4 24.7 %copy-start = (bf16[8,64,2048]{2,1,0:T(8,128)(2,1)S(1)}, bf16[8,64,2048]{2,1,0:T(8,128)(2,1)}, u32[]{:S(2)}) copy-start(bf16[8,64,2048]{2,1,0:T(8,128)(2,1)} %own_ref.5) | copy-start | bytes 6291460
  75.4 27.6 %collective-permute-start.3 = (bf16[4,6,64,128]{3,2,1,0:T(8,128)(2,1)S(1)}, bf16[4,6,64,128]{3,2,1,0:T(8,128)(2,1)S(1)}, u32[]{:S(2)}, u32[]{:S(2)}) collective-permute-start(bf16[4,6,64,128]{3,2,1,0:T(8,128)(2,1)S(1)} %slice.17), channel_id=1, source_target_pairs={{0,24},{8,0},{16,8},{24,16},{32,40},{40,48},{48,56},{56,32},{1,25}... | collective-permute-start | bytes 1179656 | tf_op jit(solution)/shard_map/ppermute | solution.py:401
  87.6 19.3 %collective-permute-start.1 = (bf16[4,6,64,128]{3,2,1,0:T(8,128)(2,1)S(1)}, bf16[4,6,64,128]{3,2,1,0:T(8,128)(2,1)S(1)}, u32[]{:S(2)}, u32[]{:S(2)}) collective-permute-start(bf16[4,6,64,128]{3,2,1,0:T(8,128)(2,1)S(1)} %slice.16), channel_id=1, source_target_pairs={{0,8},{8,16},{16,24},{24,0},{32,56},{40,32},{48,40},{56,48},{1,9},... | collective-permute-start | bytes 1179656 | tf_op jit(solution)/shard_map/ppermute | solution.py:400
  93.6 14.0 %collective-permute-start.11 = (bf16[2,10,64,128]{3,2,1,0:T(8,128)(2,1)S(1)}, bf16[2,10,64,128]{3,2,1,0:T(8,128)(2,1)S(1)}, u32[]{:S(2)}, u32[]{:S(2)}) collective-permute-start(bf16[2,10,64,128]{3,2,1,0:T(8,128)(2,1)S(1)} %slice.19), channel_id=1, source_target_pairs={{0,7},{1,0},{2,1},{3,2},{4,3},{5,4},{6,5},{7,6},{32,33},{33,34},{3... | collective-permute-start | bytes 983048 | tf_op jit(solution)/shard_map/ppermute | solution.py:414
  95.8 11.8 %collective-permute-start.10 = (bf16[2,10,64,128]{3,2,1,0:T(8,128)(2,1)S(1)}, bf16[2,10,64,128]{3,2,1,0:T(8,128)(2,1)S(1)}, u32[]{:S(2)}, u32[]{:S(2)}) collective-permute-start(bf16[2,10,64,128]{3,2,1,0:T(8,128)(2,1)S(1)} %slice.18), channel_id=1, source_target_pairs={{0,1},{1,2},{2,3},{3,4},{4,5},{5,6},{6,7},{7,0},{32,39},{33,32},{3... | collective-permute-start | bytes 983048 | tf_op jit(solution)/shard_map/ppermute | solution.py:413
  110.9 4.8 %collective-permute-start.12 = (bf16[1024,512]{1,0:T(8,128)(2,1)S(1)}, bf16[1024,512]{1,0:T(8,128)(2,1)S(1)}, u32[]{:S(2)}, u32[]{:S(2)}) collective-permute-start(bf16[1024,512]{1,0:T(8,128)(2,1)S(1)} %shard_map.63), channel_id=1, source_target_pairs={{0,32},{32,0},{1,33},{33,1},{2,34},{34,2},{3,35},{35,3},{4,36},{36... | collective-permute-start | bytes 3145736 | tf_op jit(solution)/shard_map/ppermute | solution.py:419
  115.4 21.5 %copy-start.1 = (s32[16,16]{1,0:T(8,128)S(1)}, s32[16,16]{1,0:T(8,128)}, u32[]{:S(2)}) copy-start(s32[16,16]{1,0:T(8,128)} %mask_ref.3) | copy-start | bytes 3076
  116.8 53.7 %copy-start.2 = (s32[8]{0:T(128)S(1)}, s32[8]{0:T(128)}, u32[]{:S(2)}) copy-start(s32[8]{0:T(128)} %partner_ref.1) | copy-start | bytes 100
  150.3 20.2 %all-to-all-start.3 = ((bf16[32,16,128]{2,1,0:T(8,128)(2,1)}), bf16[32,16,128]{2,1,0:T(8,128)(2,1)S(1)}, u32[]{:S(2)}, u32[]{:S(2)}) async-start(bf16[32,16,128]{2,1,0:T(8,128)(2,1)} %bitcast.2), calls=%async_computation.3 | async-start | bytes 262144 | tf_op jit(solution)/shard_map/all_to_all | solution.py:424
